TPU v7x, 32 devices: a whole 2x2x4 slice. The times are simulated.
32 devices in a mesh: groups: 2 (over y), dp: 4 (over z), feat: 2 (over x), sub: 2 (over core).
Axes of the slice: x: 2, y: 2, z: 4, core: 2. Of those that a mesh axis runs over, the one named last changes fastest.
Arguments:
- bins: int32 [32768, 1024], P(('groups', 'dp', 'sub'), 'feat'), parts along dimension 0, may hold values from 0 to 127
- grads: bfloat16 [32768, 32], P(('groups', 'dp', 'sub')), parts along dimension 0, may hold values from -6 to 6
- hess: bfloat16 [32768], P(('groups', 'dp', 'sub')), parts along dimension 0, may hold values from 0.25 to 4
- node_side: int32 [32768], P(('groups', 'dp', 'sub')), parts along dimension 0, may hold values from 0 to 1
- signs: int32 [2048], P('groups'), parts along dimension 0, may hold values from -1 to 1
- child_owner: int32 [16], P('groups'), parts along dimension 0, may hold values from 0 to 7, each once
- parent_owner: int32 [16], P('groups'), parts along dimension 0, may hold values from 0 to 7, each once
- parent_grad: float32 [16, 128, 4096], P(('groups', 'dp', 'sub'), 'feat'), parts along dimension 0, may hold values from -48 to 48
- parent_hess: float32 [16, 128, 128], P(('groups', 'dp', 'sub'), 'feat'), parts along dimension 0, may hold values from 33 to 516
- node_low: int32 [4], P('groups'), parts along dimension 0, may hold values from -40 to -5
- node_high: int32 [4], P('groups'), parts along dimension 0, may hold values from 5 to 40
Outputs:
- gains: float32 [16, 128, 2, 128], P(('groups', 'dp', 'sub'), 'feat'), parts along dimension 0
There are 2 independent parts, one for each index of `groups`. A program takes and returns all parts, laid end to end along the dimension named above; each array names one. Nothing has to cross between parts.
Inputs may be any that keep to these rules, and one draw needn't show every extreme that they name: `child_owner`: each slot number appears once. `parent_owner`: each slot number appears once.
All inputs are finite; a program needn't handle non-finite values.
Results may differ from a plain program's by a relative error of at most 0.0003.
Values sent between devices are 32-bit elements; how exact they have to be, the bound alone decides.
No kernel may reach another device: no remote copies, remote signals or barrier semaphores. Data moves between devices by JAX's collectives and lax.ppermute only.
A program may use at most 128 MiB of HBM per device.

v0:
```python
import functools

import jax
import jax.numpy as jnp
from jax import lax
from jax.experimental import pallas as pl
from jax.experimental.pallas import tpu as pltpu
from jax.sharding import PartitionSpec as P

reg_lambda = 1.0
CHUNKS = 2
TILE = 256
PACK = 128
FAST = 9
PREP_MIB = 56
MIB = 1024 * 1024
VMEM_SPEC = pl.BlockSpec(memory_space=pltpu.VMEM)
SMEM_SPEC = pl.BlockSpec(memory_space=pltpu.SMEM)


def plan_of(line):
    roles = []
    for z in range(line):
        mine = []
        for step in range(line - 1):
            if z <= step:
                mine.append(("R", step, line - 1 - step + z))
            if line - 1 - z <= step:
                mine.append(("L", step, step - (line - 1 - z)))
        mine.append(("F", line - 1, z))
        roles.append(mine)
    return roles


def prep_kernel(line, slab, owner_ref, bins_ref, grads_ref, hess_ref, side_ref, own_ref, send_ref, wt_ref, wt_send_ref, buf_ref, sems, acc_ref, acc_w_ref):
    rows, f_dev = bins_ref.shape
    half = f_dev // 2
    kdim = grads_ref.shape[0]
    reach = TILE + PACK
    blocks = rows // TILE
    copies = []
    for i in range(blocks):
        part = pl.ds(i * TILE, TILE)
        copies.append(pltpu.make_async_copy(bins_ref.at[part, :], buf_ref.at[part, :], sems.at[i]))
        copies[-1].start()

    ones = [jnp.where(side_ref[:, i * TILE : (i + 1) * TILE] == 1, 1.0, 0.0) for i in range(blocks)]
    counts = [jnp.sum(x).astype(jnp.int32) for x in ones]
    bases = [jnp.int32(0)]
    for count in counts:
        bases.append(bases[-1] + count)
    starts = [pl.multiple_of((base // PACK) * PACK, PACK) for base in bases]
    marks = jnp.concatenate(ones, axis=0)
    before = lax.broadcasted_iota(jnp.int32, (TILE, TILE), 0) < lax.broadcasted_iota(jnp.int32, (TILE, TILE), 1)
    before = jnp.where(before, 1.0, 0.0).astype(jnp.bfloat16)
    ahead = jnp.dot(marks.astype(jnp.bfloat16), before, preferred_element_type=jnp.float32).astype(jnp.int32)
    slot = lax.broadcasted_iota(jnp.int32, (reach, TILE), 0)
    acc_ref[:PACK, :] = jnp.zeros((PACK, f_dev), jnp.bfloat16)
    acc_w_ref[:, :PACK] = jnp.zeros((acc_w_ref.shape[0], PACK), jnp.float32)

    z, core = lax.axis_index("dp"), lax.axis_index("sub")
    column = lax.broadcasted_iota(jnp.int32, (1, f_dev), 1)
    position = lax.rem(column, half) // slab
    table = plan_of(line)
    chip = jnp.zeros_like(column)
    for p in range(line):
        target = jnp.int32(0)
        for zz in range(line):
            target = jnp.where(z == zz, jnp.int32(table[zz][p][2]), target)
        chip = jnp.where(position == p, target, chip)
    owner = 2 * chip + jnp.where(column < half, core, 1 - core)
    source = jnp.zeros_like(column)
    for q in range(2 * line):
        source = jnp.where(owner == owner_ref[q], q, source)
    source = source * slab + lax.rem(column, slab)
    perm = jnp.where(lax.broadcasted_iota(jnp.int32, (f_dev, f_dev), 0) == source, 1.0, 0.0).astype(jnp.bfloat16)

    for i in range(blocks):
        part = slice(i * TILE, (i + 1) * TILE)
        goal = jnp.where(ones[i] > 0.5, ahead[i : i + 1] + (bases[i] - starts[i]), -1)
        pack = jnp.where(slot == goal, 1.0, 0.0).astype(jnp.bfloat16)
        hess = jnp.broadcast_to(hess_ref[:, part], (16, TILE))
        first = lax.broadcasted_iota(jnp.int32, hess.shape, 0) == 0
        weights = jnp.concatenate([grads_ref[:, part].astype(jnp.float32), jnp.where(first, hess, 0.0)], axis=0)
        packed_w = lax.dot_general(weights.astype(jnp.bfloat16), pack, (((1,), (1,)), ((), ())), preferred_element_type=jnp.float32)
        acc_w_ref[:, pl.ds(starts[i], PACK)] += packed_w[:, :PACK]
        acc_w_ref[:, pl.ds(starts[i] + PACK, TILE)] = packed_w[:, PACK:]
        copies[i].wait()
        binned = buf_ref[part, :].astype(jnp.float32).astype(jnp.bfloat16)
        packed = jnp.dot(pack, binned, preferred_element_type=jnp.float32).astype(jnp.bfloat16)
        acc_ref[pl.ds(starts[i], PACK), :] += packed[:PACK]
        acc_ref[pl.ds(starts[i] + PACK, TILE), :] = packed[PACK:]

    def move(t, carry):
        part = pl.ds(pl.multiple_of(t * TILE, TILE), TILE)
        moved = jnp.dot(acc_ref[part, :], perm, preferred_element_type=jnp.float32)
        own_ref[part, :] = moved[:, :half].astype(jnp.bfloat16)
        send_ref[part, :] = moved[:, half:]
        return carry

    total = bases[blocks]
    lax.fori_loop(0, (total + TILE - 1) // TILE, move, 0)
    lane = lax.broadcasted_iota(jnp.int32, (acc_w_ref.shape[0], rows), 1)
    row = lax.broadcasted_iota(jnp.int32, lane.shape, 0)
    packed = jnp.where(lane < total, acc_w_ref[:, :rows], 0.0)
    packs = ((total + PACK - 1) // PACK).astype(jnp.float32)
    packed = jnp.where(row == kdim + 1, packs, packed)
    wt_ref[...] = packed.astype(jnp.bfloat16)
    wt_send_ref[...] = packed[: kdim + 8]


def prep(line, slab, owners, bins, grads, hess, side):
    rows, f_dev = bins.shape
    kdim = grads.shape[1]
    half = f_dev // 2
    return pl.pallas_call(
        functools.partial(prep_kernel, line, slab),
        in_specs=[SMEM_SPEC, pl.BlockSpec(memory_space=pl.ANY), VMEM_SPEC, VMEM_SPEC, VMEM_SPEC],
        out_specs=[VMEM_SPEC] * 4,
        out_shape=[
            jax.ShapeDtypeStruct((rows, half), jnp.bfloat16),
            jax.ShapeDtypeStruct((rows, half), jnp.float32),
            jax.ShapeDtypeStruct((kdim + 16, rows), jnp.bfloat16),
            jax.ShapeDtypeStruct((kdim + 8, rows), jnp.float32),
        ],
        scratch_shapes=[
            pltpu.VMEM((rows, f_dev), jnp.int32),
            pltpu.SemaphoreType.DMA((rows // TILE,)),
            pltpu.VMEM((rows + TILE + PACK, f_dev), jnp.bfloat16),
            pltpu.VMEM((kdim + 16, rows + TILE + PACK), jnp.float32),
        ],
        compiler_params=pltpu.CompilerParams(vmem_limit_bytes=PREP_MIB * MIB),
        cost_estimate=pl.CostEstimate(flops=4 * rows * f_dev * f_dev, bytes_accessed=8 * rows * f_dev, transcendentals=0),
        name="prep",
    )(owners, bins, grads.T, hess.astype(jnp.float32).reshape(1, rows), side.reshape(1, rows))


def tiles_in(wt_ref, kdim):
    return jnp.max(wt_ref[:, :128].astype(jnp.float32)[kdim + 1 : kdim + 2]).astype(jnp.int32)


def hist_kernel(first_column, width, levels, parts, kdim, has_init, *refs):
    pairs = [refs[2 * i : 2 * i + 2] for i in range(parts)]
    init_ref = refs[2 * parts] if has_init else None
    out_ref, rel_ref, wt_ref = refs[-3:]
    lanes = out_ref.shape[1]
    rows, half = pairs[0][0].shape
    src = lax.broadcasted_iota(jnp.int32, (half, lanes), 0)
    dst = lax.broadcasted_iota(jnp.int32, (half, lanes), 1)
    spread = jnp.where(src == first_column + lax.rem(dst, width), 1.0, 0.0).astype(jnp.bfloat16)
    lane = lax.broadcasted_iota(jnp.int32, (1, lanes), 1)
    shift = ((lane // width) * levels).astype(jnp.float32)
    one = jnp.ones((TILE, lanes), jnp.bfloat16)
    zero = jnp.zeros((TILE, lanes), jnp.bfloat16)

    def place_rows(bins_ref, source, target):
        block = bins_ref[pl.ds(source, PACK), :].astype(jnp.bfloat16)
        moved = jnp.dot(block, spread, preferred_element_type=jnp.float32)
        rel_ref[pl.ds(target, PACK), :] = (moved - shift).astype(jnp.bfloat16)

    def place_weights(height):
        for i, (_, w_ref) in enumerate(pairs):
            weights = w_ref[:, :height]
            if w_ref.dtype != jnp.bfloat16:
                weights = jnp.concatenate([weights, jnp.zeros((8, height), jnp.float32)], axis=0).astype(jnp.bfloat16)
            wt_ref[:, i * height : (i + 1) * height] = weights

    def sums_of(b, tiles):
        value = jnp.full((TILE, lanes), b.astype(jnp.float32), jnp.float32).astype(jnp.bfloat16)
        total = jnp.zeros((wt_ref.shape[0], lanes), jnp.float32)
        for first, size in tiles:
            hit = rel_ref[pl.ds(first, size), :] == value[:size]
            onehot = jnp.where(hit, one[:size], zero[:size])
            total = total + jnp.dot(wt_ref[:, pl.ds(first, size)], onehot, preferred_element_type=jnp.float32)
        return total[:kdim], total[kdim : kdim + 1]

    def spots_of(b):
        return pl.ds(pl.multiple_of(b * kdim, kdim), kdim), pl.ds(levels * kdim + b, 1)

    def fast():
        height = FAST * PACK
        for i, (bins_ref, _) in enumerate(pairs):
            for r in range(0, height, PACK):
                place_rows(bins_ref, r, i * height + r)
        place_weights(height)
        tiles = [(r, min(TILE, parts * height - r)) for r in range(0, parts * height, TILE)]

        def level(b, carry):
            grad, hess = sums_of(b, tiles)
            grad_spot, hess_spot = spots_of(b)
            if has_init:
                grad, hess = grad + init_ref[grad_spot, :], hess + init_ref[hess_spot, :]
            out_ref[grad_spot, :] = grad
            out_ref[hess_spot, :] = hess
            return carry

        lax.fori_loop(0, levels, level, 0)

    def general():
        for i, (bins_ref, _) in enumerate(pairs):

            def one_pack(p, carry):
                r = pl.multiple_of(p * PACK, PACK)
                place_rows(bins_ref, r, i * rows + r)
                return carry

            lax.fori_loop(0, rows // PACK, one_pack, 0)
        place_weights(rows)
        out_ref[...] = init_ref[...] if has_init else jnp.zeros(out_ref.shape, jnp.float32)
        step = 2 * TILE

        def group(g, carry):
            first = pl.multiple_of(g * step, step)

            def level(b, carry):
                grad, hess = sums_of(b, [(first, TILE), (first + TILE, TILE)])
                grad_spot, hess_spot = spots_of(b)
                out_ref[grad_spot, :] += grad
                out_ref[hess_spot, :] += hess
                return carry

            return lax.fori_loop(0, levels, level, carry)

        lax.fori_loop(0, parts * rows // step, group, 0)

    needed = tiles_in(pairs[0][1], kdim)
    for _, w_ref in pairs[1:]:
        needed = jnp.maximum(needed, tiles_in(w_ref, kdim))
    if FAST * PACK < rows:
        pl.when(needed <= FAST)(fast)
        pl.when(needed > FAST)(general)
    else:
        general()


def hist(first_column, width, levels, lanes, kdim, pairs, init=None, tie=()):
    rows = pairs[0][0].shape[0]
    parts = len(pairs)
    operands = [x for pair in pairs for x in pair]
    if init is not None:
        operands.append(init)
    specs = [VMEM_SPEC] * len(operands) + [pl.BlockSpec(memory_space=pl.ANY)] * len(tie)
    height = levels * (kdim + 1)
    return pl.pallas_call(
        functools.partial(hist_kernel, first_column, width, levels, parts, kdim, init is not None),
        in_specs=specs,
        out_specs=VMEM_SPEC,
        out_shape=jax.ShapeDtypeStruct((height, lanes), jnp.float32),
        scratch_shapes=[
            pltpu.VMEM((parts * rows, lanes), jnp.bfloat16),
            pltpu.VMEM((kdim + 16, parts * rows), jnp.bfloat16),
        ],
        compiler_params=pltpu.CompilerParams(vmem_limit_bytes=20 * MIB),
        cost_estimate=pl.CostEstimate(
            flops=2 * 128 * parts * rows * levels * lanes, bytes_accessed=parts * rows * lanes * 4, transcendentals=0
        ),
        name="hist",
    )(*operands, *tie)


def repeat_lanes(x, width, lanes):
    if lanes > x.shape[1]:
        x = jnp.concatenate([x] * (lanes // x.shape[1]), axis=1)
    x = jnp.where(lax.broadcasted_iota(jnp.int32, x.shape, 1) < width, x[:, :lanes], 0)
    reach = width
    while reach < lanes:
        x = x + pltpu.roll(x, reach, 1)
        reach *= 2
    return x


def layout_kernel(width, levels, kdim, chunks, owner_ref, sign_ref, parent_ref, hess_ref, tie_ref, *out_refs):
    del tie_ref
    grad_refs, hess_refs, sign_refs = out_refs[:chunks], out_refs[chunks : 2 * chunks], out_refs[2 * chunks :]
    lanes = grad_refs[0].shape[1]
    slab = width * chunks
    owners = owner_ref.shape[0]
    place = 2 * lax.axis_index("dp") + lax.axis_index("sub")
    slab_at = jnp.int32(0)
    for q in range(owners):
        slab_at = jnp.where(owner_ref[q] == place, q, slab_at)
    offset = lax.axis_index("feat") * (owners * slab) + slab_at * slab
    features = sign_ref.shape[1]
    signs = jnp.broadcast_to(sign_ref[...], (8, features))
    per_tile = 128 // width
    step = 128 // kdim
    for c in range(chunks):
        turned = pltpu.roll(signs, lax.rem(features - offset - c * width + features, features), 1)
        sign_refs[c][...] = repeat_lanes(turned[:, :128], width, lanes)
        rows = hess_ref[c * width : (c + 1) * width, :]
        turned = jnp.concatenate([rows] * (128 // width), axis=0).T
        total = jnp.zeros((levels, lanes), jnp.float32)
        for j in range(lanes // width):
            piece = turned[j * levels : (j + 1) * levels, :]
            piece = jnp.concatenate([piece] * (lanes // 128), axis=1)
            group = lax.broadcasted_iota(jnp.int32, piece.shape, 1) // width
            total = jnp.where(group == j, piece, total)
        hess_refs[c][...] = total
        for tile in range(lanes // 128):
            for b in range(0, levels, step):
                rows = []
                for jj in range(per_tile):
                    bin_at = (tile * per_tile + jj) * levels + b
                    rows.append(parent_ref[c * width : (c + 1) * width, bin_at * kdim : bin_at * kdim + 128])
                block = jnp.concatenate(rows, axis=0) if per_tile > 1 else rows[0]
                grad_refs[c][b * kdim : b * kdim + 128, tile * 128 : (tile + 1) * 128] = block.T


def parent_layout(width, levels, lanes, kdim, chunks, owners, signs, parent, hess, tie):
    shapes = [jax.ShapeDtypeStruct((levels * kdim, lanes), jnp.float32)] * chunks
    shapes += [jax.ShapeDtypeStruct((levels, lanes), jnp.float32)] * chunks
    shapes += [jax.ShapeDtypeStruct((8, lanes), jnp.int32)] * chunks
    out = pl.pallas_call(
        functools.partial(layout_kernel, width, levels, kdim, chunks),
        in_specs=[SMEM_SPEC] + [VMEM_SPEC] * 3 + [pl.BlockSpec(memory_space=pl.ANY)],
        out_specs=[VMEM_SPEC] * (3 * chunks),
        out_shape=shapes,
        compiler_params=pltpu.CompilerParams(vmem_limit_bytes=16 * MIB),
        cost_estimate=pl.CostEstimate(flops=0, bytes_accessed=2 * parent.size * 4, transcendentals=0),
        name="parent_layout",
    )(owners, signs.reshape(1, -1), parent, hess, tie)
    return out[:chunks], out[chunks : 2 * chunks], out[2 * chunks :]


def lane_prefix(total, width):
    lanes = total.shape[1]
    lane = lax.broadcasted_iota(jnp.int32, total.shape, 1)
    running = total
    reach = width
    while reach < lanes:
        running = running + jnp.where(lane >= reach, pltpu.roll(running, reach, 1), 0.0)
        reach *= 2
    whole = total
    reach = width
    while reach < lanes:
        whole = whole + pltpu.roll(whole, reach, 1)
        reach *= 2
    return running - total, running, whole


def gain_kernel(width, levels, kdim, last_ref, right_ref, left_ref, par_grad_ref, par_hess_ref, sign_ref, low_ref, high_ref, out_ref, grad_ref, hess_ref):
    hess_at = levels * kdim
    lanes = out_ref.shape[2]

    def small_at(start, size):
        return last_ref[pl.ds(start, size), :] + right_ref[pl.ds(start, size), :] + left_ref[pl.ds(start, size), :]

    sign = sign_ref[:1, :]
    small_hess = small_at(hess_at, levels)
    hess_ref[0] = small_hess
    hess_ref[1] = par_hess_ref[...] - small_hess

    def add_up(b, carry):
        g0, g1, h0, h1 = carry
        start = pl.multiple_of(b * kdim, kdim)
        small = small_at(start, kdim)
        g0 = g0 + small
        g1 = g1 + (par_grad_ref[pl.ds(start, kdim), :] - small)
        h0 = h0 + hess_ref[0, pl.ds(b, 1), :]
        h1 = h1 + hess_ref[1, pl.ds(b, 1), :]
        grad_ref[0, pl.ds(start, kdim), :] = g0
        grad_ref[1, pl.ds(start, kdim), :] = g1
        hess_ref[0, pl.ds(b, 1), :] = h0
        hess_ref[1, pl.ds(b, 1), :] = h1
        return g0, g1, h0, h1

    zero_g = jnp.zeros((kdim, lanes), jnp.float32)
    zero_h = jnp.zeros((1, lanes), jnp.float32)
    ends = lax.fori_loop(0, levels, add_up, (zero_g, zero_g, zero_h, zero_h))
    for c in range(2):
        low = low_ref[c].astype(jnp.float32) / 1024.0
        high = high_ref[c].astype(jnp.float32) / 1024.0
        middle = 0.5 * (low + high)
        low_left = jnp.where(sign < 0, middle, low)
        high_left = jnp.where(sign > 0, middle, high)
        low_right = jnp.where(sign > 0, middle, low)
        high_right = jnp.where(sign < 0, middle, high)
        grad_before, _, grad_all = lane_prefix(ends[c], width)
        hess_rows = jnp.broadcast_to(ends[2 + c], (8, lanes))
        hess_before, _, hess_all = lane_prefix(hess_rows, width)
        hess_before, hess_all = hess_before[:1], hess_all[:1]

        def score(grad, hess, lower, upper):
            denom = jnp.maximum(hess, 0.0) + reg_lambda
            weight = jnp.clip(-grad / denom, lower, upper)
            return jnp.sum((2.0 * grad + denom * weight) * weight, axis=0, keepdims=True)

        def one_bin(b, carry):
            start = pl.multiple_of(b * kdim, kdim)
            grad_left = grad_ref[c, pl.ds(start, kdim), :] + grad_before
            hess_left = hess_ref[c, pl.ds(b, 1), :] + hess_before
            left = score(grad_left, hess_left, low_left, high_left)
            right = score(grad_all - grad_left, hess_all - hess_left, low_right, high_right)
            out_ref[c, pl.ds(b, 1), :] = (left + right) * (-1.0 / kdim)
            return carry

        lax.fori_loop(0, levels, one_bin, 0)


def gains_of(width, levels, lanes, kdim, last, right, left, par_grad, par_hess, sign, node_low, node_high):
    return pl.pallas_call(
        functools.partial(gain_kernel, width, levels, kdim),
        in_specs=[VMEM_SPEC] * 6 + [SMEM_SPEC] * 2,
        out_specs=VMEM_SPEC,
        out_shape=jax.ShapeDtypeStruct((2, levels, lanes), jnp.float32),
        scratch_shapes=[
            pltpu.VMEM((2, levels * kdim, lanes), jnp.float32),
            pltpu.VMEM((2, levels, lanes), jnp.float32),
        ],
        compiler_params=pltpu.CompilerParams(vmem_limit_bytes=24 * MIB),
        cost_estimate=pl.CostEstimate(flops=50 * levels * kdim * lanes, bytes_accessed=16 * levels * kdim * lanes, transcendentals=0),
        name="gains",
    )(last, right, left, par_grad, par_hess, sign, node_low, node_high)


def source_of(place, child_ref, parent_ref):
    source = jnp.int32(0)
    for q in range(child_ref.shape[0]):
        source = jnp.where(child_ref[q] == place, parent_ref[q], source)
    return source


def choose_kernel(line, child_ref, parent_ref, *refs):
    z, core = lax.axis_index("dp"), lax.axis_index("sub")
    chip = source_of(2 * z + 1 - core, child_ref, parent_ref) // 2
    out_ref = refs[-1]
    for s in range(line):

        @pl.when(lax.rem(z - chip + line, line) == s)
        def _():
            out_ref[...] = refs[s][...]


def choose(line, child_owner, parent_owner, got):
    return pl.pallas_call(
        functools.partial(choose_kernel, line),
        in_specs=[SMEM_SPEC] * 2 + [VMEM_SPEC] * line,
        out_specs=VMEM_SPEC,
        out_shape=jax.ShapeDtypeStruct(got[0].shape, jnp.float32),
        name="choose",
    )(child_owner, parent_owner, *got)


def finish_kernel(line, chunks, width, child_ref, parent_ref, *refs):
    out_ref, held_ref = refs[-2:]
    z, core = lax.axis_index("dp"), lax.axis_index("sub")
    source = source_of(2 * z + core, child_ref, parent_ref)
    same = lax.rem(source, 2) == core
    shift = lax.rem(z - source // 2 + line, line)
    for c in range(chunks):
        got = refs[c * (line + 1) : (c + 1) * (line + 1)]
        for s in range(line):

            @pl.when(same & (shift == s))
            def _():
                held_ref[c] = got[s][...]

        @pl.when(jnp.logical_not(same))
        def _():
            held_ref[c] = got[line][...]

    slab = width * chunks
    lanes = held_ref.shape[3]
    total = jnp.zeros((128, 128), jnp.float32)
    column = lax.broadcasted_iota(jnp.int32, (128, 128), 1)
    for child in range(2):
        for c in range(chunks):
            gain = held_ref[c, child]
            at = child * slab + c * width
            pieces = []
            for j in range(lanes // width):
                turn = (at - j * width) % lanes
                turned = pltpu.roll(gain, turn, 1) if turn else gain
                pieces.append(turned[:, :128])
            stack = jnp.concatenate(pieces, axis=0)
            total = jnp.where((column >= at) & (column < at + width), stack, total)
    turned = total.T
    for child in range(2):
        out_ref[:, child, :] = turned[child * slab : (child + 1) * slab]


def finish(line, chunks, width, nbins, child_owner, parent_owner, parts):
    shape = parts[0][0].shape
    flat = [x for part in parts for x in part]
    return pl.pallas_call(
        functools.partial(finish_kernel, line, chunks, width),
        in_specs=[SMEM_SPEC] * 2 + [VMEM_SPEC] * len(flat),
        out_specs=VMEM_SPEC,
        out_shape=jax.ShapeDtypeStruct((width * chunks, 2, nbins), jnp.float32),
        scratch_shapes=[pltpu.VMEM((chunks, *shape), jnp.float32)],
        name="finish",
    )(child_owner, parent_owner, *flat)


def one_of(z, members):
    hit = z == members[0]
    for m in members[1:]:
        hit = hit | (z == m)
    return hit


def per_device(bins, grads, hess, node_side, signs, child_owner, parent_owner, parent_grad, parent_hess, node_low, node_high):
    line = lax.axis_size("dp")
    z = lax.axis_index("dp")
    kdim = grads.shape[1]
    nbins = parent_hess.shape[2]
    slab = parent_grad.shape[1]
    chunks = CHUNKS if slab >= 32 else 1
    width = slab // chunks
    lanes = min(256, width * nbins * kdim // 128)
    levels = nbins // (lanes // width)
    plan = plan_of(line)

    own, send, wt, wt_send = prep(line, slab, parent_owner, bins, grads, hess, node_side)
    swap = [(0, 1), (1, 0)]
    wt_other = lax.ppermute(wt_send, "sub", swap)
    other = lax.ppermute(send, "sub", swap)
    mine = (own, wt)
    theirs = (other, wt_other)

    units = {}
    for c in range(chunks):
        units[0, c] = hist(c * width, width, levels, lanes, kdim, [mine])
    for c in range(chunks):
        units[0, c] = hist(c * width, width, levels, lanes, kdim, [theirs], units[0, c])

    def pick(kind, step, c):
        where_at = {}
        for zz in range(line):
            for p, role in enumerate(plan[zz]):
                if role[:2] == (kind, step):
                    where_at.setdefault(p, []).append(zz)
        spots = sorted(where_at)
        value = units[spots[0], c]
        for p in spots[1:]:
            value = jnp.where(one_of(z, where_at[p]), units[p, c], value)
        return value

    from_left = [None] * chunks
    from_right = [None] * chunks
    arrived = []

    def tie_of(step, c):
        at = min(step * chunks + c - 3, (line - 2) * chunks - 1)
        return (arrived[at],) if at >= 0 else (units[0, chunks - 1],)

    last = line - 1
    for step in range(line - 1):
        for c in range(chunks):
            if step > 0:
                units[step, c] = hist(step * slab + c * width, width, levels, lanes, kdim, [mine, theirs], tie=tie_of(step, c))
            to_right = pick("R", step, c)
            to_left = pick("L", step, c)
            if step > 0:
                to_right = to_right + from_left[c]
                to_left = to_left + from_right[c]
            from_left[c] = lax.ppermute(to_right, "dp", [(i, i + 1) for i in range(step + 1)])
            from_right[c] = lax.ppermute(to_left, "dp", [(line - 1 - i, line - 2 - i) for i in range(step + 1)])
            arrived.append(from_left[c])
    par_grad, par_hess, sign = parent_layout(
        width, levels, lanes, kdim, chunks, parent_owner, signs, parent_grad[0], parent_hess[0], tie_of(last, 0)[0]
    )
    for c in range(chunks):
        units[last, c] = hist(last * slab + c * width, width, levels, lanes, kdim, [mine, theirs], tie=tie_of(last, c))

    done = []
    for c in range(chunks):
        gain = gains_of(
            width, levels, lanes, kdim, units[last, c], from_left[c], from_right[c], par_grad[c], par_hess[c], sign[c], node_low, node_high
        )
        got = [gain] + [lax.ppermute(gain, "dp", [(i, (i + s) % line) for i in range(line)]) for s in range(1, line)]
        got.append(lax.ppermute(choose(line, child_owner, parent_owner, got), "sub", swap))
        done.append(got)
    return finish(line, chunks, width, nbins, child_owner, parent_owner, done)[None]


def solution(mesh):
    return jax.shard_map(
        per_device,
        mesh=mesh,
        in_specs=(
            P(("groups", "dp", "sub"), "feat"),
            P(("groups", "dp", "sub"), None),
            P(("groups", "dp", "sub")),
            P(("groups", "dp", "sub")),
            P("groups"),
            P("groups"),
            P("groups"),
            P(("groups", "dp", "sub"), "feat", None),
            P(("groups", "dp", "sub"), "feat", None),
            P("groups"),
            P("groups"),
        ),
        out_specs=P(("groups", "dp", "sub"), "feat", None, None),
        check_vma=False,
    )
```

profile of v0, /device:TPU:0, one launch (start us, length us, event | category | flops | bytes accessed | tf_op | source)
XLA Modules:
  0.0 123.5 jit_solution(12664844563380620595)
XLA Ops:
  1.3 8.1 %prep.1 = (bf16[2048,256]{1,0:T(8,128)(2,1)}, f32[2048,256]{1,0:T(8,128)}, bf16[48,2048]{1,0:T(8,128)(2,1)}, f32[40,2048]{1,0:T(8,128)}) custom-call(s32[8]{0:T(128)} %parent_ref.5, s32[2048,512]{1,0:T(8,128)} %bins_ref.1, bf16[32,2048]{1,0:T(8,128)(2,1)} %bitcast.11, f32[1,2048]{1,0:T(1,128)} %bitcast.10, s32[1,2048]{1,0:T(1,128)} %bitcast.12), custom_call_target="tpu_custom_call" | custom-call | flops 2147483648 | bytes 8388608 | tf_op jit(solution)/shard_map/prep/pallas_call | solution.py:116
  12.1 4.1 %hist.13.refs_2_ = f32[528,256]{1,0:T(8,128)S(1)} custom-call(bf16[2048,256]{1,0:T(8,128)(2,1)S(1)} %copy-done.8, bf16[48,2048]{1,0:T(8,128)(2,1)S(1)} %copy-done.10), custom_call_target="tpu_custom_call" | custom-call | flops 2147483648 | bytes 2097152 | tf_op jit(solution)/shard_map/hist/pallas_call | solution.py:244
  16.3 4.1 %hist.10.refs_2_ = f32[528,256]{1,0:T(8,128)S(1)} custom-call(bf16[2048,256]{1,0:T(8,128)(2,1)S(1)} %copy-done.8, bf16[48,2048]{1,0:T(8,128)(2,1)S(1)} %copy-done.10), custom_call_target="tpu_custom_call" | custom-call | flops 2147483648 | bytes 2097152 | tf_op jit(solution)/shard_map/hist/pallas_call | solution.py:244
  20.4 4.1 %hist.11 = f32[528,256]{1,0:T(8,128)S(1)} custom-call(f32[2048,256]{1,0:T(8,128)S(1)} %collective-permute-done.refs_0_.refs_2_, f32[40,2048]{1,0:T(8,128)S(1)} %collective-permute-done.1.refs_1_.refs_3_, f32[528,256]{1,0:T(8,128)S(1)} %hist.10.refs_2_), custom_call_target="tpu_custom_call" | custom-call | flops 2147483648 | bytes 2097152 | tf_op jit(solution)/shard_map/hist/pallas_call | solution.py:244
  25.4 4.9 %collective-permute-start.2 = (f32[528,256]{1,0:T(8,128)S(1)}, f32[528,256]{1,0:T(8,128)S(1)}, u32[]{:S(2)}, u32[]{:S(2)}) collective-permute-start(f32[528,256]{1,0:T(8,128)S(1)} %hist.11), channel_id=1, source_target_pairs={{0,4},{1,5},{2,6},{3,7},{16,20},{17,21},{18,22},{19,23}} | collective-permute-start | bytes 1622024 | tf_op jit(solution)/shard_map/ppermute | solution.py:557
  30.4 4.1 %hist.14.refs_4_ = f32[528,256]{1,0:T(8,128)S(1)} custom-call(f32[2048,256]{1,0:T(8,128)S(1)} %collective-permute-done.refs_0_.refs_2_, f32[40,2048]{1,0:T(8,128)S(1)} %collective-permute-done.1.refs_1_.refs_3_, f32[528,256]{1,0:T(8,128)S(1)} %hist.13.refs_2_), custom_call_target="tpu_custom_call" | custom-call | flops 2147483648 | bytes 2097152 | tf_op jit(solution)/shard_map/hist/pallas_call | solution.py:244
  36.5 6.0 %hist.17 = f32[528,256]{1,0:T(8,128)S(1)} custom-call(bf16[2048,256]{1,0:T(8,128)(2,1)S(1)} %copy-done.9, bf16[48,2048]{1,0:T(8,128)(2,1)S(1)} %copy-done.10, f32[2048,256]{1,0:T(8,128)S(1)} %collective-permute-done.refs_0_.refs_2_, f32[40,2048]{1,0:T(8,128)S(1)} %collective-permute-done.1.refs_1_.refs_3_, f32[528,256]{1,0:T(8,128)S(1)} %hist.14.refs_4_), custom_call_target="tpu_custom_call" | custom-call | flops 4294967296 | bytes 4194304 | tf_op jit(solution)/shard_map/hist/pallas_call | solution.py:244
  43.8 5.0 %collective-permute-start.5 = (f32[528,256]{1,0:T(8,128)S(1)}, f32[528,256]{1,0:T(8,128)S(1)}, u32[]{:S(2)}, u32[]{:S(2)}) collective-permute-start(f32[528,256]{1,0:T(8,128)S(1)} %get-tuple-element.28), channel_id=1, source_target_pairs={{0,4},{4,8},{1,5},{5,9},{2,6},{6,10},{3,7},{7,11},{16,20},{20,24},... | collective-permute-start | bytes 1622024 | tf_op jit(solution)/shard_map/ppermute | solution.py:557
  48.8 6.0 %hist.12 = f32[528,256]{1,0:T(8,128)S(1)} custom-call(bf16[2048,256]{1,0:T(8,128)(2,1)S(1)} %copy-done.9, bf16[48,2048]{1,0:T(8,128)(2,1)S(1)} %copy-done.10, f32[2048,256]{1,0:T(8,128)S(1)} %collective-permute-done.refs_0_.refs_2_, f32[40,2048]{1,0:T(8,128)S(1)} %collective-permute-done.1.refs_1_.refs_3_, f32[528,256]{1,0:T(8,128)S(1)} %collective-permute-done.2.refs_4_), custom_call_target="tpu_custom_call" | custom-call | flops 4294967296 | bytes 4194304 | tf_op jit(solution)/shard_map/hist/pallas_call | solution.py:244
  55.7 5.1 %collective-permute-start.4 = (f32[528,256]{1,0:T(8,128)S(1)}, f32[528,256]{1,0:T(8,128)S(1)}, u32[]{:S(2)}, u32[]{:S(2)}) collective-permute-start(f32[528,256]{1,0:T(8,128)S(1)} %get-tuple-element.26), channel_id=1, source_target_pairs={{0,4},{4,8},{1,5},{5,9},{2,6},{6,10},{3,7},{7,11},{16,20},{20,24},... | collective-permute-start | bytes 1622024 | tf_op jit(solution)/shard_map/ppermute | solution.py:557
  60.8 6.0 %hist.16 = f32[528,256]{1,0:T(8,128)S(1)} custom-call(bf16[2048,256]{1,0:T(8,128)(2,1)S(1)} %copy-done.9, bf16[48,2048]{1,0:T(8,128)(2,1)S(1)} %copy-done.10, f32[2048,256]{1,0:T(8,128)S(1)} %collective-permute-done.refs_0_.refs_2_, f32[40,2048]{1,0:T(8,128)S(1)} %collective-permute-done.1.refs_1_.refs_3_, f32[528,256]{1,0:T(8,128)S(1)} %collective-permute-done.3.refs_4_), custom_call_target="tpu_custom_call" | custom-call | flops 4294967296 | bytes 4194304 | tf_op jit(solution)/shard_map/hist/pallas_call | solution.py:244
  68.3 5.2 %collective-permute-start.6 = (f32[528,256]{1,0:T(8,128)S(1)}, f32[528,256]{1,0:T(8,128)S(1)}, u32[]{:S(2)}, u32[]{:S(2)}) collective-permute-start(f32[528,256]{1,0:T(8,128)S(1)} %get-tuple-element.32), channel_id=1, source_target_pairs={{0,4},{4,8},{8,12},{1,5},{5,9},{9,13},{2,6},{6,10},{10,14},{3,7},{... | collective-permute-start | bytes 1622024 | tf_op jit(solution)/shard_map/ppermute | solution.py:557
  73.5 6.0 %hist.19 = f32[528,256]{1,0:T(8,128)S(1)} custom-call(bf16[2048,256]{1,0:T(8,128)(2,1)S(1)} %copy-done.9, bf16[48,2048]{1,0:T(8,128)(2,1)S(1)} %copy-done.10, f32[2048,256]{1,0:T(8,128)S(1)} %collective-permute-done.refs_0_.refs_2_, f32[40,2048]{1,0:T(8,128)S(1)} %collective-permute-done.1.refs_1_.refs_3_, f32[528,256]{1,0:T(8,128)S(1)} %collective-permute-done.5.refs_4_), custom_call_target="tpu_custom_call" | custom-call | flops 4294967296 | bytes 4194304 | tf_op jit(solution)/shard_map/hist/pallas_call | solution.py:244
  81.0 4.7 %collective-permute-start.14 = (f32[528,256]{1,0:T(8,128)S(1)}, f32[528,256]{1,0:T(8,128)S(1)}, u32[]{:S(2)}, u32[]{:S(2)}) collective-permute-start(f32[528,256]{1,0:T(8,128)S(1)} %get-tuple-element.30), channel_id=1, source_target_pairs={{0,4},{4,8},{8,12},{1,5},{5,9},{9,13},{2,6},{6,10},{10,14},{3,7},{... | collective-permute-start | bytes 1622024 | tf_op jit(solution)/shard_map/ppermute | solution.py:557
  85.7 6.0 %hist.15.last_ref = f32[528,256]{1,0:T(8,128)S(1)} custom-call(bf16[2048,256]{1,0:T(8,128)(2,1)S(1)} %copy-done.9, bf16[48,2048]{1,0:T(8,128)(2,1)S(1)} %copy-done.10, f32[2048,256]{1,0:T(8,128)S(1)} %collective-permute-done.refs_0_.refs_2_, f32[40,2048]{1,0:T(8,128)S(1)} %collective-permute-done.1.refs_1_.refs_3_, ...), custom_call_target="tpu_custom_call" | custom-call | flops 4294967296 | bytes 4194304 | tf_op jit(solution)/shard_map/hist/pallas_call | solution.py:244
  93.0 2.7 %gains.2.refs_0_ = f32[2,16,256]{2,1,0:T(8,128)S(1)} custom-call(f32[528,256]{1,0:T(8,128)S(1)} %hist.15.last_ref, f32[528,256]{1,0:T(8,128)S(1)} %collective-permute-done.6.right_ref, f32[528,256]{1,0:T(8,128)S(1)} %collective-permute-done.9.left_ref, f32[512,256]{1,0:T(8,128)S(1)} %get-tuple-element.19.par_grad_ref, ...), custom_call_target="tpu_custom_call" | custom-call | flops 6553600 | bytes 2097152 | tf_op jit(solution)/shard_map/gains/pallas_call | solution.py:401
  96.1 6.0 %hist.18.last_ref = f32[528,256]{1,0:T(8,128)S(1)} custom-call(bf16[2048,256]{1,0:T(8,128)(2,1)S(1)} %copy-done.9, bf16[48,2048]{1,0:T(8,128)(2,1)S(1)} %copy-done.11, f32[2048,256]{1,0:T(8,128)S(1)} %collective-permute-done.refs_0_.refs_2_, f32[40,2048]{1,0:T(8,128)S(1)} %collective-permute-done.1.refs_1_.refs_3_, ...), custom_call_target="tpu_custom_call" | custom-call | flops 4294967296 | bytes 4194304 | tf_op jit(solution)/shard_map/hist/pallas_call | solution.py:244
  102.1 3.2 %collective-permute-start.11 = (f32[2,16,256]{2,1,0:T(8,128)S(1)}, f32[2,16,256]{2,1,0:T(8,128)S(1)}, u32[]{:S(2)}, u32[]{:S(2)}) collective-permute-start(f32[2,16,256]{2,1,0:T(8,128)S(1)} %gains.2.refs_0_), channel_id=1, source_target_pairs={{0,8},{4,12},{8,0},{12,4},{1,9},{5,13},{9,1},{13,5},{2,10},{6,14},... | collective-permute-start | bytes 98312 | tf_op jit(solution)/shard_map/ppermute | solution.py:571
  105.3 2.7 %gains.3.refs_0_.refs_5_ = f32[2,16,256]{2,1,0:T(8,128)S(1)} custom-call(f32[528,256]{1,0:T(8,128)S(1)} %hist.18.last_ref, f32[528,256]{1,0:T(8,128)S(1)} %collective-permute-done.14.right_ref, f32[528,256]{1,0:T(8,128)S(1)} %collective-permute-done.17.left_ref, f32[512,256]{1,0:T(8,128)S(1)} %get-tuple-element.22.par_grad_ref, ...), custom_call_target="tpu_custom_call" | custom-call | flops 6553600 | bytes 2097152 | tf_op jit(solution)/shard_map/gains/pallas_call | solution.py:401
  108.0 3.8 %collective-permute-start.20 = (f32[2,16,256]{2,1,0:T(8,128)S(1)}, f32[2,16,256]{2,1,0:T(8,128)S(1)}, u32[]{:S(2)}, u32[]{:S(2)}) collective-permute-start(f32[2,16,256]{2,1,0:T(8,128)S(1)} %gains.3.refs_0_.refs_5_), channel_id=1, source_target_pairs={{0,12},{4,0},{8,4},{12,8},{1,13},{5,1},{9,5},{13,9},{2,14},{6,2},{... | collective-permute-start | bytes 98312 | tf_op jit(solution)/shard_map/ppermute | solution.py:571
  113.7 1.5 %choose.2 = f32[2,16,256]{2,1,0:T(8,128)} custom-call(s32[8]{0:T(128)} %child_ref.5, s32[8]{0:T(128)} %parent_ref.5, f32[2,16,256]{2,1,0:T(8,128)} %copy-done.1, f32[2,16,256]{2,1,0:T(8,128)} %copy-done.14, f32[2,16,256]{2,1,0:T(8,128)} %copy-done.13, f32[2,16,256]{2,1,0:T(8,128)} %copy-done.12), custom_call_target="tpu_custom_call" | custom-call | tf_op jit(solution)/shard_map/choose/pallas_call | solution.py:435
  115.2 1.5 %collective-permute-done.19.refs_2_.refs_7_ = f32[2,16,256]{2,1,0:T(8,128)S(1)} collective-permute-done((f32[2,16,256]{2,1,0:T(8,128)S(1)}, f32[2,16,256]{2,1,0:T(8,128)S(1)}, u32[]{:S(2)}, u32[]{:S(2)}) %collective-permute-start.19) | collective-permute-done | bytes 32800 | tf_op jit(solution)/shard_map/ppermute | solution.py:571
  118.2 1.5 %choose.3 = f32[2,16,256]{2,1,0:T(8,128)} custom-call(s32[8]{0:T(128)} %child_ref.5, s32[8]{0:T(128)} %parent_ref.5, f32[2,16,256]{2,1,0:T(8,128)} %copy-done.2, f32[2,16,256]{2,1,0:T(8,128)} %copy-done.17, f32[2,16,256]{2,1,0:T(8,128)} %copy-done.16, f32[2,16,256]{2,1,0:T(8,128)} %copy-done.15), custom_call_target="tpu_custom_call" | custom-call | tf_op jit(solution)/shard_map/choose/pallas_call | solution.py:435
  121.7 1.8 %finish.1 = f32[64,2,128]{2,1,0:T(2,128)} custom-call(s32[8]{0:T(128)} %child_ref.5, s32[8]{0:T(128)} %parent_ref.5, f32[2,16,256]{2,1,0:T(8,128)} %copy-done.1, f32[2,16,256]{2,1,0:T(8,128)} %copy-done.14, f32[2,16,256]{2,1,0:T(8,128)} %copy-done.13, f32[2,16,256]{2,1,0:T(8,128)} %copy-done.12, f32[2,16,256]{2,1,0:T(8,128)} %copy-done.18, ...), custom_call_target="tpu_custom_call" | custom-call | tf_op jit(solution)/shard_map/finish/pallas_call | solution.py:485
  (82 shorter events, 19.1 us)
Async XLA Ops:
  9.4 11.0 %collective-permute-start = (f32[2048,256]{1,0:T(8,128)}, f32[2048,256]{1,0:T(8,128)S(1)}, u32[]{:S(2)}, u32[]{:S(2)}) collective-permute-start(f32[2048,256]{1,0:T(8,128)} %get-tuple-element.17), channel_id=1, source_target_pairs={{0,1},{1,0},{2,3},{3,2},{4,5},{5,4},{6,7},{7,6},{8,9},{9,8},{10,11... | collective-permute-start | bytes 6291464 | tf_op jit(solution)/shard_map/ppermute | solution.py:517
  9.9 10.5 %collective-permute-start.1 = (f32[40,2048]{1,0:T(8,128)}, f32[40,2048]{1,0:T(8,128)S(1)}, u32[]{:S(2)}, u32[]{:S(2)}) collective-permute-start(f32[40,2048]{1,0:T(8,128)} %get-tuple-element.18), channel_id=1, source_target_pairs={{0,1},{1,0},{2,3},{3,2},{4,5},{5,4},{6,7},{7,6},{8,9},{9,8},{10,11... | collective-permute-start | bytes 983048 | tf_op jit(solution)/shard_map/ppermute | solution.py:516
  24.6 17.9 %collective-permute-start.7 = (f32[528,256]{1,0:T(8,128)S(1)}, f32[528,256]{1,0:T(8,128)S(1)}, u32[]{:S(2)}, u32[]{:S(2)}) collective-permute-start(f32[528,256]{1,0:T(8,128)S(1)} %hist.11), channel_id=1, source_target_pairs={{12,8},{13,9},{14,10},{15,11},{28,24},{29,25},{30,26},{31,27}} | collective-permute-start | bytes 1622024 | tf_op jit(solution)/shard_map/ppermute | solution.py:558
  25.4 17.6 %collective-permute-start.2 = (f32[528,256]{1,0:T(8,128)S(1)}, f32[528,256]{1,0:T(8,128)S(1)}, u32[]{:S(2)}, u32[]{:S(2)}) collective-permute-start(f32[528,256]{1,0:T(8,128)S(1)} %hist.11), channel_id=1, source_target_pairs={{0,4},{1,5},{2,6},{3,7},{16,20},{17,21},{18,22},{19,23}} | collective-permute-start | bytes 1622024 | tf_op jit(solution)/shard_map/ppermute | solution.py:557
  34.5 20.3 %collective-permute-start.3 = (f32[528,256]{1,0:T(8,128)S(1)}, f32[528,256]{1,0:T(8,128)S(1)}, u32[]{:S(2)}, u32[]{:S(2)}) collective-permute-start(f32[528,256]{1,0:T(8,128)S(1)} %hist.14.refs_4_), channel_id=1, source_target_pairs={{0,4},{1,5},{2,6},{3,7},{16,20},{17,21},{18,22},{19,23}} | collective-permute-start | bytes 1622024 | tf_op jit(solution)/shard_map/ppermute | solution.py:557
  35.8 19.0 %collective-permute-start.15 = (f32[528,256]{1,0:T(8,128)S(1)}, f32[528,256]{1,0:T(8,128)S(1)}, u32[]{:S(2)}, u32[]{:S(2)}) collective-permute-start(f32[528,256]{1,0:T(8,128)S(1)} %hist.14.refs_4_), channel_id=1, source_target_pairs={{12,8},{13,9},{14,10},{15,11},{28,24},{29,25},{30,26},{31,27}} | collective-permute-start | bytes 1622024 | tf_op jit(solution)/shard_map/ppermute | solution.py:558
  43.1 23.7 %collective-permute-start.8 = (f32[528,256]{1,0:T(8,128)S(1)}, f32[528,256]{1,0:T(8,128)S(1)}, u32[]{:S(2)}, u32[]{:S(2)}) collective-permute-start(f32[528,256]{1,0:T(8,128)S(1)} %get-tuple-element.27), channel_id=1, source_target_pairs={{12,8},{8,4},{13,9},{9,5},{14,10},{10,6},{15,11},{11,7},{28,24},{2... | collective-permute-start | bytes 1622024 | tf_op jit(solution)/shard_map/ppermute | solution.py:558
  43.8 23.0 %collective-permute-start.5 = (f32[528,256]{1,0:T(8,128)S(1)}, f32[528,256]{1,0:T(8,128)S(1)}, u32[]{:S(2)}, u32[]{:S(2)}) collective-permute-start(f32[528,256]{1,0:T(8,128)S(1)} %get-tuple-element.28), channel_id=1, source_target_pairs={{0,4},{4,8},{1,5},{5,9},{2,6},{6,10},{3,7},{7,11},{16,20},{20,24},... | collective-permute-start | bytes 1622024 | tf_op jit(solution)/shard_map/ppermute | solution.py:557
  55.0 24.5 %collective-permute-start.16 = (f32[528,256]{1,0:T(8,128)S(1)}, f32[528,256]{1,0:T(8,128)S(1)}, u32[]{:S(2)}, u32[]{:S(2)}) collective-permute-start(f32[528,256]{1,0:T(8,128)S(1)} %get-tuple-element.25), channel_id=1, source_target_pairs={{12,8},{8,4},{13,9},{9,5},{14,10},{10,6},{15,11},{11,7},{28,24},{2... | collective-permute-start | bytes 1622024 | tf_op jit(solution)/shard_map/ppermute | solution.py:558
  55.7 23.8 %collective-permute-start.4 = (f32[528,256]{1,0:T(8,128)S(1)}, f32[528,256]{1,0:T(8,128)S(1)}, u32[]{:S(2)}, u32[]{:S(2)}) collective-permute-start(f32[528,256]{1,0:T(8,128)S(1)} %get-tuple-element.26), channel_id=1, source_target_pairs={{0,4},{4,8},{1,5},{5,9},{2,6},{6,10},{3,7},{7,11},{16,20},{20,24},... | collective-permute-start | bytes 1622024 | tf_op jit(solution)/shard_map/ppermute | solution.py:557
  67.0 26.0 %collective-permute-start.9 = (f32[528,256]{1,0:T(8,128)S(1)}, f32[528,256]{1,0:T(8,128)S(1)}, u32[]{:S(2)}, u32[]{:S(2)}) collective-permute-start(f32[528,256]{1,0:T(8,128)S(1)} %get-tuple-element.31), channel_id=1, source_target_pairs={{12,8},{8,4},{4,0},{13,9},{9,5},{5,1},{14,10},{10,6},{6,2},{15,11}... | collective-permute-start | bytes 1622024 | tf_op jit(solution)/shard_map/ppermute | solution.py:558
  68.3 24.7 %collective-permute-start.6 = (f32[528,256]{1,0:T(8,128)S(1)}, f32[528,256]{1,0:T(8,128)S(1)}, u32[]{:S(2)}, u32[]{:S(2)}) collective-permute-start(f32[528,256]{1,0:T(8,128)S(1)} %get-tuple-element.32), channel_id=1, source_target_pairs={{0,4},{4,8},{8,12},{1,5},{5,9},{9,13},{2,6},{6,10},{10,14},{3,7},{... | collective-permute-start | bytes 1622024 | tf_op jit(solution)/shard_map/ppermute | solution.py:557
  79.7 25.7 %collective-permute-start.17 = (f32[528,256]{1,0:T(8,128)S(1)}, f32[528,256]{1,0:T(8,128)S(1)}, u32[]{:S(2)}, u32[]{:S(2)}) collective-permute-start(f32[528,256]{1,0:T(8,128)S(1)} %get-tuple-element.29), channel_id=1, source_target_pairs={{12,8},{8,4},{4,0},{13,9},{9,5},{5,1},{14,10},{10,6},{6,2},{15,11}... | collective-permute-start | bytes 1622024 | tf_op jit(solution)/shard_map/ppermute | solution.py:558
  81.0 12.0 %copy-start.6 = (s32[2]{0:T(128)S(1)}, s32[2]{0:T(128)}, u32[]{:S(2)}) copy-start(s32[2]{0:T(128)} %low_ref.3) | copy-start | bytes 28
  81.0 12.0 %copy-start.7 = (s32[2]{0:T(128)S(1)}, s32[2]{0:T(128)}, u32[]{:S(2)}) copy-start(s32[2]{0:T(128)} %high_ref.3) | copy-start | bytes 28
  81.0 24.3 %collective-permute-start.14 = (f32[528,256]{1,0:T(8,128)S(1)}, f32[528,256]{1,0:T(8,128)S(1)}, u32[]{:S(2)}, u32[]{:S(2)}) collective-permute-start(f32[528,256]{1,0:T(8,128)S(1)} %get-tuple-element.30), channel_id=1, source_target_pairs={{0,4},{4,8},{8,12},{1,5},{5,9},{9,13},{2,6},{6,10},{10,14},{3,7},{... | collective-permute-start | bytes 1622024 | tf_op jit(solution)/shard_map/ppermute | solution.py:557
  95.7 16.1 %collective-permute-start.12 = (f32[2,16,256]{2,1,0:T(8,128)S(1)}, f32[2,16,256]{2,1,0:T(8,128)S(1)}, u32[]{:S(2)}, u32[]{:S(2)}) collective-permute-start(f32[2,16,256]{2,1,0:T(8,128)S(1)} %gains.2.refs_0_), channel_id=1, source_target_pairs={{0,12},{4,0},{8,4},{12,8},{1,13},{5,1},{9,5},{13,9},{2,14},{6,2},{... | collective-permute-start | bytes 98312 | tf_op jit(solution)/shard_map/ppermute | solution.py:571
  102.1 10.4 %collective-permute-start.11 = (f32[2,16,256]{2,1,0:T(8,128)S(1)}, f32[2,16,256]{2,1,0:T(8,128)S(1)}, u32[]{:S(2)}, u32[]{:S(2)}) collective-permute-start(f32[2,16,256]{2,1,0:T(8,128)S(1)} %gains.2.refs_0_), channel_id=1, source_target_pairs={{0,8},{4,12},{8,0},{12,4},{1,9},{5,13},{9,1},{13,5},{2,10},{6,14},... | collective-permute-start | bytes 98312 | tf_op jit(solution)/shard_map/ppermute | solution.py:571
  105.3 7.2 %collective-permute-start.10 = (f32[2,16,256]{2,1,0:T(8,128)S(1)}, f32[2,16,256]{2,1,0:T(8,128)S(1)}, u32[]{:S(2)}, u32[]{:S(2)}) collective-permute-start(f32[2,16,256]{2,1,0:T(8,128)S(1)} %gains.2.refs_0_), channel_id=1, source_target_pairs={{0,4},{4,8},{8,12},{12,0},{1,5},{5,9},{9,13},{13,1},{2,6},{6,10},{... | collective-permute-start | bytes 98312 | tf_op jit(solution)/shard_map/ppermute | solution.py:571
  108.0 7.1 %collective-permute-start.20 = (f32[2,16,256]{2,1,0:T(8,128)S(1)}, f32[2,16,256]{2,1,0:T(8,128)S(1)}, u32[]{:S(2)}, u32[]{:S(2)}) collective-permute-start(f32[2,16,256]{2,1,0:T(8,128)S(1)} %gains.3.refs_0_.refs_5_), channel_id=1, source_target_pairs={{0,12},{4,0},{8,4},{12,8},{1,13},{5,1},{9,5},{13,9},{2,14},{6,2},{... | collective-permute-start | bytes 98312 | tf_op jit(solution)/shard_map/ppermute | solution.py:571
  111.8 4.8 %collective-permute-start.19 = (f32[2,16,256]{2,1,0:T(8,128)S(1)}, f32[2,16,256]{2,1,0:T(8,128)S(1)}, u32[]{:S(2)}, u32[]{:S(2)}) collective-permute-start(f32[2,16,256]{2,1,0:T(8,128)S(1)} %gains.3.refs_0_.refs_5_), channel_id=1, source_target_pairs={{0,8},{4,12},{8,0},{12,4},{1,9},{5,13},{9,1},{13,5},{2,10},{6,14},... | collective-permute-start | bytes 98312 | tf_op jit(solution)/shard_map/ppermute | solution.py:571
  111.8 5.8 %collective-permute-start.18 = (f32[2,16,256]{2,1,0:T(8,128)S(1)}, f32[2,16,256]{2,1,0:T(8,128)S(1)}, u32[]{:S(2)}, u32[]{:S(2)}) collective-permute-start(f32[2,16,256]{2,1,0:T(8,128)S(1)} %gains.3.refs_0_.refs_5_), channel_id=1, source_target_pairs={{0,4},{4,8},{8,12},{12,0},{1,5},{5,9},{9,13},{13,1},{2,6},{6,10},{... | collective-permute-start | bytes 98312 | tf_op jit(solution)/shard_map/ppermute | solution.py:571
  115.2 4.5 %collective-permute-start.13 = (f32[2,16,256]{2,1,0:T(8,128)}, f32[2,16,256]{2,1,0:T(8,128)S(1)}, u32[]{:S(2)}, u32[]{:S(2)}) collective-permute-start(f32[2,16,256]{2,1,0:T(8,128)} %choose.2), channel_id=1, source_target_pairs={{0,1},{1,0},{2,3},{3,2},{4,5},{5,4},{6,7},{7,6},{8,9},{9,8},{10,11... | collective-permute-start | bytes 98312 | tf_op jit(solution)/shard_map/ppermute | solution.py:572
  119.7 1.4 %collective-permute-start.21 = (f32[2,16,256]{2,1,0:T(8,128)}, f32[2,16,256]{2,1,0:T(8,128)S(1)}, u32[]{:S(2)}, u32[]{:S(2)}) collective-permute-start(f32[2,16,256]{2,1,0:T(8,128)} %choose.3), channel_id=1, source_target_pairs={{0,1},{1,0},{2,3},{3,2},{4,5},{5,4},{6,7},{7,6},{8,9},{9,8},{10,11... | collective-permute-start | bytes 98312 | tf_op jit(solution)/shard_map/ppermute | solution.py:572
  (18 other events, 88.7 us)
where the time goes:
time: 124 us
  Pallas kernels  71.7 us (58%)
  starting transfers between devices  40.5 us (33%)
  local copies, waits for them, and re-layouts  4.62 us (4%)
  waiting for transfers between devices  4.39 us (4%)
  other arithmetic  1.85 us (1%)
    pallas_call x10, Pallas kernels, hist(): pl.pallas_call(functools.partial(hist_kernel, first_column, width, levels...  52.3 us
    ppermute x6, starting transfers between devices, per_device(): lax.ppermute(to_right, 'dp', [(i, i + 1) for i in range(step + 1)])  26.3 us
    pallas_call x1, Pallas kernels, prep(): pl.pallas_call(functools.partial(prep_kernel, line, slab), in_specs=[SMEM...  8.09 us
    ppermute x6, starting transfers between devices, per_device(): lax.ppermute(gain, 'dp', [(i, (i + s) % line) for i in range(line)])  8.06 us
    ppermute x6, starting transfers between devices, per_device(): lax.ppermute(to_left, 'dp', [(line - 1 - i, line - 2 - i) for i in range(...  5.5 us
    pallas_call x2, Pallas kernels, gains_of(): pl.pallas_call(functools.partial(gain_kernel, width, levels, kdim), in_sp...  5.33 us
    unnamed x40, local copies, waits for them, and re-layouts  4.62 us
    pallas_call x2, Pallas kernels, choose(): pl.pallas_call(functools.partial(choose_kernel, line), in_specs=[SMEM_SPE...  2.94 us
  transfers between devices with their start and end apart: 22, of which 4 were waited for; matrix products, arithmetic and copies ran while one was open for 0% of the time, Pallas kernels for 47%

commit v1 on v0

--- a/solution.py
+++ b/solution.py
@@ -23,10 +23,12 @@
     for z in range(line):
         mine = []
         for step in range(line - 1):
+            now = []
             if z <= step:
-                mine.append(("R", step, line - 1 - step + z))
+                now.append(("R", step, line - 1 - step + z))
             if line - 1 - z <= step:
-                mine.append(("L", step, step - (line - 1 - z)))
+                now.append(("L", step, step - (line - 1 - z)))
+            mine.extend(now if 2 * z < line else now[::-1])
         mine.append(("F", line - 1, z))
         roles.append(mine)
     return roles
@@ -44,6 +46,7 @@
         copies.append(pltpu.make_async_copy(bins_ref.at[part, :], buf_ref.at[part, :], sems.at[i]))
         copies[-1].start()
 
+    hess_row = hess_ref[...].astype(jnp.float32).reshape(1, rows)
     ones = [jnp.where(side_ref[:, i * TILE : (i + 1) * TILE] == 1, 1.0, 0.0) for i in range(blocks)]
     counts = [jnp.sum(x).astype(jnp.int32) for x in ones]
     bases = [jnp.int32(0)]
@@ -79,7 +82,7 @@
         part = slice(i * TILE, (i + 1) * TILE)
         goal = jnp.where(ones[i] > 0.5, ahead[i : i + 1] + (bases[i] - starts[i]), -1)
         pack = jnp.where(slot == goal, 1.0, 0.0).astype(jnp.bfloat16)
-        hess = jnp.broadcast_to(hess_ref[:, part], (16, TILE))
+        hess = jnp.broadcast_to(hess_row[:, part], (16, TILE))
         first = lax.broadcasted_iota(jnp.int32, hess.shape, 0) == 0
         weights = jnp.concatenate([grads_ref[:, part].astype(jnp.float32), jnp.where(first, hess, 0.0)], axis=0)
         packed_w = lax.dot_general(weights.astype(jnp.bfloat16), pack, (((1,), (1,)), ((), ())), preferred_element_type=jnp.float32)
@@ -132,7 +135,7 @@
         compiler_params=pltpu.CompilerParams(vmem_limit_bytes=PREP_MIB * MIB),
         cost_estimate=pl.CostEstimate(flops=4 * rows * f_dev * f_dev, bytes_accessed=8 * rows * f_dev, transcendentals=0),
         name="prep",
-    )(owners, bins, grads.T, hess.astype(jnp.float32).reshape(1, rows), side.reshape(1, rows))
+    )(owners, bins, grads.T, hess, side.reshape(1, rows))
 
 
 def tiles_in(wt_ref, kdim):
@@ -153,10 +156,10 @@
     one = jnp.ones((TILE, lanes), jnp.bfloat16)
     zero = jnp.zeros((TILE, lanes), jnp.bfloat16)
 
-    def place_rows(bins_ref, source, target):
-        block = bins_ref[pl.ds(source, PACK), :].astype(jnp.bfloat16)
+    def place_rows(bins_ref, source, target, size):
+        block = bins_ref[pl.ds(source, size), :].astype(jnp.bfloat16)
         moved = jnp.dot(block, spread, preferred_element_type=jnp.float32)
-        rel_ref[pl.ds(target, PACK), :] = (moved - shift).astype(jnp.bfloat16)
+        rel_ref[pl.ds(target, size), :] = (moved - shift).astype(jnp.bfloat16)
 
     def place_weights(height):
         for i, (_, w_ref) in enumerate(pairs):
@@ -180,8 +183,8 @@
     def fast():
         height = FAST * PACK
         for i, (bins_ref, _) in enumerate(pairs):
-            for r in range(0, height, PACK):
-                place_rows(bins_ref, r, i * height + r)
+            for r in range(0, height, 3 * PACK):
+                place_rows(bins_ref, r, i * height + r, 3 * PACK)
         place_weights(height)
         tiles = [(r, min(TILE, parts * height - r)) for r in range(0, parts * height, TILE)]
 
@@ -201,7 +204,7 @@
 
             def one_pack(p, carry):
                 r = pl.multiple_of(p * PACK, PACK)
-                place_rows(bins_ref, r, i * rows + r)
+                place_rows(bins_ref, r, i * rows + r, PACK)
                 return carry
 
             lax.fori_loop(0, rows // PACK, one_pack, 0)
@@ -258,6 +261,13 @@
     )(*operands, *tie)
 
 
+def source_of(place, child_ref, parent_ref):
+    source = jnp.int32(0)
+    for q in range(child_ref.shape[0]):
+        source = jnp.where(child_ref[q] == place, parent_ref[q], source)
+    return source
+
+
 def repeat_lanes(x, width, lanes):
     if lanes > x.shape[1]:
         x = jnp.concatenate([x] * (lanes // x.shape[1]), axis=1)
@@ -269,13 +279,19 @@
     return x
 
 
-def layout_kernel(width, levels, kdim, chunks, owner_ref, sign_ref, parent_ref, hess_ref, tie_ref, *out_refs):
+def layout_kernel(width, levels, kdim, chunks, line, child_ref, owner_ref, sign_ref, parent_ref, hess_ref, tie_ref, *out_refs):
     del tie_ref
-    grad_refs, hess_refs, sign_refs = out_refs[:chunks], out_refs[chunks : 2 * chunks], out_refs[2 * chunks :]
+    grad_refs, hess_refs, sign_refs = out_refs[:chunks], out_refs[chunks : 2 * chunks], out_refs[2 * chunks : 3 * chunks]
     lanes = grad_refs[0].shape[1]
     slab = width * chunks
     owners = owner_ref.shape[0]
-    place = 2 * lax.axis_index("dp") + lax.axis_index("sub")
+    z, core = lax.axis_index("dp"), lax.axis_index("sub")
+    place = 2 * z + core
+    mine = source_of(place, child_ref, owner_ref)
+    twin = source_of(2 * z + 1 - core, child_ref, owner_ref)
+    row = lax.broadcasted_iota(jnp.int32, (8, 128), 0)
+    route = jnp.where(row == 0, lax.rem(z - mine // 2 + line, line), lax.rem(z - twin // 2 + line, line))
+    out_refs[-1][...] = jnp.where(row == 2, jnp.where(lax.rem(mine, 2) == core, 1, 0), route)
     slab_at = jnp.int32(0)
     for q in range(owners):
         slab_at = jnp.where(owner_ref[q] == place, q, slab_at)
@@ -306,20 +322,21 @@
                 grad_refs[c][b * kdim : b * kdim + 128, tile * 128 : (tile + 1) * 128] = block.T
 
 
-def parent_layout(width, levels, lanes, kdim, chunks, owners, signs, parent, hess, tie):
+def parent_layout(width, levels, lanes, kdim, chunks, line, child_owner, owners, signs, parent, hess, tie):
     shapes = [jax.ShapeDtypeStruct((levels * kdim, lanes), jnp.float32)] * chunks
     shapes += [jax.ShapeDtypeStruct((levels, lanes), jnp.float32)] * chunks
     shapes += [jax.ShapeDtypeStruct((8, lanes), jnp.int32)] * chunks
+    shapes += [jax.ShapeDtypeStruct((8, 128), jnp.int32)]
     out = pl.pallas_call(
-        functools.partial(layout_kernel, width, levels, kdim, chunks),
-        in_specs=[SMEM_SPEC] + [VMEM_SPEC] * 3 + [pl.BlockSpec(memory_space=pl.ANY)],
-        out_specs=[VMEM_SPEC] * (3 * chunks),
+        functools.partial(layout_kernel, width, levels, kdim, chunks, line),
+        in_specs=[SMEM_SPEC] * 2 + [VMEM_SPEC] * 3 + [pl.BlockSpec(memory_space=pl.ANY)],
+        out_specs=[VMEM_SPEC] * (3 * chunks + 1),
         out_shape=shapes,
         compiler_params=pltpu.CompilerParams(vmem_limit_bytes=16 * MIB),
         cost_estimate=pl.CostEstimate(flops=0, bytes_accessed=2 * parent.size * 4, transcendentals=0),
         name="parent_layout",
-    )(owners, signs.reshape(1, -1), parent, hess, tie)
-    return out[:chunks], out[chunks : 2 * chunks], out[2 * chunks :]
+    )(child_owner, owners, signs.reshape(1, -1), parent, hess, tie)
+    return out[:chunks], out[chunks : 2 * chunks], out[2 * chunks : 3 * chunks], out[-1]
 
 
 def lane_prefix(total, width):
@@ -413,59 +430,23 @@
     )(last, right, left, par_grad, par_hess, sign, node_low, node_high)
 
 
-def source_of(place, child_ref, parent_ref):
-    source = jnp.int32(0)
-    for q in range(child_ref.shape[0]):
-        source = jnp.where(child_ref[q] == place, parent_ref[q], source)
-    return source
-
-
-def choose_kernel(line, child_ref, parent_ref, *refs):
-    z, core = lax.axis_index("dp"), lax.axis_index("sub")
-    chip = source_of(2 * z + 1 - core, child_ref, parent_ref) // 2
+def chosen(shift, got):
+    value = got[0]
+    for s in range(1, len(got)):
+        value = jnp.where(shift == s, got[s], value)
+    return value
+
+
+def finish_kernel(width, *refs):
     out_ref = refs[-1]
-    for s in range(line):
-
-        @pl.when(lax.rem(z - chip + line, line) == s)
-        def _():
-            out_ref[...] = refs[s][...]
-
-
-def choose(line, child_owner, parent_owner, got):
-    return pl.pallas_call(
-        functools.partial(choose_kernel, line),
-        in_specs=[SMEM_SPEC] * 2 + [VMEM_SPEC] * line,
-        out_specs=VMEM_SPEC,
-        out_shape=jax.ShapeDtypeStruct(got[0].shape, jnp.float32),
-        name="choose",
-    )(child_owner, parent_owner, *got)
-
-
-def finish_kernel(line, chunks, width, child_ref, parent_ref, *refs):
-    out_ref, held_ref = refs[-2:]
-    z, core = lax.axis_index("dp"), lax.axis_index("sub")
-    source = source_of(2 * z + core, child_ref, parent_ref)
-    same = lax.rem(source, 2) == core
-    shift = lax.rem(z - source // 2 + line, line)
-    for c in range(chunks):
-        got = refs[c * (line + 1) : (c + 1) * (line + 1)]
-        for s in range(line):
-
-            @pl.when(same & (shift == s))
-            def _():
-                held_ref[c] = got[s][...]
-
-        @pl.when(jnp.logical_not(same))
-        def _():
-            held_ref[c] = got[line][...]
-
+    chunks = len(refs) - 1
     slab = width * chunks
-    lanes = held_ref.shape[3]
+    lanes = refs[0].shape[2]
     total = jnp.zeros((128, 128), jnp.float32)
     column = lax.broadcasted_iota(jnp.int32, (128, 128), 1)
     for child in range(2):
         for c in range(chunks):
-            gain = held_ref[c, child]
+            gain = refs[c][child]
             at = child * slab + c * width
             pieces = []
             for j in range(lanes // width):
@@ -479,17 +460,14 @@
         out_ref[:, child, :] = turned[child * slab : (child + 1) * slab]
 
 
-def finish(line, chunks, width, nbins, child_owner, parent_owner, parts):
-    shape = parts[0][0].shape
-    flat = [x for part in parts for x in part]
+def finish(width, nbins, parts):
     return pl.pallas_call(
-        functools.partial(finish_kernel, line, chunks, width),
-        in_specs=[SMEM_SPEC] * 2 + [VMEM_SPEC] * len(flat),
+        functools.partial(finish_kernel, width),
+        in_specs=[VMEM_SPEC] * len(parts),
         out_specs=VMEM_SPEC,
-        out_shape=jax.ShapeDtypeStruct((width * chunks, 2, nbins), jnp.float32),
-        scratch_shapes=[pltpu.VMEM((chunks, *shape), jnp.float32)],
+        out_shape=jax.ShapeDtypeStruct((width * len(parts), 2, nbins), jnp.float32),
         name="finish",
-    )(child_owner, parent_owner, *flat)
+    )(*parts)
 
 
 def one_of(z, members):
@@ -499,30 +477,12 @@
     return hit
 
 
-def per_device(bins, grads, hess, node_side, signs, child_owner, parent_owner, parent_grad, parent_hess, node_low, node_high):
-    line = lax.axis_size("dp")
+def sum_line(line, chunks, units, unit, set_up):
+    plan = plan_of(line)
     z = lax.axis_index("dp")
-    kdim = grads.shape[1]
-    nbins = parent_hess.shape[2]
-    slab = parent_grad.shape[1]
-    chunks = CHUNKS if slab >= 32 else 1
-    width = slab // chunks
-    lanes = min(256, width * nbins * kdim // 128)
-    levels = nbins // (lanes // width)
-    plan = plan_of(line)
-
-    own, send, wt, wt_send = prep(line, slab, parent_owner, bins, grads, hess, node_side)
-    swap = [(0, 1), (1, 0)]
-    wt_other = lax.ppermute(wt_send, "sub", swap)
-    other = lax.ppermute(send, "sub", swap)
-    mine = (own, wt)
-    theirs = (other, wt_other)
-
-    units = {}
-    for c in range(chunks):
-        units[0, c] = hist(c * width, width, levels, lanes, kdim, [mine])
-    for c in range(chunks):
-        units[0, c] = hist(c * width, width, levels, lanes, kdim, [theirs], units[0, c])
+    from_left = [None] * chunks
+    from_right = [None] * chunks
+    arrived = []
 
     def pick(kind, step, c):
         where_at = {}
@@ -536,19 +496,15 @@
             value = jnp.where(one_of(z, where_at[p]), units[p, c], value)
         return value
 
-    from_left = [None] * chunks
-    from_right = [None] * chunks
-    arrived = []
-
     def tie_of(step, c):
         at = min(step * chunks + c - 3, (line - 2) * chunks - 1)
         return (arrived[at],) if at >= 0 else (units[0, chunks - 1],)
 
     last = line - 1
-    for step in range(line - 1):
+    for step in range(last):
         for c in range(chunks):
             if step > 0:
-                units[step, c] = hist(step * slab + c * width, width, levels, lanes, kdim, [mine, theirs], tie=tie_of(step, c))
+                units[step, c] = unit(step, c, tie_of(step, c))
             to_right = pick("R", step, c)
             to_left = pick("L", step, c)
             if step > 0:
@@ -557,21 +513,74 @@
             from_left[c] = lax.ppermute(to_right, "dp", [(i, i + 1) for i in range(step + 1)])
             from_right[c] = lax.ppermute(to_left, "dp", [(line - 1 - i, line - 2 - i) for i in range(step + 1)])
             arrived.append(from_left[c])
-    par_grad, par_hess, sign = parent_layout(
-        width, levels, lanes, kdim, chunks, parent_owner, signs, parent_grad[0], parent_hess[0], tie_of(last, 0)[0]
-    )
+    layout = set_up(tie_of(last, 0)[0])
+    return [unit(last, c, tie_of(last, c)) for c in range(chunks)], from_left, from_right, layout
+
+
+def sum_line_of_4(line, chunks, units, unit, set_up):
+    inward, outer, middle = [(0, 1), (3, 2)], [(0, 1), (1, 0), (2, 3), (3, 2)], [(1, 2), (2, 1)]
+    every = range(chunks)
+    a0 = [lax.ppermute(units[0, c], "dp", inward) for c in every]
+    a1, b1, a2, b2 = [None] * chunks, [None] * chunks, [None] * chunks, [None] * chunks
+    for c in every:
+        units[1, c] = unit(1, c, (a0[c - 1],) if c else (units[0, chunks - 1],))
+        a1[c] = lax.ppermute(units[1, c], "dp", inward)
+        b1[c] = lax.ppermute(units[0, c] + a0[c], "dp", middle)
+    last = [None] * chunks
+    last[0] = unit(3, 0, (a0[chunks - 1],))
+    for c in every:
+        units[2, c] = unit(2, c, (a1[0],))
+        b2[c] = lax.ppermute(units[1, c] + a1[c], "dp", middle)
+        a2[c] = lax.ppermute(units[2, c] + b1[c], "dp", outer)
+    layout = set_up(a1[chunks - 1])
+    for c in range(1, chunks):
+        last[c] = unit(3, c, (a1[chunks - 1],))
+    return last, a2, b2, layout
+
+
+def per_device(bins, grads, hess, node_side, signs, child_owner, parent_owner, parent_grad, parent_hess, node_low, node_high):
+    line = lax.axis_size("dp")
+    kdim = grads.shape[1]
+    nbins = parent_hess.shape[2]
+    slab = parent_grad.shape[1]
+    chunks = CHUNKS if slab >= 32 else 1
+    width = slab // chunks
+    lanes = min(256, width * nbins * kdim // 128)
+    levels = nbins // (lanes // width)
+
+    own, send, wt, wt_send = prep(line, slab, parent_owner, bins, grads, hess, node_side)
+    swap = [(0, 1), (1, 0)]
+    wt_other = lax.ppermute(wt_send, "sub", swap)
+    other = lax.ppermute(send, "sub", swap)
+    mine = (own, wt)
+    theirs = (other, wt_other)
+
+    def unit(p, c, pairs, init=None, tie=()):
+        return hist(p * slab + c * width, width, levels, lanes, kdim, pairs, init, tie)
+
+    def set_up(tie):
+        return parent_layout(
+            width, levels, lanes, kdim, chunks, line, child_owner, parent_owner, signs, parent_grad[0], parent_hess[0], tie
+        )
+
+    units = {}
     for c in range(chunks):
-        units[last, c] = hist(last * slab + c * width, width, levels, lanes, kdim, [mine, theirs], tie=tie_of(last, c))
+        units[0, c] = unit(0, c, [mine])
+    for c in range(chunks):
+        units[0, c] = unit(0, c, [theirs], units[0, c], (units[0, c - 1],) if c else ())
+    collect = sum_line_of_4 if line == 4 else sum_line
+    last, from_left, from_right, layout = collect(line, chunks, units, lambda p, c, tie: unit(p, c, [mine, theirs], tie=tie), set_up)
+    par_grad, par_hess, sign, route = layout
 
     done = []
     for c in range(chunks):
         gain = gains_of(
-            width, levels, lanes, kdim, units[last, c], from_left[c], from_right[c], par_grad[c], par_hess[c], sign[c], node_low, node_high
+            width, levels, lanes, kdim, last[c], from_left[c], from_right[c], par_grad[c], par_hess[c], sign[c], node_low, node_high
         )
         got = [gain] + [lax.ppermute(gain, "dp", [(i, (i + s) % line) for i in range(line)]) for s in range(1, line)]
-        got.append(lax.ppermute(choose(line, child_owner, parent_owner, got), "sub", swap))
-        done.append(got)
-    return finish(line, chunks, width, nbins, child_owner, parent_owner, done)[None]
+        crossed = lax.ppermute(chosen(route[1, 0], got), "sub", swap)
+        done.append(jnp.where(route[2, 0] == 1, chosen(route[0, 0], got), crossed))
+    return finish(width, nbins, done)[None]
 
 
 def solution(mesh):

time: 124 us -> 147 us (1.19)
  waiting for transfers between devices: 4.39 us -> 39.2 us
  starting transfers between devices: 40.5 us -> 29.4 us
  between operations: 0.51 us -> 4.68 us
  Pallas kernels: 71.7 us -> 68.5 us
  local copies, waits for them, and re-layouts: 4.62 us -> 2.81 us
    ppermute x14 -> x12, waiting for transfers between devices: 1.94 us -> 37.3 us  [the longest x2 20.8 us: sum_line_of_4(): a0 = [lax.ppermute(units[0, c], 'dp', inward) for c in every]]
    ppermute x14 -> x12, starting transfers between devices: 31.8 us -> 19.9 us  [the longest x2 9.09 us: sum_line_of_4(): a1[c] = lax.ppermute(units[1, c], 'dp', inward)]
    pallas_call x3 -> x1, Pallas kernels: 4.76 us -> 1.61 us  [finish(): pl.pallas_call(functools.partial(finish_kernel, width), in_specs=[VMEM_SP...]
    unnamed x40 -> x20, local copies, waits for them, and re-layouts: 4.62 us -> 2.22 us
  transfers between devices with their start and end apart: 22 -> 20, of which waited for: 4 -> 7; matrix products, arithmetic and copies ran while one was open for 0% -> 1% of each run, Pallas kernels for 47% -> 31%
where the time goes in v1:
time: 147 us; the launch traced here: 146 us
  Pallas kernels  68.5 us (47%)
  waiting for transfers between devices  39.2 us (27%)
  starting transfers between devices  29.4 us (20%)
  between operations  4.68 us (3%)
  local copies, waits for them, and re-layouts  2.81 us (2%)
  other arithmetic  1.7 us (1%)
    pallas_call x10, Pallas kernels, hist(): pl.pallas_call(functools.partial(hist_kernel, first_column, width, levels...  52.3 us
    ppermute x2, waiting for transfers between devices, sum_line_of_4(): a0 = [lax.ppermute(units[0, c], 'dp', inward) for c in every]  20.8 us
    ppermute x2, waiting for transfers between devices, sum_line_of_4(): a1[c] = lax.ppermute(units[1, c], 'dp', inward)  9.93 us
    ppermute x2, starting transfers between devices, sum_line_of_4(): a1[c] = lax.ppermute(units[1, c], 'dp', inward)  9.09 us
    ppermute x6, starting transfers between devices, per_device(): lax.ppermute(gain, 'dp', [(i, (i + s) % line) for i in range(line)])  8.88 us
    pallas_call x1, Pallas kernels, prep(): pl.pallas_call(functools.partial(prep_kernel, line, slab), in_specs=[SMEM...  8.04 us
    ppermute x2, waiting for transfers between devices, sum_line_of_4(): a2[c] = lax.ppermute(units[2, c] + b1[c], 'dp', outer)  6.03 us
    pallas_call x2, Pallas kernels, gains_of(): pl.pallas_call(functools.partial(gain_kernel, width, levels, kdim), in_sp...  5.33 us
  transfers between devices with their start and end apart: 20, of which 7 were waited for; matrix products, arithmetic and copies ran while one was open for 1% of the time, Pallas kernels for 31%

profile of v1, /device:TPU:0, one launch (start us, length us, event | category | flops | bytes accessed | tf_op | source)
XLA Modules:
  0.0 146.2 jit_solution(12930906283261212563)
XLA Ops:
  0.0 8.0 %prep.1 = (bf16[2048,256]{1,0:T(8,128)(2,1)}, f32[2048,256]{1,0:T(8,128)}, bf16[48,2048]{1,0:T(8,128)(2,1)}, f32[40,2048]{1,0:T(8,128)}) custom-call(s32[8]{0:T(128)} %owner_ref.3, s32[2048,512]{1,0:T(8,128)} %bins_ref.1, bf16[32,2048]{1,0:T(8,128)(2,1)} %bitcast.16, bf16[2048]{0:T(1024)(128)(2,1)} %hess_ref.1, s32[1,2048]{1,0:T(1,128)} %bitcast.17), custom_call_target="tpu_custom_call" | custom-call | flops 2147483648 | bytes 8388608 | tf_op jit(solution)/shard_map/prep/pallas_call | solution.py:119
  10.8 4.1 %hist.13.refs_2_ = f32[528,256]{1,0:T(8,128)S(1)} custom-call(bf16[2048,256]{1,0:T(8,128)(2,1)S(1)} %copy-done.7, bf16[48,2048]{1,0:T(8,128)(2,1)S(1)} %copy-done.9), custom_call_target="tpu_custom_call" | custom-call | flops 2147483648 | bytes 2097152 | tf_op jit(solution)/shard_map/hist/pallas_call | solution.py:247
  14.9 4.1 %hist.10.refs_2_ = f32[528,256]{1,0:T(8,128)S(1)} custom-call(bf16[2048,256]{1,0:T(8,128)(2,1)S(1)} %copy-done.7, bf16[48,2048]{1,0:T(8,128)(2,1)S(1)} %copy-done.9), custom_call_target="tpu_custom_call" | custom-call | flops 2147483648 | bytes 2097152 | tf_op jit(solution)/shard_map/hist/pallas_call | solution.py:247
  19.1 4.1 %hist.11.refs_3_ = f32[528,256]{1,0:T(8,128)S(1)} custom-call(f32[2048,256]{1,0:T(8,128)S(1)} %collective-permute-done.refs_0_.refs_2_, f32[40,2048]{1,0:T(8,128)S(1)} %collective-permute-done.1.refs_1_.refs_3_, f32[528,256]{1,0:T(8,128)S(1)} %hist.10.refs_2_), custom_call_target="tpu_custom_call" | custom-call | flops 2147483648 | bytes 2097152 | tf_op jit(solution)/shard_map/hist/pallas_call | solution.py:247
  23.2 4.1 %hist.14.refs_4_ = f32[528,256]{1,0:T(8,128)S(1)} custom-call(f32[2048,256]{1,0:T(8,128)S(1)} %collective-permute-done.refs_0_.refs_2_, f32[40,2048]{1,0:T(8,128)S(1)} %collective-permute-done.1.refs_1_.refs_3_, f32[528,256]{1,0:T(8,128)S(1)} %hist.13.refs_2_, f32[528,256]{1,0:T(8,128)S(1)} %hist.11.refs_3_), custom_call_target="tpu_custom_call" | custom-call | flops 2147483648 | bytes 2097152 | tf_op jit(solution)/shard_map/hist/pallas_call | solution.py:247
  27.4 6.0 %hist.16 = f32[528,256]{1,0:T(8,128)S(1)} custom-call(bf16[2048,256]{1,0:T(8,128)(2,1)S(1)} %copy-done.8, bf16[48,2048]{1,0:T(8,128)(2,1)S(1)} %copy-done.9, f32[2048,256]{1,0:T(8,128)S(1)} %collective-permute-done.refs_0_.refs_2_, f32[40,2048]{1,0:T(8,128)S(1)} %collective-permute-done.1.refs_1_.refs_3_, f32[528,256]{1,0:T(8,128)S(1)} %hist.14.refs_4_), custom_call_target="tpu_custom_call" | custom-call | flops 4294967296 | bytes 4194304 | tf_op jit(solution)/shard_map/hist/pallas_call | solution.py:247
  33.4 4.6 %collective-permute-start.5 = (f32[528,256]{1,0:T(8,128)S(1)}, f32[528,256]{1,0:T(8,128)S(1)}, u32[]{:S(2)}, u32[]{:S(2)}) collective-permute-start(f32[528,256]{1,0:T(8,128)S(1)} %hist.16), channel_id=1, source_target_pairs={{0,4},{12,8},{1,5},{13,9},{2,6},{14,10},{3,7},{15,11},{16,20},{28,... | collective-permute-start | bytes 1622024 | tf_op jit(solution)/shard_map/ppermute | solution.py:527
  40.7 9.9 %collective-permute-done.5.refs_4_ = f32[528,256]{1,0:T(8,128)S(1)} collective-permute-done((f32[528,256]{1,0:T(8,128)S(1)}, f32[528,256]{1,0:T(8,128)S(1)}, u32[]{:S(2)}, u32[]{:S(2)}) %collective-permute-start.5) | collective-permute-done | bytes 540704 | tf_op jit(solution)/shard_map/ppermute | solution.py:527
  51.4 10.8 %collective-permute-done.4.refs_4_ = f32[528,256]{1,0:T(8,128)S(1)} collective-permute-done((f32[528,256]{1,0:T(8,128)S(1)}, f32[528,256]{1,0:T(8,128)S(1)}, u32[]{:S(2)}, u32[]{:S(2)}) %collective-permute-start.4) | collective-permute-done | bytes 540704 | tf_op jit(solution)/shard_map/ppermute | solution.py:523
  63.0 10.0 %collective-permute-done.2.refs_4_ = f32[528,256]{1,0:T(8,128)S(1)} collective-permute-done((f32[528,256]{1,0:T(8,128)S(1)}, f32[528,256]{1,0:T(8,128)S(1)}, u32[]{:S(2)}, u32[]{:S(2)}) %collective-permute-start.2) | collective-permute-done | bytes 540704 | tf_op jit(solution)/shard_map/ppermute | solution.py:523
  72.9 6.0 %hist.12 = f32[528,256]{1,0:T(8,128)S(1)} custom-call(bf16[2048,256]{1,0:T(8,128)(2,1)S(1)} %copy-done.8, bf16[48,2048]{1,0:T(8,128)(2,1)S(1)} %copy-done.9, f32[2048,256]{1,0:T(8,128)S(1)} %collective-permute-done.refs_0_.refs_2_, f32[40,2048]{1,0:T(8,128)S(1)} %collective-permute-done.1.refs_1_.refs_3_, f32[528,256]{1,0:T(8,128)S(1)} %collective-permute-done.2.refs_4_), custom_call_target="tpu_custom_call" | custom-call | flops 4294967296 | bytes 4194304 | tf_op jit(solution)/shard_map/hist/pallas_call | solution.py:247
  78.9 4.4 %collective-permute-start.3 = (f32[528,256]{1,0:T(8,128)S(1)}, f32[528,256]{1,0:T(8,128)S(1)}, u32[]{:S(2)}, u32[]{:S(2)}) collective-permute-start(f32[528,256]{1,0:T(8,128)S(1)} %hist.12), channel_id=1, source_target_pairs={{0,4},{12,8},{1,5},{13,9},{2,6},{14,10},{3,7},{15,11},{16,20},{28,... | collective-permute-start | bytes 1622024 | tf_op jit(solution)/shard_map/ppermute | solution.py:527
  84.1 6.0 %hist.19 = f32[528,256]{1,0:T(8,128)S(1)} custom-call(bf16[2048,256]{1,0:T(8,128)(2,1)S(1)} %copy-done.8, bf16[48,2048]{1,0:T(8,128)(2,1)S(1)} %copy-done.9, f32[2048,256]{1,0:T(8,128)S(1)} %collective-permute-done.refs_0_.refs_2_, f32[40,2048]{1,0:T(8,128)S(1)} %collective-permute-done.1.refs_1_.refs_3_, f32[528,256]{1,0:T(8,128)S(1)} %collective-permute-done.5.refs_4_), custom_call_target="tpu_custom_call" | custom-call | flops 4294967296 | bytes 4194304 | tf_op jit(solution)/shard_map/hist/pallas_call | solution.py:247
  90.1 6.0 %hist.17 = f32[528,256]{1,0:T(8,128)S(1)} custom-call(bf16[2048,256]{1,0:T(8,128)(2,1)S(1)} %copy-done.8, bf16[48,2048]{1,0:T(8,128)(2,1)S(1)} %copy-done.9, f32[2048,256]{1,0:T(8,128)S(1)} %collective-permute-done.refs_0_.refs_2_, f32[40,2048]{1,0:T(8,128)S(1)} %collective-permute-done.1.refs_1_.refs_3_, f32[528,256]{1,0:T(8,128)S(1)} %collective-permute-done.5.refs_4_), custom_call_target="tpu_custom_call" | custom-call | flops 4294967296 | bytes 4194304 | tf_op jit(solution)/shard_map/hist/pallas_call | solution.py:247
  96.2 2.5 %collective-permute-start.14 = (f32[528,256]{1,0:T(8,128)S(1)}, f32[528,256]{1,0:T(8,128)S(1)}, u32[]{:S(2)}, u32[]{:S(2)}) collective-permute-start(f32[528,256]{1,0:T(8,128)S(1)} %add.22), channel_id=1, source_target_pairs={{0,4},{4,0},{8,12},{12,8},{1,5},{5,1},{9,13},{13,9},{2,6},{6,2},{1... | collective-permute-start | bytes 1622024 | tf_op jit(solution)/shard_map/ppermute | solution.py:534
  99.6 2.7 %collective-permute-start.7 = (f32[528,256]{1,0:T(8,128)S(1)}, f32[528,256]{1,0:T(8,128)S(1)}, u32[]{:S(2)}, u32[]{:S(2)}) collective-permute-start(f32[528,256]{1,0:T(8,128)S(1)} %add.19), channel_id=1, source_target_pairs={{0,4},{4,0},{8,12},{12,8},{1,5},{5,1},{9,13},{13,9},{2,6},{6,2},{1... | collective-permute-start | bytes 1622024 | tf_op jit(solution)/shard_map/ppermute | solution.py:534
  102.4 6.0 %hist.15.last_ref = f32[528,256]{1,0:T(8,128)S(1)} custom-call(bf16[2048,256]{1,0:T(8,128)(2,1)S(1)} %copy-done.8, bf16[48,2048]{1,0:T(8,128)(2,1)S(1)} %copy-done.9, f32[2048,256]{1,0:T(8,128)S(1)} %collective-permute-done.refs_0_.refs_2_, f32[40,2048]{1,0:T(8,128)S(1)} %collective-permute-done.1.refs_1_.refs_3_, f32[528,256]{1,0:T(8,128)S(1)} %collective-permute-done.4.refs_4_), custom_call_target="tpu_custom_call" | custom-call | flops 4294967296 | bytes 4194304 | tf_op jit(solution)/shard_map/hist/pallas_call | solution.py:247
  109.6 6.0 %hist.18.last_ref = f32[528,256]{1,0:T(8,128)S(1)} custom-call(bf16[2048,256]{1,0:T(8,128)(2,1)S(1)} %copy-done.8, bf16[48,2048]{1,0:T(8,128)(2,1)S(1)} %copy-done.9, f32[2048,256]{1,0:T(8,128)S(1)} %collective-permute-done.refs_0_.refs_2_, f32[40,2048]{1,0:T(8,128)S(1)} %collective-permute-done.1.refs_1_.refs_3_, ...), custom_call_target="tpu_custom_call" | custom-call | flops 4294967296 | bytes 4194304 | tf_op jit(solution)/shard_map/hist/pallas_call | solution.py:247
  115.6 6.0 %collective-permute-done.7.right_ref = f32[528,256]{1,0:T(8,128)S(1)} collective-permute-done((f32[528,256]{1,0:T(8,128)S(1)}, f32[528,256]{1,0:T(8,128)S(1)}, u32[]{:S(2)}, u32[]{:S(2)}) %collective-permute-start.7) | collective-permute-done | bytes 540704 | tf_op jit(solution)/shard_map/ppermute | solution.py:534
  121.7 2.7 %gains.2 = f32[2,16,256]{2,1,0:T(8,128)S(1)} custom-call(f32[528,256]{1,0:T(8,128)S(1)} %hist.15.last_ref, f32[528,256]{1,0:T(8,128)S(1)} %collective-permute-done.7.right_ref, f32[528,256]{1,0:T(8,128)S(1)} %collective-permute-done.8.left_ref, f32[512,256]{1,0:T(8,128)S(1)} %get-tuple-element.21.par_grad_ref, f32[16,256]{1,0:T(8,128)S(1)} %get-tuple-element.22.par_hess_ref, ...), custom_call_target="tpu_custom_call" | custom-call | flops 6553600 | bytes 2097152 | tf_op jit(solution)/shard_map/gains/pallas_call | solution.py:418
  124.4 1.8 %collective-permute-start.11 = (f32[2,16,256]{2,1,0:T(8,128)S(1)}, f32[2,16,256]{2,1,0:T(8,128)S(1)}, u32[]{:S(2)}, u32[]{:S(2)}) collective-permute-start(f32[2,16,256]{2,1,0:T(8,128)S(1)} %gains.2), channel_id=1, source_target_pairs={{0,4},{4,8},{8,12},{12,0},{1,5},{5,9},{9,13},{13,1},{2,6},{6,10},{... | collective-permute-start | bytes 98312 | tf_op jit(solution)/shard_map/ppermute | solution.py:580
  133.7 2.7 %gains.3 = f32[2,16,256]{2,1,0:T(8,128)S(1)} custom-call(f32[528,256]{1,0:T(8,128)S(1)} %hist.18.last_ref, f32[528,256]{1,0:T(8,128)S(1)} %collective-permute-done.14.right_ref, f32[528,256]{1,0:T(8,128)S(1)} %collective-permute-done.15.left_ref, f32[512,256]{1,0:T(8,128)S(1)} %get-tuple-element.24.par_grad_ref, ...), custom_call_target="tpu_custom_call" | custom-call | flops 6553600 | bytes 2097152 | tf_op jit(solution)/shard_map/gains/pallas_call | solution.py:418
  136.7 2.0 %collective-permute-start.17 = (f32[2,16,256]{2,1,0:T(8,128)S(1)}, f32[2,16,256]{2,1,0:T(8,128)S(1)}, u32[]{:S(2)}, u32[]{:S(2)}) collective-permute-start(f32[2,16,256]{2,1,0:T(8,128)S(1)} %gains.3), channel_id=1, source_target_pairs={{0,8},{4,12},{8,0},{12,4},{1,9},{5,13},{9,1},{13,5},{2,10},{6,14},... | collective-permute-start | bytes 98312 | tf_op jit(solution)/shard_map/ppermute | solution.py:580
  138.7 2.1 %collective-permute-start.16 = (f32[2,16,256]{2,1,0:T(8,128)S(1)}, f32[2,16,256]{2,1,0:T(8,128)S(1)}, u32[]{:S(2)}, u32[]{:S(2)}) collective-permute-start(f32[2,16,256]{2,1,0:T(8,128)S(1)} %gains.3), channel_id=1, source_target_pairs={{0,12},{4,0},{8,4},{12,8},{1,13},{5,1},{9,5},{13,9},{2,14},{6,2},{... | collective-permute-start | bytes 98312 | tf_op jit(solution)/shard_map/ppermute | solution.py:580
  (62 shorter events, 18.9 us)
Async XLA Ops:
  8.1 11.1 %collective-permute-start = (f32[2048,256]{1,0:T(8,128)}, f32[2048,256]{1,0:T(8,128)S(1)}, u32[]{:S(2)}, u32[]{:S(2)}) collective-permute-start(f32[2048,256]{1,0:T(8,128)} %get-tuple-element.18), channel_id=1, source_target_pairs={{0,1},{1,0},{2,3},{3,2},{4,5},{5,4},{6,7},{7,6},{8,9},{9,8},{10,11... | collective-permute-start | bytes 6291464 | tf_op jit(solution)/shard_map/ppermute | solution.py:554
  8.6 10.5 %collective-permute-start.1 = (f32[40,2048]{1,0:T(8,128)}, f32[40,2048]{1,0:T(8,128)S(1)}, u32[]{:S(2)}, u32[]{:S(2)}) collective-permute-start(f32[40,2048]{1,0:T(8,128)} %get-tuple-element.19), channel_id=1, source_target_pairs={{0,1},{1,0},{2,3},{3,2},{4,5},{5,4},{6,7},{7,6},{8,9},{9,8},{10,11... | collective-permute-start | bytes 983048 | tf_op jit(solution)/shard_map/ppermute | solution.py:553
  33.4 17.3 %collective-permute-start.5 = (f32[528,256]{1,0:T(8,128)S(1)}, f32[528,256]{1,0:T(8,128)S(1)}, u32[]{:S(2)}, u32[]{:S(2)}) collective-permute-start(f32[528,256]{1,0:T(8,128)S(1)} %hist.16), channel_id=1, source_target_pairs={{0,4},{12,8},{1,5},{13,9},{2,6},{14,10},{3,7},{15,11},{16,20},{28,... | collective-permute-start | bytes 1622024 | tf_op jit(solution)/shard_map/ppermute | solution.py:527
  38.0 24.2 %collective-permute-start.4 = (f32[528,256]{1,0:T(8,128)S(1)}, f32[528,256]{1,0:T(8,128)S(1)}, u32[]{:S(2)}, u32[]{:S(2)}) collective-permute-start(f32[528,256]{1,0:T(8,128)S(1)} %hist.14.refs_4_), channel_id=1, source_target_pairs={{0,4},{12,8},{1,5},{13,9},{2,6},{14,10},{3,7},{15,11},{16,20},{28,... | collective-permute-start | bytes 1622024 | tf_op jit(solution)/shard_map/ppermute | solution.py:523
  39.3 33.6 %collective-permute-start.2 = (f32[528,256]{1,0:T(8,128)S(1)}, f32[528,256]{1,0:T(8,128)S(1)}, u32[]{:S(2)}, u32[]{:S(2)}) collective-permute-start(f32[528,256]{1,0:T(8,128)S(1)} %hist.11.refs_3_), channel_id=1, source_target_pairs={{0,4},{12,8},{1,5},{13,9},{2,6},{14,10},{3,7},{15,11},{16,20},{28,... | collective-permute-start | bytes 1622024 | tf_op jit(solution)/shard_map/ppermute | solution.py:523
  50.7 65.0 %collective-permute-start.8 = (f32[528,256]{1,0:T(8,128)S(1)}, f32[528,256]{1,0:T(8,128)S(1)}, u32[]{:S(2)}, u32[]{:S(2)}) collective-permute-start(f32[528,256]{1,0:T(8,128)S(1)} %add.20), channel_id=1, source_target_pairs={{4,8},{8,4},{5,9},{9,5},{6,10},{10,6},{7,11},{11,7},{20,24},{24,20... | collective-permute-start | bytes 1622024 | tf_op jit(solution)/shard_map/ppermute | solution.py:533
  62.3 33.8 %collective-permute-start.13 = (f32[528,256]{1,0:T(8,128)S(1)}, f32[528,256]{1,0:T(8,128)S(1)}, u32[]{:S(2)}, u32[]{:S(2)}) collective-permute-start(f32[528,256]{1,0:T(8,128)S(1)} %add.21), channel_id=1, source_target_pairs={{4,8},{8,4},{5,9},{9,5},{6,10},{10,6},{7,11},{11,7},{20,24},{24,20... | collective-permute-start | bytes 1622024 | tf_op jit(solution)/shard_map/ppermute | solution.py:528
  78.9 19.8 %collective-permute-start.3 = (f32[528,256]{1,0:T(8,128)S(1)}, f32[528,256]{1,0:T(8,128)S(1)}, u32[]{:S(2)}, u32[]{:S(2)}) collective-permute-start(f32[528,256]{1,0:T(8,128)S(1)} %hist.12), channel_id=1, source_target_pairs={{0,4},{12,8},{1,5},{13,9},{2,6},{14,10},{3,7},{15,11},{16,20},{28,... | collective-permute-start | bytes 1622024 | tf_op jit(solution)/shard_map/ppermute | solution.py:527
  83.4 16.1 %collective-permute-start.6 = (f32[528,256]{1,0:T(8,128)S(1)}, f32[528,256]{1,0:T(8,128)S(1)}, u32[]{:S(2)}, u32[]{:S(2)}) collective-permute-start(f32[528,256]{1,0:T(8,128)S(1)} %add.18), channel_id=1, source_target_pairs={{4,8},{8,4},{5,9},{9,5},{6,10},{10,6},{7,11},{11,7},{20,24},{24,20... | collective-permute-start | bytes 1622024 | tf_op jit(solution)/shard_map/ppermute | solution.py:528
  96.2 37.5 %collective-permute-start.14 = (f32[528,256]{1,0:T(8,128)S(1)}, f32[528,256]{1,0:T(8,128)S(1)}, u32[]{:S(2)}, u32[]{:S(2)}) collective-permute-start(f32[528,256]{1,0:T(8,128)S(1)} %add.22), channel_id=1, source_target_pairs={{0,4},{4,0},{8,12},{12,8},{1,5},{5,1},{9,13},{13,9},{2,6},{6,2},{1... | collective-permute-start | bytes 1622024 | tf_op jit(solution)/shard_map/ppermute | solution.py:534
  98.8 34.9 %collective-permute-start.15 = (f32[528,256]{1,0:T(8,128)S(1)}, f32[528,256]{1,0:T(8,128)S(1)}, u32[]{:S(2)}, u32[]{:S(2)}) collective-permute-start(f32[528,256]{1,0:T(8,128)S(1)} %add.23), channel_id=1, source_target_pairs={{4,8},{8,4},{5,9},{9,5},{6,10},{10,6},{7,11},{11,7},{20,24},{24,20... | collective-permute-start | bytes 1622024 | tf_op jit(solution)/shard_map/ppermute | solution.py:533
  99.6 8.8 %copy-start = (f32[1,64,4096]{2,1,0:T(8,128)S(1)}, f32[1,64,4096]{2,1,0:T(8,128)}, u32[]{:S(2)}) copy-start(f32[1,64,4096]{2,1,0:T(8,128)} %param.18) | copy-start | bytes 3145732
  99.6 8.8 %copy-start.1 = (f32[1,64,128]{2,1,0:T(8,128)S(1)}, f32[1,64,128]{2,1,0:T(8,128)}, u32[]{:S(2)}) copy-start(f32[1,64,128]{2,1,0:T(8,128)} %param.19) | copy-start | bytes 98308
  99.6 22.0 %collective-permute-start.7 = (f32[528,256]{1,0:T(8,128)S(1)}, f32[528,256]{1,0:T(8,128)S(1)}, u32[]{:S(2)}, u32[]{:S(2)}) collective-permute-start(f32[528,256]{1,0:T(8,128)S(1)} %add.19), channel_id=1, source_target_pairs={{0,4},{4,0},{8,12},{12,8},{1,5},{5,1},{9,13},{13,9},{2,6},{6,2},{1... | collective-permute-start | bytes 1622024 | tf_op jit(solution)/shard_map/ppermute | solution.py:534
  109.6 12.1 %copy-start.3 = (s32[2]{0:T(128)S(1)}, s32[2]{0:T(128)}, u32[]{:S(2)}) copy-start(s32[2]{0:T(128)} %low_ref.3) | copy-start | bytes 28
  109.6 12.1 %copy-start.4 = (s32[2]{0:T(128)S(1)}, s32[2]{0:T(128)}, u32[]{:S(2)}) copy-start(s32[2]{0:T(128)} %high_ref.3) | copy-start | bytes 28
  124.4 14.4 %collective-permute-start.11 = (f32[2,16,256]{2,1,0:T(8,128)S(1)}, f32[2,16,256]{2,1,0:T(8,128)S(1)}, u32[]{:S(2)}, u32[]{:S(2)}) collective-permute-start(f32[2,16,256]{2,1,0:T(8,128)S(1)} %gains.2), channel_id=1, source_target_pairs={{0,4},{4,8},{8,12},{12,0},{1,5},{5,9},{9,13},{13,1},{2,6},{6,10},{... | collective-permute-start | bytes 98312 | tf_op jit(solution)/shard_map/ppermute | solution.py:580
  126.1 14.6 %collective-permute-start.10 = (f32[2,16,256]{2,1,0:T(8,128)S(1)}, f32[2,16,256]{2,1,0:T(8,128)S(1)}, u32[]{:S(2)}, u32[]{:S(2)}) collective-permute-start(f32[2,16,256]{2,1,0:T(8,128)S(1)} %gains.2), channel_id=1, source_target_pairs={{0,8},{4,12},{8,0},{12,4},{1,9},{5,13},{9,1},{13,5},{2,10},{6,14},... | collective-permute-start | bytes 98312 | tf_op jit(solution)/shard_map/ppermute | solution.py:580
  127.1 13.7 %collective-permute-start.9 = (f32[2,16,256]{2,1,0:T(8,128)S(1)}, f32[2,16,256]{2,1,0:T(8,128)S(1)}, u32[]{:S(2)}, u32[]{:S(2)}) collective-permute-start(f32[2,16,256]{2,1,0:T(8,128)S(1)} %gains.2), channel_id=1, source_target_pairs={{0,12},{4,0},{8,4},{12,8},{1,13},{5,1},{9,5},{13,9},{2,14},{6,2},{... | collective-permute-start | bytes 98312 | tf_op jit(solution)/shard_map/ppermute | solution.py:580
  136.4 5.8 %collective-permute-start.18 = (f32[2,16,256]{2,1,0:T(8,128)S(1)}, f32[2,16,256]{2,1,0:T(8,128)S(1)}, u32[]{:S(2)}, u32[]{:S(2)}) collective-permute-start(f32[2,16,256]{2,1,0:T(8,128)S(1)} %gains.3), channel_id=1, source_target_pairs={{0,4},{4,8},{8,12},{12,0},{1,5},{5,9},{9,13},{13,1},{2,6},{6,10},{... | collective-permute-start | bytes 98312 | tf_op jit(solution)/shard_map/ppermute | solution.py:580
  136.7 5.4 %collective-permute-start.17 = (f32[2,16,256]{2,1,0:T(8,128)S(1)}, f32[2,16,256]{2,1,0:T(8,128)S(1)}, u32[]{:S(2)}, u32[]{:S(2)}) collective-permute-start(f32[2,16,256]{2,1,0:T(8,128)S(1)} %gains.3), channel_id=1, source_target_pairs={{0,8},{4,12},{8,0},{12,4},{1,9},{5,13},{9,1},{13,5},{2,10},{6,14},... | collective-permute-start | bytes 98312 | tf_op jit(solution)/shard_map/ppermute | solution.py:580
  138.7 4.0 %collective-permute-start.16 = (f32[2,16,256]{2,1,0:T(8,128)S(1)}, f32[2,16,256]{2,1,0:T(8,128)S(1)}, u32[]{:S(2)}, u32[]{:S(2)}) collective-permute-start(f32[2,16,256]{2,1,0:T(8,128)S(1)} %gains.3), channel_id=1, source_target_pairs={{0,12},{4,0},{8,4},{12,8},{1,13},{5,1},{9,5},{13,9},{2,14},{6,2},{... | collective-permute-start | bytes 98312 | tf_op jit(solution)/shard_map/ppermute | solution.py:580
  140.8 2.0 %collective-permute-start.12 = (f32[2,16,256]{2,1,0:T(8,128)S(1)}, f32[2,16,256]{2,1,0:T(8,128)S(1)}, u32[]{:S(2)}, u32[]{:S(2)}) collective-permute-start(f32[2,16,256]{2,1,0:T(8,128)S(1)} %select_select_fusion.2), channel_id=1, source_target_pairs={{0,1},{1,0},{2,3},{3,2},{4,5},{5,4},{6,7},{7,6},{8,9},{9,8},{10,11... | collective-permute-start | bytes 98312 | tf_op jit(solution)/shard_map/ppermute | solution.py:581
  142.7 1.3 collective-permute-start.19
  (6 other events, 32.6 us)

commit v2 on v1

--- a/solution.py
+++ b/solution.py
@@ -255,7 +255,7 @@
         ],
         compiler_params=pltpu.CompilerParams(vmem_limit_bytes=20 * MIB),
         cost_estimate=pl.CostEstimate(
-            flops=2 * 128 * parts * rows * levels * lanes, bytes_accessed=parts * rows * lanes * 4, transcendentals=0
+            flops=parts * rows * lanes, bytes_accessed=parts * rows * lanes, transcendentals=0
         ),
         name="hist",
     )(*operands, *tie)
@@ -519,23 +519,19 @@
 
 def sum_line_of_4(line, chunks, units, unit, set_up):
     inward, outer, middle = [(0, 1), (3, 2)], [(0, 1), (1, 0), (2, 3), (3, 2)], [(1, 2), (2, 1)]
-    every = range(chunks)
-    a0 = [lax.ppermute(units[0, c], "dp", inward) for c in every]
-    a1, b1, a2, b2 = [None] * chunks, [None] * chunks, [None] * chunks, [None] * chunks
-    for c in every:
-        units[1, c] = unit(1, c, (a0[c - 1],) if c else (units[0, chunks - 1],))
+    a0, a1, a2, b1, b2, last = {}, {}, {}, {}, {}, {}
+    for c in range(chunks):
+        a0[c] = lax.ppermute(units[0, c], "dp", inward)
+    for c in range(chunks):
+        units[1, c] = unit(1, c, (a0[c], units[1, c - 1] if c else units[0, chunks - 1]))
+        b1[c] = lax.ppermute(units[0, c] + a0[c], "dp", middle)
         a1[c] = lax.ppermute(units[1, c], "dp", inward)
-        b1[c] = lax.ppermute(units[0, c] + a0[c], "dp", middle)
-    last = [None] * chunks
-    last[0] = unit(3, 0, (a0[chunks - 1],))
-    for c in every:
-        units[2, c] = unit(2, c, (a1[0],))
+    for c in range(chunks):
+        units[2, c] = unit(2, c, (a1[c], last[c - 1] if c else units[1, chunks - 1]))
         b2[c] = lax.ppermute(units[1, c] + a1[c], "dp", middle)
         a2[c] = lax.ppermute(units[2, c] + b1[c], "dp", outer)
-    layout = set_up(a1[chunks - 1])
-    for c in range(1, chunks):
-        last[c] = unit(3, c, (a1[chunks - 1],))
-    return last, a2, b2, layout
+        last[c] = unit(3, c, (units[2, c],))
+    return last, a2, b2, set_up(units[2, chunks - 1])
 
 
 def per_device(bins, grads, hess, node_side, signs, child_owner, parent_owner, parent_grad, parent_hess, node_low, node_high):
@@ -564,10 +560,9 @@
         )
 
     units = {}
-    for c in range(chunks):
-        units[0, c] = unit(0, c, [mine])
-    for c in range(chunks):
-        units[0, c] = unit(0, c, [theirs], units[0, c], (units[0, c - 1],) if c else ())
+    units[0, 0] = unit(0, 0, [theirs], unit(0, 0, [mine]))
+    for c in range(1, chunks):
+        units[0, c] = unit(0, c, [mine, theirs], tie=(units[0, c - 1],))
     collect = sum_line_of_4 if line == 4 else sum_line
     last, from_left, from_right, layout = collect(line, chunks, units, lambda p, c, tie: unit(p, c, [mine, theirs], tie=tie), set_up)
     par_grad, par_hess, sign, route = layout

time: 147 us -> 122 us (0.83)
  waiting for transfers between devices: 39.2 us -> 10.4 us
  starting transfers between devices: 29.4 us -> 35.4 us
  Pallas kernels: 68.5 us -> 65.8 us
    ppermute x2, waiting for transfers between devices: 20.8 us -> 5.69 us  [sum_line_of_4(): a0[c] = lax.ppermute(units[0, c], 'dp', inward)]
    ppermute x2, waiting for transfers between devices: 9.93 us -> 2.59 us  [sum_line_of_4(): a1[c] = lax.ppermute(units[1, c], 'dp', inward)]
    ppermute x2, waiting for transfers between devices: 6.03 us -> 0.01 us  [sum_line_of_4(): a2[c] = lax.ppermute(units[2, c] + b1[c], 'dp', outer)]
    ppermute x2, starting transfers between devices: 2.65 us -> 6.59 us  [sum_line_of_4(): a0[c] = lax.ppermute(units[0, c], 'dp', inward)]
    pallas_call x10 -> x9, Pallas kernels: 52.3 us -> 50 us  [hist(): pl.pallas_call(functools.partial(hist_kernel, first_column, width, levels...]
    ppermute x2, starting transfers between devices: 5.23 us -> 7.57 us  [sum_line_of_4(): a2[c] = lax.ppermute(units[2, c] + b1[c], 'dp', outer)]
  transfers between devices with their start and end apart: 20 -> 20, of which waited for: 7 -> 7; matrix products, arithmetic and copies ran while one was open for 1% -> 1% of each run, Pallas kernels for 31% -> 43%
where the time goes in v2:
time: 122 us; the launch traced here: 121 us
  Pallas kernels  65.8 us (54%)
  starting transfers between devices  35.4 us (29%)
  waiting for transfers between devices  10.4 us (9%)
  between operations  5 us (4%)
  local copies, waits for them, and re-layouts  2.82 us (2%)
  other arithmetic  1.68 us (1%)
    pallas_call x9, Pallas kernels, hist(): pl.pallas_call(functools.partial(hist_kernel, first_column, width, levels...  50 us
    ppermute x6, starting transfers between devices, per_device(): lax.ppermute(gain, 'dp', [(i, (i + s) % line) for i in range(line)])  8.88 us
    ppermute x2, starting transfers between devices, sum_line_of_4(): a1[c] = lax.ppermute(units[1, c], 'dp', inward)  8.87 us
    pallas_call x1, Pallas kernels, prep(): pl.pallas_call(functools.partial(prep_kernel, line, slab), in_specs=[SMEM...  7.73 us
    ppermute x2, starting transfers between devices, sum_line_of_4(): a2[c] = lax.ppermute(units[2, c] + b1[c], 'dp', outer)  7.57 us
    ppermute x2, starting transfers between devices, sum_line_of_4(): a0[c] = lax.ppermute(units[0, c], 'dp', inward)  6.59 us
    ppermute x2, waiting for transfers between devices, sum_line_of_4(): a0[c] = lax.ppermute(units[0, c], 'dp', inward)  5.69 us
    pallas_call x2, Pallas kernels, gains_of(): pl.pallas_call(functools.partial(gain_kernel, width, levels, kdim), in_sp...  5.33 us
  transfers between devices with their start and end apart: 20, of which 7 were waited for; matrix products, arithmetic and copies ran while one was open for 1% of the time, Pallas kernels for 43%

profile of v2, /device:TPU:0, one launch (start us, length us, event | category | flops | bytes accessed | tf_op | source)
XLA Modules:
  0.0 121.2 jit_solution(18238535190764396666)
XLA Ops:
  0.0 7.7 %prep.1 = (bf16[2048,256]{1,0:T(8,128)(2,1)}, f32[2048,256]{1,0:T(8,128)}, bf16[48,2048]{1,0:T(8,128)(2,1)}, f32[40,2048]{1,0:T(8,128)}) custom-call(s32[8]{0:T(128)} %owner_ref.3, s32[2048,512]{1,0:T(8,128)} %bins_ref.1, bf16[32,2048]{1,0:T(8,128)(2,1)} %bitcast.16, bf16[2048]{0:T(1024)(128)(2,1)} %hess_ref.1, s32[1,2048]{1,0:T(1,128)} %bitcast.17), custom_call_target="tpu_custom_call" | custom-call | flops 2147483648 | bytes 8388608 | tf_op jit(solution)/shard_map/prep/pallas_call | solution.py:119
  10.5 4.1 %hist.9.refs_2_ = f32[528,256]{1,0:T(8,128)S(1)} custom-call(bf16[2048,256]{1,0:T(8,128)(2,1)S(1)} %copy-done, bf16[48,2048]{1,0:T(8,128)(2,1)S(1)} %copy-done.2), custom_call_target="tpu_custom_call" | custom-call | flops 524288 | bytes 524288 | tf_op jit(solution)/shard_map/hist/pallas_call | solution.py:247
  14.7 4.1 %hist.10.refs_4_ = f32[528,256]{1,0:T(8,128)S(1)} custom-call(f32[2048,256]{1,0:T(8,128)S(1)} %collective-permute-done.refs_0_.refs_2_, f32[40,2048]{1,0:T(8,128)S(1)} %collective-permute-done.1.refs_1_.refs_3_, f32[528,256]{1,0:T(8,128)S(1)} %hist.9.refs_2_), custom_call_target="tpu_custom_call" | custom-call | flops 524288 | bytes 524288 | tf_op jit(solution)/shard_map/hist/pallas_call | solution.py:247
  18.8 5.2 %collective-permute-start.3 = (f32[528,256]{1,0:T(8,128)S(1)}, f32[528,256]{1,0:T(8,128)S(1)}, u32[]{:S(2)}, u32[]{:S(2)}) collective-permute-start(f32[528,256]{1,0:T(8,128)S(1)} %hist.10.refs_4_), channel_id=1, source_target_pairs={{0,4},{12,8},{1,5},{13,9},{2,6},{14,10},{3,7},{15,11},{16,20},{28,... | collective-permute-start | bytes 1622024 | tf_op jit(solution)/shard_map/ppermute | solution.py:524
  24.1 6.0 %hist.11.refs_5_ = f32[528,256]{1,0:T(8,128)S(1)} custom-call(bf16[2048,256]{1,0:T(8,128)(2,1)S(1)} %copy-done.1, bf16[48,2048]{1,0:T(8,128)(2,1)S(1)} %copy-done.2, f32[2048,256]{1,0:T(8,128)S(1)} %collective-permute-done.refs_0_.refs_2_, f32[40,2048]{1,0:T(8,128)S(1)} %collective-permute-done.1.refs_1_.refs_3_, f32[528,256]{1,0:T(8,128)S(1)} %hist.10.refs_4_), custom_call_target="tpu_custom_call" | custom-call | flops 1048576 | bytes 1048576 | tf_op jit(solution)/shard_map/hist/pallas_call | solution.py:247
  30.0 1.3 %collective-permute-start.2 = (f32[528,256]{1,0:T(8,128)S(1)}, f32[528,256]{1,0:T(8,128)S(1)}, u32[]{:S(2)}, u32[]{:S(2)}) collective-permute-start(f32[528,256]{1,0:T(8,128)S(1)} %hist.11.refs_5_), channel_id=1, source_target_pairs={{0,4},{12,8},{1,5},{13,9},{2,6},{14,10},{3,7},{15,11},{16,20},{28,... | collective-permute-start | bytes 1622024 | tf_op jit(solution)/shard_map/ppermute | solution.py:524
  31.4 5.3 %collective-permute-done.3.refs_4_ = f32[528,256]{1,0:T(8,128)S(1)} collective-permute-done((f32[528,256]{1,0:T(8,128)S(1)}, f32[528,256]{1,0:T(8,128)S(1)}, u32[]{:S(2)}, u32[]{:S(2)}) %collective-permute-start.3) | collective-permute-done | bytes 540704 | tf_op jit(solution)/shard_map/ppermute | solution.py:524
  36.6 5.9 %hist.12.refs_5_ = f32[528,256]{1,0:T(8,128)S(1)} custom-call(bf16[2048,256]{1,0:T(8,128)(2,1)S(1)} %copy-done.1, bf16[48,2048]{1,0:T(8,128)(2,1)S(1)} %copy-done.2, f32[2048,256]{1,0:T(8,128)S(1)} %collective-permute-done.refs_0_.refs_2_, f32[40,2048]{1,0:T(8,128)S(1)} %collective-permute-done.1.refs_1_.refs_3_, ...), custom_call_target="tpu_custom_call" | custom-call | flops 1048576 | bytes 1048576 | tf_op jit(solution)/shard_map/hist/pallas_call | solution.py:247
  42.6 4.4 %collective-permute-start.5 = (f32[528,256]{1,0:T(8,128)S(1)}, f32[528,256]{1,0:T(8,128)S(1)}, u32[]{:S(2)}, u32[]{:S(2)}) collective-permute-start(f32[528,256]{1,0:T(8,128)S(1)} %hist.12.refs_5_), channel_id=1, source_target_pairs={{0,4},{12,8},{1,5},{13,9},{2,6},{14,10},{3,7},{15,11},{16,20},{28,... | collective-permute-start | bytes 1622024 | tf_op jit(solution)/shard_map/ppermute | solution.py:528
  48.2 6.0 %hist.13.refs_5_ = f32[528,256]{1,0:T(8,128)S(1)} custom-call(bf16[2048,256]{1,0:T(8,128)(2,1)S(1)} %copy-done.1, bf16[48,2048]{1,0:T(8,128)(2,1)S(1)} %copy-done.2, f32[2048,256]{1,0:T(8,128)S(1)} %collective-permute-done.refs_0_.refs_2_, f32[40,2048]{1,0:T(8,128)S(1)} %collective-permute-done.1.refs_1_.refs_3_, ...), custom_call_target="tpu_custom_call" | custom-call | flops 1048576 | bytes 1048576 | tf_op jit(solution)/shard_map/hist/pallas_call | solution.py:247
  54.2 4.4 %collective-permute-start.4 = (f32[528,256]{1,0:T(8,128)S(1)}, f32[528,256]{1,0:T(8,128)S(1)}, u32[]{:S(2)}, u32[]{:S(2)}) collective-permute-start(f32[528,256]{1,0:T(8,128)S(1)} %hist.13.refs_5_), channel_id=1, source_target_pairs={{0,4},{12,8},{1,5},{13,9},{2,6},{14,10},{3,7},{15,11},{16,20},{28,... | collective-permute-start | bytes 1622024 | tf_op jit(solution)/shard_map/ppermute | solution.py:528
  59.8 6.0 %hist.14.refs_4_ = f32[528,256]{1,0:T(8,128)S(1)} custom-call(bf16[2048,256]{1,0:T(8,128)(2,1)S(1)} %copy-done.1, bf16[48,2048]{1,0:T(8,128)(2,1)S(1)} %copy-done.2, f32[2048,256]{1,0:T(8,128)S(1)} %collective-permute-done.refs_0_.refs_2_, f32[40,2048]{1,0:T(8,128)S(1)} %collective-permute-done.1.refs_1_.refs_3_, ...), custom_call_target="tpu_custom_call" | custom-call | flops 1048576 | bytes 1048576 | tf_op jit(solution)/shard_map/hist/pallas_call | solution.py:247
  65.9 2.6 %collective-permute-start.7 = (f32[528,256]{1,0:T(8,128)S(1)}, f32[528,256]{1,0:T(8,128)S(1)}, u32[]{:S(2)}, u32[]{:S(2)}) collective-permute-start(f32[528,256]{1,0:T(8,128)S(1)} %add.19), channel_id=1, source_target_pairs={{0,4},{4,0},{8,12},{12,8},{1,5},{5,1},{9,13},{13,9},{2,6},{6,2},{1... | collective-permute-start | bytes 1622024 | tf_op jit(solution)/shard_map/ppermute | solution.py:532
  69.2 2.2 %collective-permute-done.4.refs_4_ = f32[528,256]{1,0:T(8,128)S(1)} collective-permute-done((f32[528,256]{1,0:T(8,128)S(1)}, f32[528,256]{1,0:T(8,128)S(1)}, u32[]{:S(2)}, u32[]{:S(2)}) %collective-permute-start.4) | collective-permute-done | bytes 540704 | tf_op jit(solution)/shard_map/ppermute | solution.py:528
  72.2 6.0 %hist.15.refs_5_.last_ref = f32[528,256]{1,0:T(8,128)S(1)} custom-call(bf16[2048,256]{1,0:T(8,128)(2,1)S(1)} %copy-done.1, bf16[48,2048]{1,0:T(8,128)(2,1)S(1)} %copy-done.2, f32[2048,256]{1,0:T(8,128)S(1)} %collective-permute-done.refs_0_.refs_2_, f32[40,2048]{1,0:T(8,128)S(1)} %collective-permute-done.1.refs_1_.refs_3_, f32[528,256]{1,0:T(8,128)S(1)} %hist.14.refs_4_), custom_call_target="tpu_custom_call" | custom-call | flops 1048576 | bytes 1048576 | tf_op jit(solution)/shard_map/hist/pallas_call | solution.py:247
  78.2 6.0 %hist.16.tie_ref.refs_4_ = f32[528,256]{1,0:T(8,128)S(1)} custom-call(bf16[2048,256]{1,0:T(8,128)(2,1)S(1)} %copy-done.1, bf16[48,2048]{1,0:T(8,128)(2,1)S(1)} %copy-done.2, f32[2048,256]{1,0:T(8,128)S(1)} %collective-permute-done.refs_0_.refs_2_, f32[40,2048]{1,0:T(8,128)S(1)} %collective-permute-done.1.refs_1_.refs_3_, ...), custom_call_target="tpu_custom_call" | custom-call | flops 1048576 | bytes 1048576 | tf_op jit(solution)/shard_map/hist/pallas_call | solution.py:247
  84.3 5.0 %collective-permute-start.14 = (f32[528,256]{1,0:T(8,128)S(1)}, f32[528,256]{1,0:T(8,128)S(1)}, u32[]{:S(2)}, u32[]{:S(2)}) collective-permute-start(f32[528,256]{1,0:T(8,128)S(1)} %add.22), channel_id=1, source_target_pairs={{0,4},{4,0},{8,12},{12,8},{1,5},{5,1},{9,13},{13,9},{2,6},{6,2},{1... | collective-permute-start | bytes 1622024 | tf_op jit(solution)/shard_map/ppermute | solution.py:532
  90.6 2.7 %gains.2 = f32[2,16,256]{2,1,0:T(8,128)S(1)} custom-call(f32[528,256]{1,0:T(8,128)S(1)} %hist.15.refs_5_.last_ref, f32[528,256]{1,0:T(8,128)S(1)} %collective-permute-done.7.right_ref, f32[528,256]{1,0:T(8,128)S(1)} %collective-permute-done.8.left_ref, f32[512,256]{1,0:T(8,128)S(1)} %get-tuple-element.21.par_grad_ref, ...), custom_call_target="tpu_custom_call" | custom-call | flops 6553600 | bytes 2097152 | tf_op jit(solution)/shard_map/gains/pallas_call | solution.py:418
  95.6 1.9 %collective-permute-start.9 = (f32[2,16,256]{2,1,0:T(8,128)S(1)}, f32[2,16,256]{2,1,0:T(8,128)S(1)}, u32[]{:S(2)}, u32[]{:S(2)}) collective-permute-start(f32[2,16,256]{2,1,0:T(8,128)S(1)} %gains.2), channel_id=1, source_target_pairs={{0,12},{4,0},{8,4},{12,8},{1,13},{5,1},{9,5},{13,9},{2,14},{6,2},{... | collective-permute-start | bytes 98312 | tf_op jit(solution)/shard_map/ppermute | solution.py:575
  102.7 6.0 %hist.17.last_ref = f32[528,256]{1,0:T(8,128)S(1)} custom-call(bf16[2048,256]{1,0:T(8,128)(2,1)S(1)} %copy-done.1, bf16[48,2048]{1,0:T(8,128)(2,1)S(1)} %copy-done.3, f32[2048,256]{1,0:T(8,128)S(1)} %collective-permute-done.refs_0_.refs_2_, f32[40,2048]{1,0:T(8,128)S(1)} %collective-permute-done.1.refs_1_.refs_3_, f32[528,256]{1,0:T(8,128)S(1)} %hist.16.tie_ref.refs_4_), custom_call_target="tpu_custom_call" | custom-call | flops 1048576 | bytes 1048576 | tf_op jit(solution)/shard_map/hist/pallas_call | solution.py:247
  108.7 2.7 %gains.3 = f32[2,16,256]{2,1,0:T(8,128)S(1)} custom-call(f32[528,256]{1,0:T(8,128)S(1)} %hist.17.last_ref, f32[528,256]{1,0:T(8,128)S(1)} %collective-permute-done.14.right_ref, f32[528,256]{1,0:T(8,128)S(1)} %collective-permute-done.15.left_ref, f32[512,256]{1,0:T(8,128)S(1)} %get-tuple-element.24.par_grad_ref, ...), custom_call_target="tpu_custom_call" | custom-call | flops 6553600 | bytes 2097152 | tf_op jit(solution)/shard_map/gains/pallas_call | solution.py:418
  111.7 1.6 %collective-permute-start.17 = (f32[2,16,256]{2,1,0:T(8,128)S(1)}, f32[2,16,256]{2,1,0:T(8,128)S(1)}, u32[]{:S(2)}, u32[]{:S(2)}) collective-permute-start(f32[2,16,256]{2,1,0:T(8,128)S(1)} %gains.3), channel_id=1, source_target_pairs={{0,8},{4,12},{8,0},{12,4},{1,9},{5,13},{9,1},{13,5},{2,10},{6,14},... | collective-permute-start | bytes 98312 | tf_op jit(solution)/shard_map/ppermute | solution.py:575
  113.2 2.8 %collective-permute-start.16 = (f32[2,16,256]{2,1,0:T(8,128)S(1)}, f32[2,16,256]{2,1,0:T(8,128)S(1)}, u32[]{:S(2)}, u32[]{:S(2)}) collective-permute-start(f32[2,16,256]{2,1,0:T(8,128)S(1)} %gains.3), channel_id=1, source_target_pairs={{0,12},{4,0},{8,4},{12,8},{1,13},{5,1},{9,5},{13,9},{2,14},{6,2},{... | collective-permute-start | bytes 98312 | tf_op jit(solution)/shard_map/ppermute | solution.py:575
  119.6 1.6 %finish.1 = f32[64,2,128]{2,1,0:T(2,128)} custom-call(f32[2,16,256]{2,1,0:T(8,128)} %select_select_fusion.3.refs_0_, f32[2,16,256]{2,1,0:T(8,128)} %select_select_fusion.1.refs_1_), custom_call_target="tpu_custom_call" | custom-call | tf_op jit(solution)/shard_map/finish/pallas_call | solution.py:464
  (63 shorter events, 14.8 us)
Async XLA Ops:
  7.7 6.9 %collective-permute-start = (f32[2048,256]{1,0:T(8,128)}, f32[2048,256]{1,0:T(8,128)S(1)}, u32[]{:S(2)}, u32[]{:S(2)}) collective-permute-start(f32[2048,256]{1,0:T(8,128)} %get-tuple-element.18), channel_id=1, source_target_pairs={{0,1},{1,0},{2,3},{3,2},{4,5},{5,4},{6,7},{7,6},{8,9},{9,8},{10,11... | collective-permute-start | bytes 6291464 | tf_op jit(solution)/shard_map/ppermute | solution.py:550
  8.3 6.4 %collective-permute-start.1 = (f32[40,2048]{1,0:T(8,128)}, f32[40,2048]{1,0:T(8,128)S(1)}, u32[]{:S(2)}, u32[]{:S(2)}) collective-permute-start(f32[40,2048]{1,0:T(8,128)} %get-tuple-element.19), channel_id=1, source_target_pairs={{0,1},{1,0},{2,3},{3,2},{4,5},{5,4},{6,7},{7,6},{8,9},{9,8},{10,11... | collective-permute-start | bytes 983048 | tf_op jit(solution)/shard_map/ppermute | solution.py:549
  18.8 17.9 %collective-permute-start.3 = (f32[528,256]{1,0:T(8,128)S(1)}, f32[528,256]{1,0:T(8,128)S(1)}, u32[]{:S(2)}, u32[]{:S(2)}) collective-permute-start(f32[528,256]{1,0:T(8,128)S(1)} %hist.10.refs_4_), channel_id=1, source_target_pairs={{0,4},{12,8},{1,5},{13,9},{2,6},{14,10},{3,7},{15,11},{16,20},{28,... | collective-permute-start | bytes 1622024 | tf_op jit(solution)/shard_map/ppermute | solution.py:524
  30.0 18.2 %collective-permute-start.2 = (f32[528,256]{1,0:T(8,128)S(1)}, f32[528,256]{1,0:T(8,128)S(1)}, u32[]{:S(2)}, u32[]{:S(2)}) collective-permute-start(f32[528,256]{1,0:T(8,128)S(1)} %hist.11.refs_5_), channel_id=1, source_target_pairs={{0,4},{12,8},{1,5},{13,9},{2,6},{14,10},{3,7},{15,11},{16,20},{28,... | collective-permute-start | bytes 1622024 | tf_op jit(solution)/shard_map/ppermute | solution.py:524
  42.6 17.2 %collective-permute-start.5 = (f32[528,256]{1,0:T(8,128)S(1)}, f32[528,256]{1,0:T(8,128)S(1)}, u32[]{:S(2)}, u32[]{:S(2)}) collective-permute-start(f32[528,256]{1,0:T(8,128)S(1)} %hist.12.refs_5_), channel_id=1, source_target_pairs={{0,4},{12,8},{1,5},{13,9},{2,6},{14,10},{3,7},{15,11},{16,20},{28,... | collective-permute-start | bytes 1622024 | tf_op jit(solution)/shard_map/ppermute | solution.py:528
  47.1 18.7 %collective-permute-start.6 = (f32[528,256]{1,0:T(8,128)S(1)}, f32[528,256]{1,0:T(8,128)S(1)}, u32[]{:S(2)}, u32[]{:S(2)}) collective-permute-start(f32[528,256]{1,0:T(8,128)S(1)} %add.18), channel_id=1, source_target_pairs={{4,8},{8,4},{5,9},{9,5},{6,10},{10,6},{7,11},{11,7},{20,24},{24,20... | collective-permute-start | bytes 1622024 | tf_op jit(solution)/shard_map/ppermute | solution.py:527
  54.2 17.2 %collective-permute-start.4 = (f32[528,256]{1,0:T(8,128)S(1)}, f32[528,256]{1,0:T(8,128)S(1)}, u32[]{:S(2)}, u32[]{:S(2)}) collective-permute-start(f32[528,256]{1,0:T(8,128)S(1)} %hist.13.refs_5_), channel_id=1, source_target_pairs={{0,4},{12,8},{1,5},{13,9},{2,6},{14,10},{3,7},{15,11},{16,20},{28,... | collective-permute-start | bytes 1622024 | tf_op jit(solution)/shard_map/ppermute | solution.py:528
  58.7 25.5 %collective-permute-start.13 = (f32[528,256]{1,0:T(8,128)S(1)}, f32[528,256]{1,0:T(8,128)S(1)}, u32[]{:S(2)}, u32[]{:S(2)}) collective-permute-start(f32[528,256]{1,0:T(8,128)S(1)} %add.21), channel_id=1, source_target_pairs={{4,8},{8,4},{5,9},{9,5},{6,10},{10,6},{7,11},{11,7},{20,24},{24,20... | collective-permute-start | bytes 1622024 | tf_op jit(solution)/shard_map/ppermute | solution.py:527
  65.9 24.7 %collective-permute-start.7 = (f32[528,256]{1,0:T(8,128)S(1)}, f32[528,256]{1,0:T(8,128)S(1)}, u32[]{:S(2)}, u32[]{:S(2)}) collective-permute-start(f32[528,256]{1,0:T(8,128)S(1)} %add.19), channel_id=1, source_target_pairs={{0,4},{4,0},{8,12},{12,8},{1,5},{5,1},{9,13},{13,9},{2,6},{6,2},{1... | collective-permute-start | bytes 1622024 | tf_op jit(solution)/shard_map/ppermute | solution.py:532
  68.5 22.1 %collective-permute-start.8 = (f32[528,256]{1,0:T(8,128)S(1)}, f32[528,256]{1,0:T(8,128)S(1)}, u32[]{:S(2)}, u32[]{:S(2)}) collective-permute-start(f32[528,256]{1,0:T(8,128)S(1)} %add.20), channel_id=1, source_target_pairs={{4,8},{8,4},{5,9},{9,5},{6,10},{10,6},{7,11},{11,7},{20,24},{24,20... | collective-permute-start | bytes 1622024 | tf_op jit(solution)/shard_map/ppermute | solution.py:531
  71.5 37.2 %collective-permute-start.15 = (f32[528,256]{1,0:T(8,128)S(1)}, f32[528,256]{1,0:T(8,128)S(1)}, u32[]{:S(2)}, u32[]{:S(2)}) collective-permute-start(f32[528,256]{1,0:T(8,128)S(1)} %add.23), channel_id=1, source_target_pairs={{4,8},{8,4},{5,9},{9,5},{6,10},{10,6},{7,11},{11,7},{20,24},{24,20... | collective-permute-start | bytes 1622024 | tf_op jit(solution)/shard_map/ppermute | solution.py:531
  78.2 11.2 %copy-start.5 = (f32[1,64,128]{2,1,0:T(8,128)S(1)}, f32[1,64,128]{2,1,0:T(8,128)}, u32[]{:S(2)}) copy-start(f32[1,64,128]{2,1,0:T(8,128)} %param.19) | copy-start | bytes 98308
  78.2 11.2 %copy-start.6 = (s32[1024]{0:T(1024)S(1)}, s32[1024]{0:T(1024)}, u32[]{:S(2)}) copy-start(s32[1024]{0:T(1024)} %param.15) | copy-start | bytes 12292
  78.2 11.2 %copy-start.9 = (s32[8]{0:T(128)S(1)}, s32[8]{0:T(128)}, u32[]{:S(2)}) copy-start(s32[8]{0:T(128)} %owner_ref.3) | copy-start | bytes 100
  84.3 18.3 %copy-start.3 = (bf16[48,2048]{1,0:T(8,128)(2,1)S(1)}, bf16[48,2048]{1,0:T(8,128)(2,1)}, u32[]{:S(2)}) copy-start(bf16[48,2048]{1,0:T(8,128)(2,1)} %get-tuple-element.17.refs_1_) | copy-start | bytes 589828
  84.3 24.4 %collective-permute-start.14 = (f32[528,256]{1,0:T(8,128)S(1)}, f32[528,256]{1,0:T(8,128)S(1)}, u32[]{:S(2)}, u32[]{:S(2)}) collective-permute-start(f32[528,256]{1,0:T(8,128)S(1)} %add.22), channel_id=1, source_target_pairs={{0,4},{4,0},{8,12},{12,8},{1,5},{5,1},{9,13},{13,9},{2,6},{6,2},{1... | collective-permute-start | bytes 1622024 | tf_op jit(solution)/shard_map/ppermute | solution.py:532
  93.3 19.9 %collective-permute-start.11 = (f32[2,16,256]{2,1,0:T(8,128)S(1)}, f32[2,16,256]{2,1,0:T(8,128)S(1)}, u32[]{:S(2)}, u32[]{:S(2)}) collective-permute-start(f32[2,16,256]{2,1,0:T(8,128)S(1)} %gains.2), channel_id=1, source_target_pairs={{0,4},{4,8},{8,12},{12,0},{1,5},{5,9},{9,13},{13,1},{2,6},{6,10},{... | collective-permute-start | bytes 98312 | tf_op jit(solution)/shard_map/ppermute | solution.py:575
  94.4 21.7 %collective-permute-start.10 = (f32[2,16,256]{2,1,0:T(8,128)S(1)}, f32[2,16,256]{2,1,0:T(8,128)S(1)}, u32[]{:S(2)}, u32[]{:S(2)}) collective-permute-start(f32[2,16,256]{2,1,0:T(8,128)S(1)} %gains.2), channel_id=1, source_target_pairs={{0,8},{4,12},{8,0},{12,4},{1,9},{5,13},{9,1},{13,5},{2,10},{6,14},... | collective-permute-start | bytes 98312 | tf_op jit(solution)/shard_map/ppermute | solution.py:575
  95.6 20.5 %collective-permute-start.9 = (f32[2,16,256]{2,1,0:T(8,128)S(1)}, f32[2,16,256]{2,1,0:T(8,128)S(1)}, u32[]{:S(2)}, u32[]{:S(2)}) collective-permute-start(f32[2,16,256]{2,1,0:T(8,128)S(1)} %gains.2), channel_id=1, source_target_pairs={{0,12},{4,0},{8,4},{12,8},{1,13},{5,1},{9,5},{13,9},{2,14},{6,2},{... | collective-permute-start | bytes 98312 | tf_op jit(solution)/shard_map/ppermute | solution.py:575
  111.4 5.8 %collective-permute-start.18 = (f32[2,16,256]{2,1,0:T(8,128)S(1)}, f32[2,16,256]{2,1,0:T(8,128)S(1)}, u32[]{:S(2)}, u32[]{:S(2)}) collective-permute-start(f32[2,16,256]{2,1,0:T(8,128)S(1)} %gains.3), channel_id=1, source_target_pairs={{0,4},{4,8},{8,12},{12,0},{1,5},{5,9},{9,13},{13,1},{2,6},{6,10},{... | collective-permute-start | bytes 98312 | tf_op jit(solution)/shard_map/ppermute | solution.py:575
  111.7 5.5 %collective-permute-start.17 = (f32[2,16,256]{2,1,0:T(8,128)S(1)}, f32[2,16,256]{2,1,0:T(8,128)S(1)}, u32[]{:S(2)}, u32[]{:S(2)}) collective-permute-start(f32[2,16,256]{2,1,0:T(8,128)S(1)} %gains.3), channel_id=1, source_target_pairs={{0,8},{4,12},{8,0},{12,4},{1,9},{5,13},{9,1},{13,5},{2,10},{6,14},... | collective-permute-start | bytes 98312 | tf_op jit(solution)/shard_map/ppermute | solution.py:575
  113.2 4.5 %collective-permute-start.16 = (f32[2,16,256]{2,1,0:T(8,128)S(1)}, f32[2,16,256]{2,1,0:T(8,128)S(1)}, u32[]{:S(2)}, u32[]{:S(2)}) collective-permute-start(f32[2,16,256]{2,1,0:T(8,128)S(1)} %gains.3), channel_id=1, source_target_pairs={{0,12},{4,0},{8,4},{12,8},{1,13},{5,1},{9,5},{13,9},{2,14},{6,2},{... | collective-permute-start | bytes 98312 | tf_op jit(solution)/shard_map/ppermute | solution.py:575
  116.1 1.7 %collective-permute-start.12 = (f32[2,16,256]{2,1,0:T(8,128)S(1)}, f32[2,16,256]{2,1,0:T(8,128)S(1)}, u32[]{:S(2)}, u32[]{:S(2)}) collective-permute-start(f32[2,16,256]{2,1,0:T(8,128)S(1)} %select_select_fusion.2), channel_id=1, source_target_pairs={{0,1},{1,0},{2,3},{3,2},{4,5},{5,4},{6,7},{7,6},{8,9},{9,8},{10,11... | collective-permute-start | bytes 98312 | tf_op jit(solution)/shard_map/ppermute | solution.py:576
  117.7 1.3 %collective-permute-start.19 = (f32[2,16,256]{2,1,0:T(8,128)S(1)}, f32[2,16,256]{2,1,0:T(8,128)S(1)}, u32[]{:S(2)}, u32[]{:S(2)}) collective-permute-start(f32[2,16,256]{2,1,0:T(8,128)S(1)} %select_select_fusion), channel_id=1, source_target_pairs={{0,1},{1,0},{2,3},{3,2},{4,5},{5,4},{6,7},{7,6},{8,9},{9,8},{10,11... | collective-permute-start | bytes 98312 | tf_op jit(solution)/shard_map/ppermute | solution.py:576
  (7 other events, 40.7 us)

commit v3 on v2

--- a/solution.py
+++ b/solution.py
@@ -279,9 +279,9 @@
     return x
 
 
-def layout_kernel(width, levels, kdim, chunks, line, child_ref, owner_ref, sign_ref, parent_ref, hess_ref, tie_ref, *out_refs):
+def layout_kernel(width, levels, kdim, chunks, line, child_ref, owner_ref, low_ref, high_ref, sign_ref, parent_ref, hess_ref, tie_ref, *out_refs):
     del tie_ref
-    grad_refs, hess_refs, sign_refs = out_refs[:chunks], out_refs[chunks : 2 * chunks], out_refs[2 * chunks : 3 * chunks]
+    grad_refs, hess_refs, bound_refs = out_refs[:chunks], out_refs[chunks : 2 * chunks], out_refs[2 * chunks : 3 * chunks]
     lanes = grad_refs[0].shape[1]
     slab = width * chunks
     owners = owner_ref.shape[0]
@@ -289,7 +289,7 @@
     place = 2 * z + core
     mine = source_of(place, child_ref, owner_ref)
     twin = source_of(2 * z + 1 - core, child_ref, owner_ref)
-    row = lax.broadcasted_iota(jnp.int32, (8, 128), 0)
+    row = lax.broadcasted_iota(jnp.int32, (8, lanes), 0)
     route = jnp.where(row == 0, lax.rem(z - mine // 2 + line, line), lax.rem(z - twin // 2 + line, line))
     out_refs[-1][...] = jnp.where(row == 2, jnp.where(lax.rem(mine, 2) == core, 1, 0), route)
     slab_at = jnp.int32(0)
@@ -302,7 +302,17 @@
     step = 128 // kdim
     for c in range(chunks):
         turned = pltpu.roll(signs, lax.rem(features - offset - c * width + features, features), 1)
-        sign_refs[c][...] = repeat_lanes(turned[:, :128], width, lanes)
+        sign = repeat_lanes(turned[:, :128], width, lanes)[:1]
+        bounds = []
+        for child in range(2):
+            low = low_ref[child].astype(jnp.float32) / 1024.0
+            high = high_ref[child].astype(jnp.float32) / 1024.0
+            middle = 0.5 * (low + high)
+            bounds.append(jnp.where(sign < 0, middle, low))
+            bounds.append(jnp.where(sign > 0, middle, high))
+            bounds.append(jnp.where(sign > 0, middle, low))
+            bounds.append(jnp.where(sign < 0, middle, high))
+        bound_refs[c][...] = jnp.concatenate(bounds, axis=0)
         rows = hess_ref[c * width : (c + 1) * width, :]
         turned = jnp.concatenate([rows] * (128 // width), axis=0).T
         total = jnp.zeros((levels, lanes), jnp.float32)
@@ -322,20 +332,20 @@
                 grad_refs[c][b * kdim : b * kdim + 128, tile * 128 : (tile + 1) * 128] = block.T
 
 
-def parent_layout(width, levels, lanes, kdim, chunks, line, child_owner, owners, signs, parent, hess, tie):
+def parent_layout(width, levels, lanes, kdim, chunks, line, child_owner, owners, low, high, signs, parent, hess, tie):
     shapes = [jax.ShapeDtypeStruct((levels * kdim, lanes), jnp.float32)] * chunks
     shapes += [jax.ShapeDtypeStruct((levels, lanes), jnp.float32)] * chunks
-    shapes += [jax.ShapeDtypeStruct((8, lanes), jnp.int32)] * chunks
-    shapes += [jax.ShapeDtypeStruct((8, 128), jnp.int32)]
+    shapes += [jax.ShapeDtypeStruct((8, lanes), jnp.float32)] * chunks
+    shapes += [jax.ShapeDtypeStruct((8, lanes), jnp.int32)]
     out = pl.pallas_call(
         functools.partial(layout_kernel, width, levels, kdim, chunks, line),
-        in_specs=[SMEM_SPEC] * 2 + [VMEM_SPEC] * 3 + [pl.BlockSpec(memory_space=pl.ANY)],
+        in_specs=[SMEM_SPEC] * 4 + [VMEM_SPEC] * 3 + [pl.BlockSpec(memory_space=pl.ANY)],
         out_specs=[VMEM_SPEC] * (3 * chunks + 1),
         out_shape=shapes,
         compiler_params=pltpu.CompilerParams(vmem_limit_bytes=16 * MIB),
         cost_estimate=pl.CostEstimate(flops=0, bytes_accessed=2 * parent.size * 4, transcendentals=0),
         name="parent_layout",
-    )(child_owner, owners, signs.reshape(1, -1), parent, hess, tie)
+    )(child_owner, owners, low, high, signs.reshape(1, -1), parent, hess, tie)
     return out[:chunks], out[chunks : 2 * chunks], out[2 * chunks : 3 * chunks], out[-1]
 
 
@@ -355,14 +365,14 @@
     return running - total, running, whole
 
 
-def gain_kernel(width, levels, kdim, last_ref, right_ref, left_ref, par_grad_ref, par_hess_ref, sign_ref, low_ref, high_ref, out_ref, grad_ref, hess_ref):
+def gain_kernel(width, levels, kdim, last_ref, right_ref, left_ref, par_grad_ref, par_hess_ref, bound_ref, tie_ref, out_ref, grad_ref, hess_ref):
+    del tie_ref
     hess_at = levels * kdim
     lanes = out_ref.shape[2]
 
     def small_at(start, size):
         return last_ref[pl.ds(start, size), :] + right_ref[pl.ds(start, size), :] + left_ref[pl.ds(start, size), :]
 
-    sign = sign_ref[:1, :]
     small_hess = small_at(hess_at, levels)
     hess_ref[0] = small_hess
     hess_ref[1] = par_hess_ref[...] - small_hess
@@ -383,15 +393,9 @@
 
     zero_g = jnp.zeros((kdim, lanes), jnp.float32)
     zero_h = jnp.zeros((1, lanes), jnp.float32)
-    ends = lax.fori_loop(0, levels, add_up, (zero_g, zero_g, zero_h, zero_h))
+    ends = lax.fori_loop(0, levels, add_up, (zero_g, zero_g, zero_h, zero_h), unroll=4)
     for c in range(2):
-        low = low_ref[c].astype(jnp.float32) / 1024.0
-        high = high_ref[c].astype(jnp.float32) / 1024.0
-        middle = 0.5 * (low + high)
-        low_left = jnp.where(sign < 0, middle, low)
-        high_left = jnp.where(sign > 0, middle, high)
-        low_right = jnp.where(sign > 0, middle, low)
-        high_right = jnp.where(sign < 0, middle, high)
+        low_left, high_left, low_right, high_right = [bound_ref[4 * c + i : 4 * c + i + 1, :] for i in range(4)]
         grad_before, _, grad_all = lane_prefix(ends[c], width)
         hess_rows = jnp.broadcast_to(ends[2 + c], (8, lanes))
         hess_before, _, hess_all = lane_prefix(hess_rows, width)
@@ -411,13 +415,13 @@
             out_ref[c, pl.ds(b, 1), :] = (left + right) * (-1.0 / kdim)
             return carry
 
-        lax.fori_loop(0, levels, one_bin, 0)
-
-
-def gains_of(width, levels, lanes, kdim, last, right, left, par_grad, par_hess, sign, node_low, node_high):
+        lax.fori_loop(0, levels, one_bin, 0, unroll=4)
+
+
+def gains_of(width, levels, lanes, kdim, last, right, left, par_grad, par_hess, bounds, tie):
     return pl.pallas_call(
         functools.partial(gain_kernel, width, levels, kdim),
-        in_specs=[VMEM_SPEC] * 6 + [SMEM_SPEC] * 2,
+        in_specs=[VMEM_SPEC] * 6 + [pl.BlockSpec(memory_space=pl.ANY)],
         out_specs=VMEM_SPEC,
         out_shape=jax.ShapeDtypeStruct((2, levels, lanes), jnp.float32),
         scratch_shapes=[
@@ -427,7 +431,7 @@
         compiler_params=pltpu.CompilerParams(vmem_limit_bytes=24 * MIB),
         cost_estimate=pl.CostEstimate(flops=50 * levels * kdim * lanes, bytes_accessed=16 * levels * kdim * lanes, transcendentals=0),
         name="gains",
-    )(last, right, left, par_grad, par_hess, sign, node_low, node_high)
+    )(last, right, left, par_grad, par_hess, bounds, tie)
 
 
 def chosen(shift, got):
@@ -437,16 +441,18 @@
     return value
 
 
-def finish_kernel(width, *refs):
+def finish_kernel(width, line, route_ref, *refs):
     out_ref = refs[-1]
-    chunks = len(refs) - 1
+    chunks = (len(refs) - 1) // (line + 1)
     slab = width * chunks
-    lanes = refs[0].shape[2]
+    lanes = route_ref.shape[1]
+    shift, same = route_ref[:1, :], route_ref[2:3, :]
     total = jnp.zeros((128, 128), jnp.float32)
     column = lax.broadcasted_iota(jnp.int32, (128, 128), 1)
     for child in range(2):
         for c in range(chunks):
-            gain = refs[c][child]
+            got = [ref[child] for ref in refs[c * (line + 1) : (c + 1) * (line + 1)]]
+            gain = jnp.where(same == 1, chosen(shift, got[:line]), got[line])
             at = child * slab + c * width
             pieces = []
             for j in range(lanes // width):
@@ -460,14 +466,15 @@
         out_ref[:, child, :] = turned[child * slab : (child + 1) * slab]
 
 
-def finish(width, nbins, parts):
+def finish(width, nbins, line, route, parts):
+    flat = [x for part in parts for x in part]
     return pl.pallas_call(
-        functools.partial(finish_kernel, width),
-        in_specs=[VMEM_SPEC] * len(parts),
+        functools.partial(finish_kernel, width, line),
+        in_specs=[VMEM_SPEC] * (1 + len(flat)),
         out_specs=VMEM_SPEC,
         out_shape=jax.ShapeDtypeStruct((width * len(parts), 2, nbins), jnp.float32),
         name="finish",
-    )(*parts)
+    )(route, *flat)
 
 
 def one_of(z, members):
@@ -522,16 +529,19 @@
     a0, a1, a2, b1, b2, last = {}, {}, {}, {}, {}, {}
     for c in range(chunks):
         a0[c] = lax.ppermute(units[0, c], "dp", inward)
+    last[0] = unit(3, 0, (units[0, chunks - 1],))
     for c in range(chunks):
-        units[1, c] = unit(1, c, (a0[c], units[1, c - 1] if c else units[0, chunks - 1]))
+        units[1, c] = unit(1, c, (a0[c], units[1, c - 1] if c else last[0]))
         b1[c] = lax.ppermute(units[0, c] + a0[c], "dp", middle)
         a1[c] = lax.ppermute(units[1, c], "dp", inward)
     for c in range(chunks):
-        units[2, c] = unit(2, c, (a1[c], last[c - 1] if c else units[1, chunks - 1]))
+        units[2, c] = unit(2, c, (a1[c], units[2, c - 1] if c else units[1, chunks - 1]))
         b2[c] = lax.ppermute(units[1, c] + a1[c], "dp", middle)
         a2[c] = lax.ppermute(units[2, c] + b1[c], "dp", outer)
-        last[c] = unit(3, c, (units[2, c],))
-    return last, a2, b2, set_up(units[2, chunks - 1])
+    layout = set_up(units[2, 0])
+    for c in range(1, chunks):
+        last[c] = unit(3, c, (units[2, chunks - 1],))
+    return last, a2, b2, layout
 
 
 def per_device(bins, grads, hess, node_side, signs, child_owner, parent_owner, parent_grad, parent_hess, node_low, node_high):
@@ -556,7 +566,7 @@
 
     def set_up(tie):
         return parent_layout(
-            width, levels, lanes, kdim, chunks, line, child_owner, parent_owner, signs, parent_grad[0], parent_hess[0], tie
+            width, levels, lanes, kdim, chunks, line, child_owner, parent_owner, node_low, node_high, signs, parent_grad[0], parent_hess[0], tie
         )
 
     units = {}
@@ -565,17 +575,17 @@
         units[0, c] = unit(0, c, [mine, theirs], tie=(units[0, c - 1],))
     collect = sum_line_of_4 if line == 4 else sum_line
     last, from_left, from_right, layout = collect(line, chunks, units, lambda p, c, tie: unit(p, c, [mine, theirs], tie=tie), set_up)
-    par_grad, par_hess, sign, route = layout
+    par_grad, par_hess, bounds, route = layout
 
     done = []
     for c in range(chunks):
         gain = gains_of(
-            width, levels, lanes, kdim, last[c], from_left[c], from_right[c], par_grad[c], par_hess[c], sign[c], node_low, node_high
+            width, levels, lanes, kdim, last[c], from_left[c], from_right[c], par_grad[c], par_hess[c], bounds[c], last[chunks - 1]
         )
         got = [gain] + [lax.ppermute(gain, "dp", [(i, (i + s) % line) for i in range(line)]) for s in range(1, line)]
         crossed = lax.ppermute(chosen(route[1, 0], got), "sub", swap)
-        done.append(jnp.where(route[2, 0] == 1, chosen(route[0, 0], got), crossed))
-    return finish(width, nbins, done)[None]
+        done.append([*got, crossed])
+    return finish(width, nbins, line, route, done)[None]
 
 
 def solution(mesh):

time: 122 us -> 113 us (0.926)
  waiting for transfers between devices: 10.4 us -> 7.04 us
  between operations: 5 us -> 2.47 us
  Pallas kernels: 65.8 us -> 63.9 us
  other arithmetic: 1.68 us -> 0.45 us
    ppermute x2, waiting for transfers between devices: 5.69 us -> 0.43 us  [sum_line_of_4(): a0[c] = lax.ppermute(units[0, c], 'dp', inward)]
    ppermute x6, waiting for transfers between devices: 1.54 us -> 4.98 us  [per_device(): lax.ppermute(gain, 'dp', [(i, (i + s) % line) for i in range(line)])]
    ppermute x2, starting transfers between devices: 7.57 us -> 10.1 us  [sum_line_of_4(): a2[c] = lax.ppermute(units[2, c] + b1[c], 'dp', outer)]
    pallas_call x2, Pallas kernels: 5.33 us -> 3.14 us  [gains_of(): pl.pallas_call(functools.partial(gain_kernel, width, levels, kdim), in_sp...]
    ppermute x2, waiting for transfers between devices: 2.59 us -> 0.4 us  [sum_line_of_4(): a1[c] = lax.ppermute(units[1, c], 'dp', inward)]
    ppermute x6, starting transfers between devices: 8.88 us -> 7.08 us  [per_device(): lax.ppermute(gain, 'dp', [(i, (i + s) % line) for i in range(line)])]
    select_n x2 -> x0, other arithmetic: 1.24 us -> none  [per_device(): done.append(jnp.where(route[2, 0] == 1, chosen(route[0, 0], got), crossed))]
    unnamed x22 -> x42, local copies, waits for them, and re-layouts: 2.24 us -> 2.86 us
  transfers between devices with their start and end apart: 20 -> 20, of which waited for: 7 -> 6; matrix products, arithmetic and copies ran while one was open for 1% -> 1% of each run, Pallas kernels for 43% -> 45%
where the time goes in v3:
time: 113 us
  Pallas kernels  63.9 us (57%)
  starting transfers between devices  35.5 us (31%)
  waiting for transfers between devices  7.04 us (6%)
  local copies, waits for them, and re-layouts  3.38 us (3%)
  between operations  2.47 us (2%)
    pallas_call x9, Pallas kernels, hist(): pl.pallas_call(functools.partial(hist_kernel, first_column, width, levels...  50 us
    ppermute x2, starting transfers between devices, sum_line_of_4(): a2[c] = lax.ppermute(units[2, c] + b1[c], 'dp', outer)  10.1 us
    ppermute x2, starting transfers between devices, sum_line_of_4(): a1[c] = lax.ppermute(units[1, c], 'dp', inward)  8.15 us
    pallas_call x1, Pallas kernels, prep(): pl.pallas_call(functools.partial(prep_kernel, line, slab), in_specs=[SMEM...  7.75 us
    ppermute x6, starting transfers between devices, per_device(): lax.ppermute(gain, 'dp', [(i, (i + s) % line) for i in range(line)])  7.08 us
    ppermute x2, starting transfers between devices, sum_line_of_4(): a0[c] = lax.ppermute(units[0, c], 'dp', inward)  6.59 us
    ppermute x6, waiting for transfers between devices, per_device(): lax.ppermute(gain, 'dp', [(i, (i + s) % line) for i in range(line)])  4.98 us
    pallas_call x2, Pallas kernels, gains_of(): pl.pallas_call(functools.partial(gain_kernel, width, levels, kdim), in_sp...  3.14 us
  transfers between devices with their start and end apart: 20, of which 6 were waited for; matrix products, arithmetic and copies ran while one was open for 1% of the time, Pallas kernels for 45%

profile of v3, /device:TPU:0, one launch (start us, length us, event | category | flops | bytes accessed | tf_op | source)
XLA Modules:
  0.0 112.7 jit_solution(6599954072885347245)
XLA Ops:
  0.0 7.7 %prep.1 = (bf16[2048,256]{1,0:T(8,128)(2,1)}, f32[2048,256]{1,0:T(8,128)}, bf16[48,2048]{1,0:T(8,128)(2,1)}, f32[40,2048]{1,0:T(8,128)}) custom-call(s32[8]{0:T(128)} %owner_ref.3, s32[2048,512]{1,0:T(8,128)} %bins_ref.1, bf16[32,2048]{1,0:T(8,128)(2,1)} %bitcast.12, bf16[2048]{0:T(1024)(128)(2,1)} %hess_ref.1, s32[1,2048]{1,0:T(1,128)} %bitcast.13), custom_call_target="tpu_custom_call" | custom-call | flops 2147483648 | bytes 8388608 | tf_op jit(solution)/shard_map/prep/pallas_call | solution.py:119
  8.4 1.2 %copy-done = bf16[2048,256]{1,0:T(8,128)(2,1)S(1)} copy-done((bf16[2048,256]{1,0:T(8,128)(2,1)S(1)}, bf16[2048,256]{1,0:T(8,128)(2,1)}, u32[]{:S(2)}) %copy-start) | copy-done | bytes 1048600
  10.5 4.1 %hist.9.refs_2_ = f32[528,256]{1,0:T(8,128)S(1)} custom-call(bf16[2048,256]{1,0:T(8,128)(2,1)S(1)} %copy-done, bf16[48,2048]{1,0:T(8,128)(2,1)S(1)} %copy-done.2), custom_call_target="tpu_custom_call" | custom-call | flops 524288 | bytes 524288 | tf_op jit(solution)/shard_map/hist/pallas_call | solution.py:247
  14.7 4.1 %hist.10.refs_4_ = f32[528,256]{1,0:T(8,128)S(1)} custom-call(f32[2048,256]{1,0:T(8,128)S(1)} %collective-permute-done.refs_0_.refs_2_, f32[40,2048]{1,0:T(8,128)S(1)} %collective-permute-done.1.refs_1_.refs_3_, f32[528,256]{1,0:T(8,128)S(1)} %hist.9.refs_2_), custom_call_target="tpu_custom_call" | custom-call | flops 524288 | bytes 524288 | tf_op jit(solution)/shard_map/hist/pallas_call | solution.py:247
  18.8 5.2 %collective-permute-start.2 = (f32[528,256]{1,0:T(8,128)S(1)}, f32[528,256]{1,0:T(8,128)S(1)}, u32[]{:S(2)}, u32[]{:S(2)}) collective-permute-start(f32[528,256]{1,0:T(8,128)S(1)} %hist.10.refs_4_), channel_id=1, source_target_pairs={{0,4},{12,8},{1,5},{13,9},{2,6},{14,10},{3,7},{15,11},{16,20},{28,... | collective-permute-start | bytes 1622024 | tf_op jit(solution)/shard_map/ppermute | solution.py:531
  24.1 6.0 %hist.11.refs_4_ = f32[528,256]{1,0:T(8,128)S(1)} custom-call(bf16[2048,256]{1,0:T(8,128)(2,1)S(1)} %copy-done.1, bf16[48,2048]{1,0:T(8,128)(2,1)S(1)} %copy-done.2, f32[2048,256]{1,0:T(8,128)S(1)} %collective-permute-done.refs_0_.refs_2_, f32[40,2048]{1,0:T(8,128)S(1)} %collective-permute-done.1.refs_1_.refs_3_, f32[528,256]{1,0:T(8,128)S(1)} %hist.10.refs_4_), custom_call_target="tpu_custom_call" | custom-call | flops 1048576 | bytes 1048576 | tf_op jit(solution)/shard_map/hist/pallas_call | solution.py:247
  30.0 1.3 %collective-permute-start.4 = (f32[528,256]{1,0:T(8,128)S(1)}, f32[528,256]{1,0:T(8,128)S(1)}, u32[]{:S(2)}, u32[]{:S(2)}) collective-permute-start(f32[528,256]{1,0:T(8,128)S(1)} %hist.11.refs_4_), channel_id=1, source_target_pairs={{0,4},{12,8},{1,5},{13,9},{2,6},{14,10},{3,7},{15,11},{16,20},{28,... | collective-permute-start | bytes 1622024 | tf_op jit(solution)/shard_map/ppermute | solution.py:531
  31.4 6.0 %hist.12.refs_5_.last_ref = f32[528,256]{1,0:T(8,128)S(1)} custom-call(bf16[2048,256]{1,0:T(8,128)(2,1)S(1)} %copy-done.1, bf16[48,2048]{1,0:T(8,128)(2,1)S(1)} %copy-done.2, f32[2048,256]{1,0:T(8,128)S(1)} %collective-permute-done.refs_0_.refs_2_, f32[40,2048]{1,0:T(8,128)S(1)} %collective-permute-done.1.refs_1_.refs_3_, f32[528,256]{1,0:T(8,128)S(1)} %hist.11.refs_4_), custom_call_target="tpu_custom_call" | custom-call | flops 1048576 | bytes 1048576 | tf_op jit(solution)/shard_map/hist/pallas_call | solution.py:247
  37.4 5.9 %hist.13.refs_5_ = f32[528,256]{1,0:T(8,128)S(1)} custom-call(bf16[2048,256]{1,0:T(8,128)(2,1)S(1)} %copy-done.1, bf16[48,2048]{1,0:T(8,128)(2,1)S(1)} %copy-done.2, f32[2048,256]{1,0:T(8,128)S(1)} %collective-permute-done.refs_0_.refs_2_, f32[40,2048]{1,0:T(8,128)S(1)} %collective-permute-done.1.refs_1_.refs_3_, ...), custom_call_target="tpu_custom_call" | custom-call | flops 1048576 | bytes 1048576 | tf_op jit(solution)/shard_map/hist/pallas_call | solution.py:247
  43.3 3.7 %collective-permute-start.3 = (f32[528,256]{1,0:T(8,128)S(1)}, f32[528,256]{1,0:T(8,128)S(1)}, u32[]{:S(2)}, u32[]{:S(2)}) collective-permute-start(f32[528,256]{1,0:T(8,128)S(1)} %hist.13.refs_5_), channel_id=1, source_target_pairs={{0,4},{12,8},{1,5},{13,9},{2,6},{14,10},{3,7},{15,11},{16,20},{28,... | collective-permute-start | bytes 1622024 | tf_op jit(solution)/shard_map/ppermute | solution.py:536
  48.2 6.0 %hist.14.refs_5_ = f32[528,256]{1,0:T(8,128)S(1)} custom-call(bf16[2048,256]{1,0:T(8,128)(2,1)S(1)} %copy-done.1, bf16[48,2048]{1,0:T(8,128)(2,1)S(1)} %copy-done.2, f32[2048,256]{1,0:T(8,128)S(1)} %collective-permute-done.refs_0_.refs_2_, f32[40,2048]{1,0:T(8,128)S(1)} %collective-permute-done.1.refs_1_.refs_3_, ...), custom_call_target="tpu_custom_call" | custom-call | flops 1048576 | bytes 1048576 | tf_op jit(solution)/shard_map/hist/pallas_call | solution.py:247
  54.2 4.4 %collective-permute-start.8 = (f32[528,256]{1,0:T(8,128)S(1)}, f32[528,256]{1,0:T(8,128)S(1)}, u32[]{:S(2)}, u32[]{:S(2)}) collective-permute-start(f32[528,256]{1,0:T(8,128)S(1)} %hist.14.refs_5_), channel_id=1, source_target_pairs={{0,4},{12,8},{1,5},{13,9},{2,6},{14,10},{3,7},{15,11},{16,20},{28,... | collective-permute-start | bytes 1622024 | tf_op jit(solution)/shard_map/ppermute | solution.py:536
  60.6 6.0 %hist.15.tie_ref.refs_5_ = f32[528,256]{1,0:T(8,128)S(1)} custom-call(bf16[2048,256]{1,0:T(8,128)(2,1)S(1)} %copy-done.1, bf16[48,2048]{1,0:T(8,128)(2,1)S(1)} %copy-done.2, f32[2048,256]{1,0:T(8,128)S(1)} %collective-permute-done.refs_0_.refs_2_, f32[40,2048]{1,0:T(8,128)S(1)} %collective-permute-done.1.refs_1_.refs_3_, ...), custom_call_target="tpu_custom_call" | custom-call | flops 1048576 | bytes 1048576 | tf_op jit(solution)/shard_map/hist/pallas_call | solution.py:247
  66.7 5.3 %collective-permute-start.6 = (f32[528,256]{1,0:T(8,128)S(1)}, f32[528,256]{1,0:T(8,128)S(1)}, u32[]{:S(2)}, u32[]{:S(2)}) collective-permute-start(f32[528,256]{1,0:T(8,128)S(1)} %add.19), channel_id=1, source_target_pairs={{0,4},{4,0},{8,12},{12,8},{1,5},{5,1},{9,13},{13,9},{2,6},{6,2},{1... | collective-permute-start | bytes 1622024 | tf_op jit(solution)/shard_map/ppermute | solution.py:540
  73.0 6.0 %hist.16.refs_4_ = f32[528,256]{1,0:T(8,128)S(1)} custom-call(bf16[2048,256]{1,0:T(8,128)(2,1)S(1)} %copy-done.1, bf16[48,2048]{1,0:T(8,128)(2,1)S(1)} %copy-done.2, f32[2048,256]{1,0:T(8,128)S(1)} %collective-permute-done.refs_0_.refs_2_, f32[40,2048]{1,0:T(8,128)S(1)} %collective-permute-done.1.refs_1_.refs_3_, ...), custom_call_target="tpu_custom_call" | custom-call | flops 1048576 | bytes 1048576 | tf_op jit(solution)/shard_map/hist/pallas_call | solution.py:247
  79.1 4.7 %collective-permute-start.14 = (f32[528,256]{1,0:T(8,128)S(1)}, f32[528,256]{1,0:T(8,128)S(1)}, u32[]{:S(2)}, u32[]{:S(2)}) collective-permute-start(f32[528,256]{1,0:T(8,128)S(1)} %add.22), channel_id=1, source_target_pairs={{0,4},{4,0},{8,12},{12,8},{1,5},{5,1},{9,13},{13,9},{2,6},{6,2},{1... | collective-permute-start | bytes 1622024 | tf_op jit(solution)/shard_map/ppermute | solution.py:540
  83.9 1.2 %parent_layout.1 = (f32[512,256]{1,0:T(8,128)S(1)}, f32[512,256]{1,0:T(8,128)S(1)}, f32[16,256]{1,0:T(8,128)S(1)}, f32[16,256]{1,0:T(8,128)S(1)}, f32[8,256]{1,0...) custom-call(s32[8]{0:T(128)S(1)} %copy-done.9, s32[8]{0:T(128)S(1)} %copy-done.10, s32[2]{0:T(128)S(1)} %copy-done.11, ...), custom_call_target="tpu_custom_call" | custom-call | bytes 2097152 | tf_op jit(solution)/shard_map/parent_layout/pallas_call | solution.py:340
  85.1 6.0 %hist.17.tie_ref.last_ref = f32[528,256]{1,0:T(8,128)S(1)} custom-call(bf16[2048,256]{1,0:T(8,128)(2,1)S(1)} %copy-done.1, bf16[48,2048]{1,0:T(8,128)(2,1)S(1)} %copy-done.2, f32[2048,256]{1,0:T(8,128)S(1)} %collective-permute-done.refs_0_.refs_2_, f32[40,2048]{1,0:T(8,128)S(1)} %collective-permute-done.1.refs_1_.refs_3_, f32[528,256]{1,0:T(8,128)S(1)} %hist.16.refs_4_), custom_call_target="tpu_custom_call" | custom-call | flops 1048576 | bytes 1048576 | tf_op jit(solution)/shard_map/hist/pallas_call | solution.py:247
  91.1 1.6 %gains.2.refs_0_ = f32[2,16,256]{2,1,0:T(8,128)S(1)} custom-call(f32[528,256]{1,0:T(8,128)S(1)} %hist.12.refs_5_.last_ref, f32[528,256]{1,0:T(8,128)S(1)} %collective-permute-done.6.right_ref, f32[528,256]{1,0:T(8,128)S(1)} %collective-permute-done.7.left_ref, f32[512,256]{1,0:T(8,128)S(1)} %get-tuple-element.21.par_grad_ref, ...), custom_call_target="tpu_custom_call" | custom-call | flops 6553600 | bytes 2097152 | tf_op jit(solution)/shard_map/gains/pallas_call | solution.py:422
  93.7 1.6 %collective-permute-start.10 = (f32[2,16,256]{2,1,0:T(8,128)S(1)}, f32[2,16,256]{2,1,0:T(8,128)S(1)}, u32[]{:S(2)}, u32[]{:S(2)}) collective-permute-start(f32[2,16,256]{2,1,0:T(8,128)S(1)} %gains.2.refs_0_), channel_id=1, source_target_pairs={{0,8},{4,12},{8,0},{12,4},{1,9},{5,13},{9,1},{13,5},{2,10},{6,14},... | collective-permute-start | bytes 98312 | tf_op jit(solution)/shard_map/ppermute | solution.py:585
  97.8 1.6 %gains.3.refs_5_ = f32[2,16,256]{2,1,0:T(8,128)S(1)} custom-call(f32[528,256]{1,0:T(8,128)S(1)} %hist.17.tie_ref.last_ref, f32[528,256]{1,0:T(8,128)S(1)} %collective-permute-done.14.right_ref, f32[528,256]{1,0:T(8,128)S(1)} %collective-permute-done.15.left_ref, f32[512,256]{1,0:T(8,128)S(1)} %get-tuple-element.24.par_grad_ref, ...), custom_call_target="tpu_custom_call" | custom-call | flops 6553600 | bytes 2097152 | tf_op jit(solution)/shard_map/gains/pallas_call | solution.py:422
  99.3 3.9 %collective-permute-start.18 = (f32[2,16,256]{2,1,0:T(8,128)S(1)}, f32[2,16,256]{2,1,0:T(8,128)S(1)}, u32[]{:S(2)}, u32[]{:S(2)}) collective-permute-start(f32[2,16,256]{2,1,0:T(8,128)S(1)} %gains.3.refs_5_), channel_id=1, source_target_pairs={{0,12},{4,0},{8,4},{12,8},{1,13},{5,1},{9,5},{13,9},{2,14},{6,2},{... | collective-permute-start | bytes 98312 | tf_op jit(solution)/shard_map/ppermute | solution.py:585
  104.8 3.2 %collective-permute-done.17.refs_7_ = f32[2,16,256]{2,1,0:T(8,128)S(1)} collective-permute-done((f32[2,16,256]{2,1,0:T(8,128)S(1)}, f32[2,16,256]{2,1,0:T(8,128)S(1)}, u32[]{:S(2)}, u32[]{:S(2)}) %collective-permute-start.17) | collective-permute-done | bytes 32800 | tf_op jit(solution)/shard_map/ppermute | solution.py:585
  111.0 1.8 %finish.1 = f32[64,2,128]{2,1,0:T(2,128)} custom-call(s32[8,256]{1,0:T(8,128)} %copy-done.7, f32[2,16,256]{2,1,0:T(8,128)} %copy-done.4, f32[2,16,256]{2,1,0:T(8,128)} %copy-done.15, f32[2,16,256]{2,1,0:T(8,128)} %copy-done.14, f32[2,16,256]{2,1,0:T(8,128)} %copy-done.13, f32[2,16,256]{2,1,0:T(8,128)} %copy-done.19, f32[2,16,256]{2,1,0:T(8,128)} %copy-done.5, ...), custom_call_target="tpu_custom_call" | custom-call | tf_op jit(solution)/shard_map/finish/pallas_call | solution.py:471
  (81 shorter events, 11.7 us)
Async XLA Ops:
  7.8 6.9 %collective-permute-start = (f32[2048,256]{1,0:T(8,128)}, f32[2048,256]{1,0:T(8,128)S(1)}, u32[]{:S(2)}, u32[]{:S(2)}) collective-permute-start(f32[2048,256]{1,0:T(8,128)} %get-tuple-element.18), channel_id=1, source_target_pairs={{0,1},{1,0},{2,3},{3,2},{4,5},{5,4},{6,7},{7,6},{8,9},{9,8},{10,11... | collective-permute-start | bytes 6291464 | tf_op jit(solution)/shard_map/ppermute | solution.py:560
  8.3 6.4 %collective-permute-start.1 = (f32[40,2048]{1,0:T(8,128)}, f32[40,2048]{1,0:T(8,128)S(1)}, u32[]{:S(2)}, u32[]{:S(2)}) collective-permute-start(f32[40,2048]{1,0:T(8,128)} %get-tuple-element.19), channel_id=1, source_target_pairs={{0,1},{1,0},{2,3},{3,2},{4,5},{5,4},{6,7},{7,6},{8,9},{9,8},{10,11... | collective-permute-start | bytes 983048 | tf_op jit(solution)/shard_map/ppermute | solution.py:559
  18.8 18.6 %collective-permute-start.2 = (f32[528,256]{1,0:T(8,128)S(1)}, f32[528,256]{1,0:T(8,128)S(1)}, u32[]{:S(2)}, u32[]{:S(2)}) collective-permute-start(f32[528,256]{1,0:T(8,128)S(1)} %hist.10.refs_4_), channel_id=1, source_target_pairs={{0,4},{12,8},{1,5},{13,9},{2,6},{14,10},{3,7},{15,11},{16,20},{28,... | collective-permute-start | bytes 1622024 | tf_op jit(solution)/shard_map/ppermute | solution.py:531
  30.0 18.2 %collective-permute-start.4 = (f32[528,256]{1,0:T(8,128)S(1)}, f32[528,256]{1,0:T(8,128)S(1)}, u32[]{:S(2)}, u32[]{:S(2)}) collective-permute-start(f32[528,256]{1,0:T(8,128)S(1)} %hist.11.refs_4_), channel_id=1, source_target_pairs={{0,4},{12,8},{1,5},{13,9},{2,6},{14,10},{3,7},{15,11},{16,20},{28,... | collective-permute-start | bytes 1622024 | tf_op jit(solution)/shard_map/ppermute | solution.py:531
  43.3 16.5 %collective-permute-start.3 = (f32[528,256]{1,0:T(8,128)S(1)}, f32[528,256]{1,0:T(8,128)S(1)}, u32[]{:S(2)}, u32[]{:S(2)}) collective-permute-start(f32[528,256]{1,0:T(8,128)S(1)} %hist.13.refs_5_), channel_id=1, source_target_pairs={{0,4},{12,8},{1,5},{13,9},{2,6},{14,10},{3,7},{15,11},{16,20},{28,... | collective-permute-start | bytes 1622024 | tf_op jit(solution)/shard_map/ppermute | solution.py:536
  47.1 19.5 %collective-permute-start.5 = (f32[528,256]{1,0:T(8,128)S(1)}, f32[528,256]{1,0:T(8,128)S(1)}, u32[]{:S(2)}, u32[]{:S(2)}) collective-permute-start(f32[528,256]{1,0:T(8,128)S(1)} %add.18), channel_id=1, source_target_pairs={{4,8},{8,4},{5,9},{9,5},{6,10},{10,6},{7,11},{11,7},{20,24},{24,20... | collective-permute-start | bytes 1622024 | tf_op jit(solution)/shard_map/ppermute | solution.py:535
  54.2 17.8 %collective-permute-start.8 = (f32[528,256]{1,0:T(8,128)S(1)}, f32[528,256]{1,0:T(8,128)S(1)}, u32[]{:S(2)}, u32[]{:S(2)}) collective-permute-start(f32[528,256]{1,0:T(8,128)S(1)} %hist.14.refs_5_), channel_id=1, source_target_pairs={{0,4},{12,8},{1,5},{13,9},{2,6},{14,10},{3,7},{15,11},{16,20},{28,... | collective-permute-start | bytes 1622024 | tf_op jit(solution)/shard_map/ppermute | solution.py:536
  58.7 20.3 %collective-permute-start.13 = (f32[528,256]{1,0:T(8,128)S(1)}, f32[528,256]{1,0:T(8,128)S(1)}, u32[]{:S(2)}, u32[]{:S(2)}) collective-permute-start(f32[528,256]{1,0:T(8,128)S(1)} %add.21), channel_id=1, source_target_pairs={{4,8},{8,4},{5,9},{9,5},{6,10},{10,6},{7,11},{11,7},{20,24},{24,20... | collective-permute-start | bytes 1622024 | tf_op jit(solution)/shard_map/ppermute | solution.py:535
  59.9 31.2 %collective-permute-start.7 = (f32[528,256]{1,0:T(8,128)S(1)}, f32[528,256]{1,0:T(8,128)S(1)}, u32[]{:S(2)}, u32[]{:S(2)}) collective-permute-start(f32[528,256]{1,0:T(8,128)S(1)} %add.20), channel_id=1, source_target_pairs={{4,8},{8,4},{5,9},{9,5},{6,10},{10,6},{7,11},{11,7},{20,24},{24,20... | collective-permute-start | bytes 1622024 | tf_op jit(solution)/shard_map/ppermute | solution.py:539
  66.7 24.5 %collective-permute-start.6 = (f32[528,256]{1,0:T(8,128)S(1)}, f32[528,256]{1,0:T(8,128)S(1)}, u32[]{:S(2)}, u32[]{:S(2)}) collective-permute-start(f32[528,256]{1,0:T(8,128)S(1)} %add.19), channel_id=1, source_target_pairs={{0,4},{4,0},{8,12},{12,8},{1,5},{5,1},{9,13},{13,9},{2,6},{6,2},{1... | collective-permute-start | bytes 1622024 | tf_op jit(solution)/shard_map/ppermute | solution.py:540
  72.1 11.7 %copy-start.6 = (f32[1,64,128]{2,1,0:T(8,128)S(1)}, f32[1,64,128]{2,1,0:T(8,128)}, u32[]{:S(2)}) copy-start(f32[1,64,128]{2,1,0:T(8,128)} %param.19) | copy-start | bytes 98308
  72.1 11.7 %copy-start.8 = (s32[1024]{0:T(1024)S(1)}, s32[1024]{0:T(1024)}, u32[]{:S(2)}) copy-start(s32[1024]{0:T(1024)} %param.15) | copy-start | bytes 12292
  72.1 11.7 %copy-start.9 = (s32[8]{0:T(128)S(1)}, s32[8]{0:T(128)}, u32[]{:S(2)}) copy-start(s32[8]{0:T(128)} %child_ref.1) | copy-start | bytes 100
  72.2 25.6 %collective-permute-start.15 = (f32[528,256]{1,0:T(8,128)S(1)}, f32[528,256]{1,0:T(8,128)S(1)}, u32[]{:S(2)}, u32[]{:S(2)}) collective-permute-start(f32[528,256]{1,0:T(8,128)S(1)} %add.23), channel_id=1, source_target_pairs={{4,8},{8,4},{5,9},{9,5},{6,10},{10,6},{7,11},{11,7},{20,24},{24,20... | collective-permute-start | bytes 1622024 | tf_op jit(solution)/shard_map/ppermute | solution.py:539
  79.1 18.7 %collective-permute-start.14 = (f32[528,256]{1,0:T(8,128)S(1)}, f32[528,256]{1,0:T(8,128)S(1)}, u32[]{:S(2)}, u32[]{:S(2)}) collective-permute-start(f32[528,256]{1,0:T(8,128)S(1)} %add.22), channel_id=1, source_target_pairs={{0,4},{4,0},{8,12},{12,8},{1,5},{5,1},{9,13},{13,9},{2,6},{6,2},{1... | collective-permute-start | bytes 1622024 | tf_op jit(solution)/shard_map/ppermute | solution.py:540
  92.7 17.6 %copy-start.4 = (f32[2,16,256]{2,1,0:T(8,128)}, f32[2,16,256]{2,1,0:T(8,128)S(1)}, u32[]{:S(2)}) copy-start(f32[2,16,256]{2,1,0:T(8,128)S(1)} %gains.2.refs_0_) | copy-start | bytes 98308
  92.7 10.5 %collective-permute-start.11 = (f32[2,16,256]{2,1,0:T(8,128)S(1)}, f32[2,16,256]{2,1,0:T(8,128)S(1)}, u32[]{:S(2)}, u32[]{:S(2)}) collective-permute-start(f32[2,16,256]{2,1,0:T(8,128)S(1)} %gains.2.refs_0_), channel_id=1, source_target_pairs={{0,12},{4,0},{8,4},{12,8},{1,13},{5,1},{9,5},{13,9},{2,14},{6,2},{... | collective-permute-start | bytes 98312 | tf_op jit(solution)/shard_map/ppermute | solution.py:585
  93.7 10.2 %collective-permute-start.10 = (f32[2,16,256]{2,1,0:T(8,128)S(1)}, f32[2,16,256]{2,1,0:T(8,128)S(1)}, u32[]{:S(2)}, u32[]{:S(2)}) collective-permute-start(f32[2,16,256]{2,1,0:T(8,128)S(1)} %gains.2.refs_0_), channel_id=1, source_target_pairs={{0,8},{4,12},{8,0},{12,4},{1,9},{5,13},{9,1},{13,5},{2,10},{6,14},... | collective-permute-start | bytes 98312 | tf_op jit(solution)/shard_map/ppermute | solution.py:585
  95.3 8.6 %collective-permute-start.9 = (f32[2,16,256]{2,1,0:T(8,128)S(1)}, f32[2,16,256]{2,1,0:T(8,128)S(1)}, u32[]{:S(2)}, u32[]{:S(2)}) collective-permute-start(f32[2,16,256]{2,1,0:T(8,128)S(1)} %gains.2.refs_0_), channel_id=1, source_target_pairs={{0,4},{4,8},{8,12},{12,0},{1,5},{5,9},{9,13},{13,1},{2,6},{6,10},{... | collective-permute-start | bytes 98312 | tf_op jit(solution)/shard_map/ppermute | solution.py:585
  99.3 5.5 %collective-permute-start.18 = (f32[2,16,256]{2,1,0:T(8,128)S(1)}, f32[2,16,256]{2,1,0:T(8,128)S(1)}, u32[]{:S(2)}, u32[]{:S(2)}) collective-permute-start(f32[2,16,256]{2,1,0:T(8,128)S(1)} %gains.3.refs_5_), channel_id=1, source_target_pairs={{0,12},{4,0},{8,4},{12,8},{1,13},{5,1},{9,5},{13,9},{2,14},{6,2},{... | collective-permute-start | bytes 98312 | tf_op jit(solution)/shard_map/ppermute | solution.py:585
  103.2 4.8 %collective-permute-start.17 = (f32[2,16,256]{2,1,0:T(8,128)S(1)}, f32[2,16,256]{2,1,0:T(8,128)S(1)}, u32[]{:S(2)}, u32[]{:S(2)}) collective-permute-start(f32[2,16,256]{2,1,0:T(8,128)S(1)} %gains.3.refs_5_), channel_id=1, source_target_pairs={{0,8},{4,12},{8,0},{12,4},{1,9},{5,13},{9,1},{13,5},{2,10},{6,14},... | collective-permute-start | bytes 98312 | tf_op jit(solution)/shard_map/ppermute | solution.py:585
  103.2 5.8 %collective-permute-start.16 = (f32[2,16,256]{2,1,0:T(8,128)S(1)}, f32[2,16,256]{2,1,0:T(8,128)S(1)}, u32[]{:S(2)}, u32[]{:S(2)}) collective-permute-start(f32[2,16,256]{2,1,0:T(8,128)S(1)} %gains.3.refs_5_), channel_id=1, source_target_pairs={{0,4},{4,8},{8,12},{12,0},{1,5},{5,9},{9,13},{13,1},{2,6},{6,10},{... | collective-permute-start | bytes 98312 | tf_op jit(solution)/shard_map/ppermute | solution.py:585
  103.9 5.1 %collective-permute-start.12 = (f32[2,16,256]{2,1,0:T(8,128)S(1)}, f32[2,16,256]{2,1,0:T(8,128)S(1)}, u32[]{:S(2)}, u32[]{:S(2)}) collective-permute-start(f32[2,16,256]{2,1,0:T(8,128)S(1)} %select_select_fusion.1), channel_id=1, source_target_pairs={{0,1},{1,0},{2,3},{3,2},{4,5},{5,4},{6,7},{7,6},{8,9},{9,8},{10,11... | collective-permute-start | bytes 98312 | tf_op jit(solution)/shard_map/ppermute | solution.py:586
  109.0 1.3 %collective-permute-start.19 = (f32[2,16,256]{2,1,0:T(8,128)S(1)}, f32[2,16,256]{2,1,0:T(8,128)S(1)}, u32[]{:S(2)}, u32[]{:S(2)}) collective-permute-start(f32[2,16,256]{2,1,0:T(8,128)S(1)} %select_select_fusion), channel_id=1, source_target_pairs={{0,1},{1,0},{2,3},{3,2},{4,5},{5,4},{6,7},{7,6},{8,9},{9,8},{10,11... | collective-permute-start | bytes 98312 | tf_op jit(solution)/shard_map/ppermute | solution.py:586
  (17 other events, 103.5 us)

commit v4 on v3

--- a/solution.py
+++ b/solution.py
@@ -34,7 +34,7 @@
     return roles
 
 
-def prep_kernel(line, slab, owner_ref, bins_ref, grads_ref, hess_ref, side_ref, own_ref, send_ref, wt_ref, wt_send_ref, buf_ref, sems, acc_ref, acc_w_ref):
+def prep_kernel(line, slab, owner_ref, bins_ref, grads_ref, hess_ref, side_ref, own_ref, send_ref, wt_ref, wt_send_ref, buf_ref, sems, acc_ref, acc_w_ref, own_buf, send_buf, out_sems):
     rows, f_dev = bins_ref.shape
     half = f_dev // 2
     kdim = grads_ref.shape[0]
@@ -97,12 +97,21 @@
     def move(t, carry):
         part = pl.ds(pl.multiple_of(t * TILE, TILE), TILE)
         moved = jnp.dot(acc_ref[part, :], perm, preferred_element_type=jnp.float32)
-        own_ref[part, :] = moved[:, :half].astype(jnp.bfloat16)
-        send_ref[part, :] = moved[:, half:]
+        own_buf[part, :] = moved[:, :half].astype(jnp.bfloat16)
+        send_buf[part, :] = moved[:, half:]
+        pltpu.make_async_copy(own_buf.at[part, :], own_ref.at[part, :], out_sems.at[t, 0]).start()
+        pltpu.make_async_copy(send_buf.at[part, :], send_ref.at[part, :], out_sems.at[t, 1]).start()
         return carry
 
+    def moved_out(t, carry):
+        part = pl.ds(pl.multiple_of(t * TILE, TILE), TILE)
+        pltpu.make_async_copy(own_buf.at[part, :], own_ref.at[part, :], out_sems.at[t, 0]).wait()
+        pltpu.make_async_copy(send_buf.at[part, :], send_ref.at[part, :], out_sems.at[t, 1]).wait()
+        return carry
+
     total = bases[blocks]
-    lax.fori_loop(0, (total + TILE - 1) // TILE, move, 0)
+    used = (total + TILE - 1) // TILE
+    lax.fori_loop(0, used, move, 0)
     lane = lax.broadcasted_iota(jnp.int32, (acc_w_ref.shape[0], rows), 1)
     row = lax.broadcasted_iota(jnp.int32, lane.shape, 0)
     packed = jnp.where(lane < total, acc_w_ref[:, :rows], 0.0)
@@ -110,6 +119,7 @@
     packed = jnp.where(row == kdim + 1, packs, packed)
     wt_ref[...] = packed.astype(jnp.bfloat16)
     wt_send_ref[...] = packed[: kdim + 8]
+    lax.fori_loop(0, used, moved_out, 0)
 
 
 def prep(line, slab, owners, bins, grads, hess, side):
@@ -119,7 +129,7 @@
     return pl.pallas_call(
         functools.partial(prep_kernel, line, slab),
         in_specs=[SMEM_SPEC, pl.BlockSpec(memory_space=pl.ANY), VMEM_SPEC, VMEM_SPEC, VMEM_SPEC],
-        out_specs=[VMEM_SPEC] * 4,
+        out_specs=[pl.BlockSpec(memory_space=pl.ANY)] * 2 + [VMEM_SPEC] * 2,
         out_shape=[
             jax.ShapeDtypeStruct((rows, half), jnp.bfloat16),
             jax.ShapeDtypeStruct((rows, half), jnp.float32),
@@ -131,6 +141,9 @@
             pltpu.SemaphoreType.DMA((rows // TILE,)),
             pltpu.VMEM((rows + TILE + PACK, f_dev), jnp.bfloat16),
             pltpu.VMEM((kdim + 16, rows + TILE + PACK), jnp.float32),
+            pltpu.VMEM((rows, half), jnp.bfloat16),
+            pltpu.VMEM((rows, half), jnp.float32),
+            pltpu.SemaphoreType.DMA((rows // TILE, 2)),
         ],
         compiler_params=pltpu.CompilerParams(vmem_limit_bytes=PREP_MIB * MIB),
         cost_estimate=pl.CostEstimate(flops=4 * rows * f_dev * f_dev, bytes_accessed=8 * rows * f_dev, transcendentals=0),
@@ -168,14 +181,16 @@
                 weights = jnp.concatenate([weights, jnp.zeros((8, height), jnp.float32)], axis=0).astype(jnp.bfloat16)
             wt_ref[:, i * height : (i + 1) * height] = weights
 
-    def sums_of(b, tiles):
-        value = jnp.full((TILE, lanes), b.astype(jnp.float32), jnp.float32).astype(jnp.bfloat16)
-        total = jnp.zeros((wt_ref.shape[0], lanes), jnp.float32)
+    def sums_of(some, tiles):
+        values = [jnp.full((TILE, lanes), b.astype(jnp.float32), jnp.float32).astype(jnp.bfloat16) for b in some]
+        totals = [jnp.zeros((wt_ref.shape[0], lanes), jnp.float32) for _ in some]
         for first, size in tiles:
-            hit = rel_ref[pl.ds(first, size), :] == value[:size]
-            onehot = jnp.where(hit, one[:size], zero[:size])
-            total = total + jnp.dot(wt_ref[:, pl.ds(first, size)], onehot, preferred_element_type=jnp.float32)
-        return total[:kdim], total[kdim : kdim + 1]
+            found = rel_ref[pl.ds(first, size), :]
+            weights = wt_ref[:, pl.ds(first, size)]
+            for i, value in enumerate(values):
+                onehot = jnp.where(found == value[:size], one[:size], zero[:size])
+                totals[i] = totals[i] + jnp.dot(weights, onehot, preferred_element_type=jnp.float32)
+        return [(total[:kdim], total[kdim : kdim + 1]) for total in totals]
 
     def spots_of(b):
         return pl.ds(pl.multiple_of(b * kdim, kdim), kdim), pl.ds(levels * kdim + b, 1)
@@ -188,16 +203,17 @@
         place_weights(height)
         tiles = [(r, min(TILE, parts * height - r)) for r in range(0, parts * height, TILE)]
 
-        def level(b, carry):
-            grad, hess = sums_of(b, tiles)
-            grad_spot, hess_spot = spots_of(b)
-            if has_init:
-                grad, hess = grad + init_ref[grad_spot, :], hess + init_ref[hess_spot, :]
-            out_ref[grad_spot, :] = grad
-            out_ref[hess_spot, :] = hess
+        def two_levels(step, carry):
+            some = [2 * step, 2 * step + 1]
+            for b, (grad, hess) in zip(some, sums_of(some, tiles)):
+                grad_spot, hess_spot = spots_of(b)
+                if has_init:
+                    grad, hess = grad + init_ref[grad_spot, :], hess + init_ref[hess_spot, :]
+                out_ref[grad_spot, :] = grad
+                out_ref[hess_spot, :] = hess
             return carry
 
-        lax.fori_loop(0, levels, level, 0)
+        lax.fori_loop(0, levels // 2, two_levels, 0)
 
     def general():
         for i, (bins_ref, _) in enumerate(pairs):
@@ -216,7 +232,7 @@
             first = pl.multiple_of(g * step, step)
 
             def level(b, carry):
-                grad, hess = sums_of(b, [(first, TILE), (first + TILE, TILE)])
+                ((grad, hess),) = sums_of([b], [(first, TILE), (first + TILE, TILE)])
                 grad_spot, hess_spot = spots_of(b)
                 out_ref[grad_spot, :] += grad
                 out_ref[hess_spot, :] += hess
@@ -279,7 +295,7 @@
     return x
 
 
-def layout_kernel(width, levels, kdim, chunks, line, child_ref, owner_ref, low_ref, high_ref, sign_ref, parent_ref, hess_ref, tie_ref, *out_refs):
+def layout_kernel(width, levels, kdim, chunks, child_ref, owner_ref, low_ref, high_ref, sign_ref, parent_ref, hess_ref, tie_ref, *out_refs):
     del tie_ref
     grad_refs, hess_refs, bound_refs = out_refs[:chunks], out_refs[chunks : 2 * chunks], out_refs[2 * chunks : 3 * chunks]
     lanes = grad_refs[0].shape[1]
@@ -287,11 +303,8 @@
     owners = owner_ref.shape[0]
     z, core = lax.axis_index("dp"), lax.axis_index("sub")
     place = 2 * z + core
-    mine = source_of(place, child_ref, owner_ref)
-    twin = source_of(2 * z + 1 - core, child_ref, owner_ref)
-    row = lax.broadcasted_iota(jnp.int32, (8, lanes), 0)
-    route = jnp.where(row == 0, lax.rem(z - mine // 2 + line, line), lax.rem(z - twin // 2 + line, line))
-    out_refs[-1][...] = jnp.where(row == 2, jnp.where(lax.rem(mine, 2) == core, 1, 0), route)
+    route_ref = out_refs[-1]
+    route_ref[...] = jnp.full(route_ref.shape, source_of(place, child_ref, owner_ref), jnp.int32)
     slab_at = jnp.int32(0)
     for q in range(owners):
         slab_at = jnp.where(owner_ref[q] == place, q, slab_at)
@@ -332,13 +345,13 @@
                 grad_refs[c][b * kdim : b * kdim + 128, tile * 128 : (tile + 1) * 128] = block.T
 
 
-def parent_layout(width, levels, lanes, kdim, chunks, line, child_owner, owners, low, high, signs, parent, hess, tie):
+def parent_layout(width, levels, lanes, kdim, chunks, child_owner, owners, low, high, signs, parent, hess, tie):
     shapes = [jax.ShapeDtypeStruct((levels * kdim, lanes), jnp.float32)] * chunks
     shapes += [jax.ShapeDtypeStruct((levels, lanes), jnp.float32)] * chunks
     shapes += [jax.ShapeDtypeStruct((8, lanes), jnp.float32)] * chunks
     shapes += [jax.ShapeDtypeStruct((8, lanes), jnp.int32)]
     out = pl.pallas_call(
-        functools.partial(layout_kernel, width, levels, kdim, chunks, line),
+        functools.partial(layout_kernel, width, levels, kdim, chunks),
         in_specs=[SMEM_SPEC] * 4 + [VMEM_SPEC] * 3 + [pl.BlockSpec(memory_space=pl.ANY)],
         out_specs=[VMEM_SPEC] * (3 * chunks + 1),
         out_shape=shapes,
@@ -434,25 +447,19 @@
     )(last, right, left, par_grad, par_hess, bounds, tie)
 
 
-def chosen(shift, got):
-    value = got[0]
-    for s in range(1, len(got)):
-        value = jnp.where(shift == s, got[s], value)
-    return value
-
-
-def finish_kernel(width, line, route_ref, *refs):
+def finish_kernel(width, route_ref, *refs):
     out_ref = refs[-1]
-    chunks = (len(refs) - 1) // (line + 1)
+    chunks = len(refs) - 1
     slab = width * chunks
     lanes = route_ref.shape[1]
-    shift, same = route_ref[:1, :], route_ref[2:3, :]
+    source = route_ref[:1, :]
     total = jnp.zeros((128, 128), jnp.float32)
     column = lax.broadcasted_iota(jnp.int32, (128, 128), 1)
     for child in range(2):
         for c in range(chunks):
-            got = [ref[child] for ref in refs[c * (line + 1) : (c + 1) * (line + 1)]]
-            gain = jnp.where(same == 1, chosen(shift, got[:line]), got[line])
+            gain = refs[c][0, child]
+            for s in range(1, refs[c].shape[0]):
+                gain = jnp.where(source == s, refs[c][s, child], gain)
             at = child * slab + c * width
             pieces = []
             for j in range(lanes // width):
@@ -466,15 +473,14 @@
         out_ref[:, child, :] = turned[child * slab : (child + 1) * slab]
 
 
-def finish(width, nbins, line, route, parts):
-    flat = [x for part in parts for x in part]
+def finish(width, nbins, route, parts):
     return pl.pallas_call(
-        functools.partial(finish_kernel, width, line),
-        in_specs=[VMEM_SPEC] * (1 + len(flat)),
+        functools.partial(finish_kernel, width),
+        in_specs=[VMEM_SPEC] * (1 + len(parts)),
         out_specs=VMEM_SPEC,
         out_shape=jax.ShapeDtypeStruct((width * len(parts), 2, nbins), jnp.float32),
         name="finish",
-    )(route, *flat)
+    )(route, *parts)
 
 
 def one_of(z, members):
@@ -566,7 +572,7 @@
 
     def set_up(tie):
         return parent_layout(
-            width, levels, lanes, kdim, chunks, line, child_owner, parent_owner, node_low, node_high, signs, parent_grad[0], parent_hess[0], tie
+            width, levels, lanes, kdim, chunks, child_owner, parent_owner, node_low, node_high, signs, parent_grad[0], parent_hess[0], tie
         )
 
     units = {}
@@ -582,10 +588,9 @@
         gain = gains_of(
             width, levels, lanes, kdim, last[c], from_left[c], from_right[c], par_grad[c], par_hess[c], bounds[c], last[chunks - 1]
         )
-        got = [gain] + [lax.ppermute(gain, "dp", [(i, (i + s) % line) for i in range(line)]) for s in range(1, line)]
-        crossed = lax.ppermute(chosen(route[1, 0], got), "sub", swap)
-        done.append([*got, crossed])
-    return finish(width, nbins, line, route, done)[None]
+        everyone = jnp.broadcast_to(gain[None], (2 * line, *gain.shape))
+        done.append(lax.all_to_all(everyone, ("dp", "sub"), 0, 0))
+    return finish(width, nbins, route, done)[None]
 
 
 def solution(mesh):

time: 113 us -> 117 us (1.035)
  blocking collectives: 0 us -> 12.8 us
  Pallas kernels: 63.9 us -> 54.2 us
  waiting for transfers between devices: 7.04 us -> 13.6 us
  starting transfers between devices: 35.5 us -> 32.1 us
  between operations: 2.47 us -> 0.4 us
    all_to_all x0 -> x1, blocking collectives: none -> 12.8 us  [per_device(): done.append(lax.all_to_all(everyone, ('dp', 'sub'), 0, 0))]
    pallas_call x9, Pallas kernels: 50 us -> 40 us  [hist(): pl.pallas_call(functools.partial(hist_kernel, first_column, width, levels...]
    all_to_all x0 -> x1, waiting for transfers between devices: none -> 8.06 us  [per_device(): done.append(lax.all_to_all(everyone, ('dp', 'sub'), 0, 0))]
    ppermute x8 -> x0, starting transfers between devices: 7.22 us -> none  [the longest x6 7.08 us: per_device(): lax.ppermute(gain, 'dp', [(i, (i + s) % line) for i in range(line)])]
    ppermute x8 -> x0, waiting for transfers between devices: 6.15 us -> none  [the longest x6 4.98 us: per_device(): lax.ppermute(gain, 'dp', [(i, (i + s) % line) for i in range(line)])]
    all_to_all x0 -> x1, starting transfers between devices: none -> 3.41 us  [per_device(): done.append(lax.all_to_all(everyone, ('dp', 'sub'), 0, 0))]
    ppermute x2, waiting for transfers between devices: 0.43 us -> 3.13 us  [sum_line_of_4(): a0[c] = lax.ppermute(units[0, c], 'dp', inward)]
    ppermute x2, waiting for transfers between devices: 0.4 us -> 2.39 us  [sum_line_of_4(): a1[c] = lax.ppermute(units[1, c], 'dp', inward)]
  transfers between devices with their start and end apart: 20 -> 13, of which waited for: 6 -> 5; matrix products, arithmetic and copies ran while one was open for 1% -> 1% of each run, Pallas kernels for 45% -> 35%
where the time goes in v4:
time: 117 us; the launch traced here: 116 us
  Pallas kernels  54.2 us (46%)
  starting transfers between devices  32.1 us (27%)
  waiting for transfers between devices  13.6 us (12%)
  blocking collectives  12.8 us (11%)
  local copies, waits for them, and re-layouts  2.95 us (3%)
    pallas_call x9, Pallas kernels, hist(): pl.pallas_call(functools.partial(hist_kernel, first_column, width, levels...  40 us
    all_to_all x1, blocking collectives, per_device(): done.append(lax.all_to_all(everyone, ('dp', 'sub'), 0, 0))  12.8 us
    ppermute x2, starting transfers between devices, sum_line_of_4(): a2[c] = lax.ppermute(units[2, c] + b1[c], 'dp', outer)  10.1 us
    ppermute x2, starting transfers between devices, sum_line_of_4(): a1[c] = lax.ppermute(units[1, c], 'dp', inward)  8.83 us
    all_to_all x1, waiting for transfers between devices, per_device(): done.append(lax.all_to_all(everyone, ('dp', 'sub'), 0, 0))  8.06 us
    pallas_call x1, Pallas kernels, prep(): pl.pallas_call(functools.partial(prep_kernel, line, slab), in_specs=[SMEM...  7.94 us
    ppermute x2, starting transfers between devices, sum_line_of_4(): a0[c] = lax.ppermute(units[0, c], 'dp', inward)  6.27 us
    all_to_all x1, starting transfers between devices, per_device(): done.append(lax.all_to_all(everyone, ('dp', 'sub'), 0, 0))  3.41 us
  transfers between devices with their start and end apart: 13, of which 5 were waited for; matrix products, arithmetic and copies ran while one was open for 1% of the time, Pallas kernels for 35%

profile of v4, /device:TPU:0, one launch (start us, length us, event | category | flops | bytes accessed | tf_op | source)
XLA Modules:
  0.0 116.4 jit_solution(12203731361669626395)
XLA Ops:
  0.0 7.9 %prep.1 = (bf16[2048,256]{1,0:T(8,128)(2,1)}, f32[2048,256]{1,0:T(8,128)}, bf16[48,2048]{1,0:T(8,128)(2,1)}, f32[40,2048]{1,0:T(8,128)}) custom-call(s32[8]{0:T(128)} %owner_ref.3, s32[2048,512]{1,0:T(8,128)} %bins_ref.1, bf16[32,2048]{1,0:T(8,128)(2,1)} %bitcast.9, bf16[2048]{0:T(1024)(128)(2,1)} %hess_ref.1, s32[1,2048]{1,0:T(1,128)} %bitcast.10), custom_call_target="tpu_custom_call" | custom-call | flops 2147483648 | bytes 8388608 | tf_op jit(solution)/shard_map/prep/pallas_call | solution.py:129
  10.7 3.1 %hist.9.refs_2_ = f32[528,256]{1,0:T(8,128)S(1)} custom-call(bf16[2048,256]{1,0:T(8,128)(2,1)S(1)} %copy-done, bf16[48,2048]{1,0:T(8,128)(2,1)S(1)} %copy-done.2), custom_call_target="tpu_custom_call" | custom-call | flops 524288 | bytes 524288 | tf_op jit(solution)/shard_map/hist/pallas_call | solution.py:263
  13.8 3.1 %hist.10.refs_4_ = f32[528,256]{1,0:T(8,128)S(1)} custom-call(f32[2048,256]{1,0:T(8,128)S(1)} %collective-permute-done.refs_0_.refs_2_, f32[40,2048]{1,0:T(8,128)S(1)} %collective-permute-done.1.refs_1_.refs_3_, f32[528,256]{1,0:T(8,128)S(1)} %hist.9.refs_2_), custom_call_target="tpu_custom_call" | custom-call | flops 524288 | bytes 524288 | tf_op jit(solution)/shard_map/hist/pallas_call | solution.py:263
  16.9 4.9 %collective-permute-start.2 = (f32[528,256]{1,0:T(8,128)S(1)}, f32[528,256]{1,0:T(8,128)S(1)}, u32[]{:S(2)}, u32[]{:S(2)}) collective-permute-start(f32[528,256]{1,0:T(8,128)S(1)} %hist.10.refs_4_), channel_id=1, source_target_pairs={{0,4},{12,8},{1,5},{13,9},{2,6},{14,10},{3,7},{15,11},{16,20},{28,... | collective-permute-start | bytes 1622024 | tf_op jit(solution)/shard_map/ppermute | solution.py:537
  21.8 4.8 %hist.11.refs_4_ = f32[528,256]{1,0:T(8,128)S(1)} custom-call(bf16[2048,256]{1,0:T(8,128)(2,1)S(1)} %copy-done.1, bf16[48,2048]{1,0:T(8,128)(2,1)S(1)} %copy-done.2, f32[2048,256]{1,0:T(8,128)S(1)} %collective-permute-done.refs_0_.refs_2_, f32[40,2048]{1,0:T(8,128)S(1)} %collective-permute-done.1.refs_1_.refs_3_, f32[528,256]{1,0:T(8,128)S(1)} %hist.10.refs_4_), custom_call_target="tpu_custom_call" | custom-call | flops 1048576 | bytes 1048576 | tf_op jit(solution)/shard_map/hist/pallas_call | solution.py:263
  28.0 4.8 %hist.12.refs_5_.last_ref = f32[528,256]{1,0:T(8,128)S(1)} custom-call(bf16[2048,256]{1,0:T(8,128)(2,1)S(1)} %copy-done.1, bf16[48,2048]{1,0:T(8,128)(2,1)S(1)} %copy-done.2, f32[2048,256]{1,0:T(8,128)S(1)} %collective-permute-done.refs_0_.refs_2_, f32[40,2048]{1,0:T(8,128)S(1)} %collective-permute-done.1.refs_1_.refs_3_, f32[528,256]{1,0:T(8,128)S(1)} %hist.11.refs_4_), custom_call_target="tpu_custom_call" | custom-call | flops 1048576 | bytes 1048576 | tf_op jit(solution)/shard_map/hist/pallas_call | solution.py:263
  32.8 1.6 %collective-permute-done.2.refs_4_ = f32[528,256]{1,0:T(8,128)S(1)} collective-permute-done((f32[528,256]{1,0:T(8,128)S(1)}, f32[528,256]{1,0:T(8,128)S(1)}, u32[]{:S(2)}, u32[]{:S(2)}) %collective-permute-start.2) | collective-permute-done | bytes 540704 | tf_op jit(solution)/shard_map/ppermute | solution.py:537
  34.4 4.8 %hist.13.refs_5_ = f32[528,256]{1,0:T(8,128)S(1)} custom-call(bf16[2048,256]{1,0:T(8,128)(2,1)S(1)} %copy-done.1, bf16[48,2048]{1,0:T(8,128)(2,1)S(1)} %copy-done.2, f32[2048,256]{1,0:T(8,128)S(1)} %collective-permute-done.refs_0_.refs_2_, f32[40,2048]{1,0:T(8,128)S(1)} %collective-permute-done.1.refs_1_.refs_3_, ...), custom_call_target="tpu_custom_call" | custom-call | flops 1048576 | bytes 1048576 | tf_op jit(solution)/shard_map/hist/pallas_call | solution.py:263
  39.3 4.4 %collective-permute-start.3 = (f32[528,256]{1,0:T(8,128)S(1)}, f32[528,256]{1,0:T(8,128)S(1)}, u32[]{:S(2)}, u32[]{:S(2)}) collective-permute-start(f32[528,256]{1,0:T(8,128)S(1)} %hist.13.refs_5_), channel_id=1, source_target_pairs={{0,4},{12,8},{1,5},{13,9},{2,6},{14,10},{3,7},{15,11},{16,20},{28,... | collective-permute-start | bytes 1622024 | tf_op jit(solution)/shard_map/ppermute | solution.py:542
  44.5 1.5 %collective-permute-done.4.refs_4_ = f32[528,256]{1,0:T(8,128)S(1)} collective-permute-done((f32[528,256]{1,0:T(8,128)S(1)}, f32[528,256]{1,0:T(8,128)S(1)}, u32[]{:S(2)}, u32[]{:S(2)}) %collective-permute-start.4) | collective-permute-done | bytes 540704 | tf_op jit(solution)/shard_map/ppermute | solution.py:537
  46.0 4.8 %hist.14.refs_5_ = f32[528,256]{1,0:T(8,128)S(1)} custom-call(bf16[2048,256]{1,0:T(8,128)(2,1)S(1)} %copy-done.1, bf16[48,2048]{1,0:T(8,128)(2,1)S(1)} %copy-done.2, f32[2048,256]{1,0:T(8,128)S(1)} %collective-permute-done.refs_0_.refs_2_, f32[40,2048]{1,0:T(8,128)S(1)} %collective-permute-done.1.refs_1_.refs_3_, ...), custom_call_target="tpu_custom_call" | custom-call | flops 1048576 | bytes 1048576 | tf_op jit(solution)/shard_map/hist/pallas_call | solution.py:263
  50.9 4.4 %collective-permute-start.8 = (f32[528,256]{1,0:T(8,128)S(1)}, f32[528,256]{1,0:T(8,128)S(1)}, u32[]{:S(2)}, u32[]{:S(2)}) collective-permute-start(f32[528,256]{1,0:T(8,128)S(1)} %hist.14.refs_5_), channel_id=1, source_target_pairs={{0,4},{12,8},{1,5},{13,9},{2,6},{14,10},{3,7},{15,11},{16,20},{28,... | collective-permute-start | bytes 1622024 | tf_op jit(solution)/shard_map/ppermute | solution.py:542
  56.1 1.5 %collective-permute-done.3.refs_4_ = f32[528,256]{1,0:T(8,128)S(1)} collective-permute-done((f32[528,256]{1,0:T(8,128)S(1)}, f32[528,256]{1,0:T(8,128)S(1)}, u32[]{:S(2)}, u32[]{:S(2)}) %collective-permute-start.3) | collective-permute-done | bytes 540704 | tf_op jit(solution)/shard_map/ppermute | solution.py:542
  58.4 4.8 %hist.15.tie_ref.refs_5_ = f32[528,256]{1,0:T(8,128)S(1)} custom-call(bf16[2048,256]{1,0:T(8,128)(2,1)S(1)} %copy-done.1, bf16[48,2048]{1,0:T(8,128)(2,1)S(1)} %copy-done.2, f32[2048,256]{1,0:T(8,128)S(1)} %collective-permute-done.refs_0_.refs_2_, f32[40,2048]{1,0:T(8,128)S(1)} %collective-permute-done.1.refs_1_.refs_3_, ...), custom_call_target="tpu_custom_call" | custom-call | flops 1048576 | bytes 1048576 | tf_op jit(solution)/shard_map/hist/pallas_call | solution.py:263
  63.3 5.0 %collective-permute-start.6 = (f32[528,256]{1,0:T(8,128)S(1)}, f32[528,256]{1,0:T(8,128)S(1)}, u32[]{:S(2)}, u32[]{:S(2)}) collective-permute-start(f32[528,256]{1,0:T(8,128)S(1)} %add.19), channel_id=1, source_target_pairs={{0,4},{4,0},{8,12},{12,8},{1,5},{5,1},{9,13},{13,9},{2,6},{6,2},{1... | collective-permute-start | bytes 1622024 | tf_op jit(solution)/shard_map/ppermute | solution.py:546
  70.2 4.8 %hist.16.refs_4_ = f32[528,256]{1,0:T(8,128)S(1)} custom-call(bf16[2048,256]{1,0:T(8,128)(2,1)S(1)} %copy-done.1, bf16[48,2048]{1,0:T(8,128)(2,1)S(1)} %copy-done.2, f32[2048,256]{1,0:T(8,128)S(1)} %collective-permute-done.refs_0_.refs_2_, f32[40,2048]{1,0:T(8,128)S(1)} %collective-permute-done.1.refs_1_.refs_3_, ...), custom_call_target="tpu_custom_call" | custom-call | flops 1048576 | bytes 1048576 | tf_op jit(solution)/shard_map/hist/pallas_call | solution.py:263
  75.1 5.0 %collective-permute-start.10 = (f32[528,256]{1,0:T(8,128)S(1)}, f32[528,256]{1,0:T(8,128)S(1)}, u32[]{:S(2)}, u32[]{:S(2)}) collective-permute-start(f32[528,256]{1,0:T(8,128)S(1)} %add.22), channel_id=1, source_target_pairs={{0,4},{4,0},{8,12},{12,8},{1,5},{5,1},{9,13},{13,9},{2,6},{6,2},{1... | collective-permute-start | bytes 1622024 | tf_op jit(solution)/shard_map/ppermute | solution.py:546
  81.4 4.9 %hist.17.tie_ref.last_ref = f32[528,256]{1,0:T(8,128)S(1)} custom-call(bf16[2048,256]{1,0:T(8,128)(2,1)S(1)} %copy-done.1, bf16[48,2048]{1,0:T(8,128)(2,1)S(1)} %copy-done.2, f32[2048,256]{1,0:T(8,128)S(1)} %collective-permute-done.refs_0_.refs_2_, f32[40,2048]{1,0:T(8,128)S(1)} %collective-permute-done.1.refs_1_.refs_3_, f32[528,256]{1,0:T(8,128)S(1)} %hist.16.refs_4_), custom_call_target="tpu_custom_call" | custom-call | flops 1048576 | bytes 1048576 | tf_op jit(solution)/shard_map/hist/pallas_call | solution.py:263
  86.3 1.6 %gains.2 = f32[2,16,256]{2,1,0:T(8,128)S(1)} custom-call(f32[528,256]{1,0:T(8,128)S(1)} %hist.12.refs_5_.last_ref, f32[528,256]{1,0:T(8,128)S(1)} %collective-permute-done.6.right_ref, f32[528,256]{1,0:T(8,128)S(1)} %collective-permute-done.7.left_ref, f32[512,256]{1,0:T(8,128)S(1)} %get-tuple-element.21.par_grad_ref, ...), custom_call_target="tpu_custom_call" | custom-call | flops 6553600 | bytes 2097152 | tf_op jit(solution)/shard_map/gains/pallas_call | solution.py:435
  88.6 3.4 %all-to-all-start = ((f32[8,2,16,256]{3,2,1,0:T(8,128)}), f32[8,2,16,256]{3,2,1,0:T(8,128)S(1)}, u32[]{:S(2)}, u32[]{:S(2)}) async-start(f32[8,2,16,256]{3,2,1,0:T(8,128)} %broadcast_in_dim.6), calls=%async_computation | async-start | bytes 524288 | tf_op jit(solution)/shard_map/all_to_all | solution.py:592
  92.1 1.6 %gains.3 = f32[2,16,256]{2,1,0:T(8,128)S(1)} custom-call(f32[528,256]{1,0:T(8,128)S(1)} %hist.17.tie_ref.last_ref, f32[528,256]{1,0:T(8,128)S(1)} %collective-permute-done.10.right_ref, f32[528,256]{1,0:T(8,128)S(1)} %collective-permute-done.11.left_ref, f32[512,256]{1,0:T(8,128)S(1)} %get-tuple-element.24.par_grad_ref, ...), custom_call_target="tpu_custom_call" | custom-call | flops 6553600 | bytes 2097152 | tf_op jit(solution)/shard_map/gains/pallas_call | solution.py:435
  93.6 8.1 %all-to-all-done.refs_0_ = f32[8,2,16,256]{3,2,1,0:T(8,128)S(1)} async-done(((f32[8,2,16,256]{3,2,1,0:T(8,128)}), f32[8,2,16,256]{3,2,1,0:T(8,128)S(1)}, u32[]{:S(2)}, u32[]{:S(2)}) %all-to-all-start) | async-done | bytes 262176 | tf_op jit(solution)/shard_map/all_to_all | solution.py:592
  101.7 12.8 %all_to_all.10.refs_1_ = f32[8,2,16,256]{3,2,1,0:T(8,128)} all-to-all(f32[8,2,16,256]{3,2,1,0:T(8,128)S(1)} %broadcast_in_dim.7), channel_id=1, replica_groups=mesh['groups'=2,'dp'=4,'feat'=2,'sub'=2] {'dp','sub'}, dimensions={0} | all-to-all | bytes 524288 | tf_op jit(solution)/shard_map/all_to_all | solution.py:592
  114.5 1.9 %finish.1 = f32[64,2,128]{2,1,0:T(2,128)} custom-call(s32[8,256]{1,0:T(8,128)} %copy-done.5, f32[8,2,16,256]{3,2,1,0:T(8,128)} %copy-done.11, f32[8,2,16,256]{3,2,1,0:T(8,128)} %all_to_all.10.refs_1_), custom_call_target="tpu_custom_call" | custom-call | tf_op jit(solution)/shard_map/finish/pallas_call | solution.py:477
  (49 shorter events, 10.3 us)
Async XLA Ops:
  8.0 5.8 %collective-permute-start = (f32[2048,256]{1,0:T(8,128)}, f32[2048,256]{1,0:T(8,128)S(1)}, u32[]{:S(2)}, u32[]{:S(2)}) collective-permute-start(f32[2048,256]{1,0:T(8,128)} %get-tuple-element.18), channel_id=1, source_target_pairs={{0,1},{1,0},{2,3},{3,2},{4,5},{5,4},{6,7},{7,6},{8,9},{9,8},{10,11... | collective-permute-start | bytes 6291464 | tf_op jit(solution)/shard_map/ppermute | solution.py:566
  8.2 5.6 %collective-permute-start.1 = (f32[40,2048]{1,0:T(8,128)}, f32[40,2048]{1,0:T(8,128)S(1)}, u32[]{:S(2)}, u32[]{:S(2)}) collective-permute-start(f32[40,2048]{1,0:T(8,128)} %get-tuple-element.19), channel_id=1, source_target_pairs={{0,1},{1,0},{2,3},{3,2},{4,5},{5,4},{6,7},{7,6},{8,9},{9,8},{10,11... | collective-permute-start | bytes 983048 | tf_op jit(solution)/shard_map/ppermute | solution.py:565
  8.5 1.2 %copy-start = (bf16[2048,256]{1,0:T(8,128)(2,1)S(1)}, bf16[2048,256]{1,0:T(8,128)(2,1)}, u32[]{:S(2)}) copy-start(bf16[2048,256]{1,0:T(8,128)(2,1)} %get-tuple-element.16.refs_0_) | copy-start | bytes 3145732
  13.8 8.1 %copy-start.1 = (bf16[2048,256]{1,0:T(8,128)(2,1)S(1)}, bf16[2048,256]{1,0:T(8,128)(2,1)}, u32[]{:S(2)}) copy-start(bf16[2048,256]{1,0:T(8,128)(2,1)} %get-tuple-element.16.refs_0_) | copy-start | bytes 3145732
  16.9 17.6 %collective-permute-start.2 = (f32[528,256]{1,0:T(8,128)S(1)}, f32[528,256]{1,0:T(8,128)S(1)}, u32[]{:S(2)}, u32[]{:S(2)}) collective-permute-start(f32[528,256]{1,0:T(8,128)S(1)} %hist.10.refs_4_), channel_id=1, source_target_pairs={{0,4},{12,8},{1,5},{13,9},{2,6},{14,10},{3,7},{15,11},{16,20},{28,... | collective-permute-start | bytes 1622024 | tf_op jit(solution)/shard_map/ppermute | solution.py:537
  26.7 19.3 %collective-permute-start.4 = (f32[528,256]{1,0:T(8,128)S(1)}, f32[528,256]{1,0:T(8,128)S(1)}, u32[]{:S(2)}, u32[]{:S(2)}) collective-permute-start(f32[528,256]{1,0:T(8,128)S(1)} %hist.11.refs_4_), channel_id=1, source_target_pairs={{0,4},{12,8},{1,5},{13,9},{2,6},{14,10},{3,7},{15,11},{16,20},{28,... | collective-permute-start | bytes 1622024 | tf_op jit(solution)/shard_map/ppermute | solution.py:537
  39.3 18.3 %collective-permute-start.3 = (f32[528,256]{1,0:T(8,128)S(1)}, f32[528,256]{1,0:T(8,128)S(1)}, u32[]{:S(2)}, u32[]{:S(2)}) collective-permute-start(f32[528,256]{1,0:T(8,128)S(1)} %hist.13.refs_5_), channel_id=1, source_target_pairs={{0,4},{12,8},{1,5},{13,9},{2,6},{14,10},{3,7},{15,11},{16,20},{28,... | collective-permute-start | bytes 1622024 | tf_op jit(solution)/shard_map/ppermute | solution.py:542
  43.8 19.5 %collective-permute-start.5 = (f32[528,256]{1,0:T(8,128)S(1)}, f32[528,256]{1,0:T(8,128)S(1)}, u32[]{:S(2)}, u32[]{:S(2)}) collective-permute-start(f32[528,256]{1,0:T(8,128)S(1)} %add.18), channel_id=1, source_target_pairs={{4,8},{8,4},{5,9},{9,5},{6,10},{10,6},{7,11},{11,7},{20,24},{24,20... | collective-permute-start | bytes 1622024 | tf_op jit(solution)/shard_map/ppermute | solution.py:541
  50.9 18.3 %collective-permute-start.8 = (f32[528,256]{1,0:T(8,128)S(1)}, f32[528,256]{1,0:T(8,128)S(1)}, u32[]{:S(2)}, u32[]{:S(2)}) collective-permute-start(f32[528,256]{1,0:T(8,128)S(1)} %hist.14.refs_5_), channel_id=1, source_target_pairs={{0,4},{12,8},{1,5},{13,9},{2,6},{14,10},{3,7},{15,11},{16,20},{28,... | collective-permute-start | bytes 1622024 | tf_op jit(solution)/shard_map/ppermute | solution.py:542
  55.4 19.7 %collective-permute-start.9 = (f32[528,256]{1,0:T(8,128)S(1)}, f32[528,256]{1,0:T(8,128)S(1)}, u32[]{:S(2)}, u32[]{:S(2)}) collective-permute-start(f32[528,256]{1,0:T(8,128)S(1)} %add.21), channel_id=1, source_target_pairs={{4,8},{8,4},{5,9},{9,5},{6,10},{10,6},{7,11},{11,7},{20,24},{24,20... | collective-permute-start | bytes 1622024 | tf_op jit(solution)/shard_map/ppermute | solution.py:541
  57.7 28.6 %collective-permute-start.7 = (f32[528,256]{1,0:T(8,128)S(1)}, f32[528,256]{1,0:T(8,128)S(1)}, u32[]{:S(2)}, u32[]{:S(2)}) collective-permute-start(f32[528,256]{1,0:T(8,128)S(1)} %add.20), channel_id=1, source_target_pairs={{4,8},{8,4},{5,9},{9,5},{6,10},{10,6},{7,11},{11,7},{20,24},{24,20... | collective-permute-start | bytes 1622024 | tf_op jit(solution)/shard_map/ppermute | solution.py:545
  63.3 23.0 %collective-permute-start.6 = (f32[528,256]{1,0:T(8,128)S(1)}, f32[528,256]{1,0:T(8,128)S(1)}, u32[]{:S(2)}, u32[]{:S(2)}) collective-permute-start(f32[528,256]{1,0:T(8,128)S(1)} %add.19), channel_id=1, source_target_pairs={{0,4},{4,0},{8,12},{12,8},{1,5},{5,1},{9,13},{13,9},{2,6},{6,2},{1... | collective-permute-start | bytes 1622024 | tf_op jit(solution)/shard_map/ppermute | solution.py:546
  69.3 10.9 %copy-start.4 = (f32[1,64,128]{2,1,0:T(8,128)S(1)}, f32[1,64,128]{2,1,0:T(8,128)}, u32[]{:S(2)}) copy-start(f32[1,64,128]{2,1,0:T(8,128)} %param.19) | copy-start | bytes 98308
  69.3 10.9 %copy-start.6 = (s32[1024]{0:T(1024)S(1)}, s32[1024]{0:T(1024)}, u32[]{:S(2)}) copy-start(s32[1024]{0:T(1024)} %param.15) | copy-start | bytes 12292
  69.3 10.9 %copy-start.7 = (s32[8]{0:T(128)S(1)}, s32[8]{0:T(128)}, u32[]{:S(2)}) copy-start(s32[8]{0:T(128)} %child_ref.1) | copy-start | bytes 100
  69.3 10.9 %copy-start.8 = (s32[8]{0:T(128)S(1)}, s32[8]{0:T(128)}, u32[]{:S(2)}) copy-start(s32[8]{0:T(128)} %owner_ref.3) | copy-start | bytes 100
  69.3 10.8 %copy-start.9 = (s32[2]{0:T(128)S(1)}, s32[2]{0:T(128)}, u32[]{:S(2)}) copy-start(s32[2]{0:T(128)} %low_ref.1) | copy-start | bytes 28
  69.3 10.8 %copy-start.10 = (s32[2]{0:T(128)S(1)}, s32[2]{0:T(128)}, u32[]{:S(2)}) copy-start(s32[2]{0:T(128)} %high_ref.1) | copy-start | bytes 28
  69.3 22.7 %collective-permute-start.11 = (f32[528,256]{1,0:T(8,128)S(1)}, f32[528,256]{1,0:T(8,128)S(1)}, u32[]{:S(2)}, u32[]{:S(2)}) collective-permute-start(f32[528,256]{1,0:T(8,128)S(1)} %add.23), channel_id=1, source_target_pairs={{4,8},{8,4},{5,9},{9,5},{6,10},{10,6},{7,11},{11,7},{20,24},{24,20... | collective-permute-start | bytes 1622024 | tf_op jit(solution)/shard_map/ppermute | solution.py:545
  75.0 5.2 %copy-start.3 = (f32[1,64,4096]{2,1,0:T(8,128)S(1)}, f32[1,64,4096]{2,1,0:T(8,128)}, u32[]{:S(2)}) copy-start(f32[1,64,4096]{2,1,0:T(8,128)} %param.18) | copy-start | bytes 3145732
  75.1 16.9 %collective-permute-start.10 = (f32[528,256]{1,0:T(8,128)S(1)}, f32[528,256]{1,0:T(8,128)S(1)}, u32[]{:S(2)}, u32[]{:S(2)}) collective-permute-start(f32[528,256]{1,0:T(8,128)S(1)} %add.22), channel_id=1, source_target_pairs={{0,4},{4,0},{8,12},{12,8},{1,5},{5,1},{9,13},{13,9},{2,6},{6,2},{1... | collective-permute-start | bytes 1622024 | tf_op jit(solution)/shard_map/ppermute | solution.py:546
  81.4 4.9 %copy-start.5 = (s32[8,256]{1,0:T(8,128)}, s32[8,256]{1,0:T(8,128)S(1)}, u32[]{:S(2)}) copy-start(s32[8,256]{1,0:T(8,128)S(1)} %get-tuple-element.20.route_ref) | copy-start | bytes 24580
  88.6 13.1 %all-to-all-start = ((f32[8,2,16,256]{3,2,1,0:T(8,128)}), f32[8,2,16,256]{3,2,1,0:T(8,128)S(1)}, u32[]{:S(2)}, u32[]{:S(2)}) async-start(f32[8,2,16,256]{3,2,1,0:T(8,128)} %broadcast_in_dim.6), calls=%async_computation | async-start | bytes 524288 | tf_op jit(solution)/shard_map/all_to_all | solution.py:592
  101.7 12.8 %copy-start.11 = (f32[8,2,16,256]{3,2,1,0:T(8,128)}, f32[8,2,16,256]{3,2,1,0:T(8,128)S(1)}, u32[]{:S(2)}) copy-start(f32[8,2,16,256]{3,2,1,0:T(8,128)S(1)} %all-to-all-done.refs_0_) | copy-start | bytes 786436
  (1 other events, 0.9 us)

commit v5 on v4

--- a/solution.py
+++ b/solution.py
@@ -16,6 +16,23 @@
 MIB = 1024 * 1024
 VMEM_SPEC = pl.BlockSpec(memory_space=pltpu.VMEM)
 SMEM_SPEC = pl.BlockSpec(memory_space=pltpu.SMEM)
+
+
+def sum_after_kernel(x_ref, y_ref, tie_ref, out_ref):
+    del tie_ref
+    out_ref[...] = x_ref[...] + y_ref[...]
+
+
+def sum_after(x, y, tie):
+    return pl.pallas_call(
+        sum_after_kernel,
+        in_specs=[VMEM_SPEC] * 2 + [pl.BlockSpec(memory_space=pl.ANY)],
+        out_specs=VMEM_SPEC,
+        out_shape=jax.ShapeDtypeStruct(x.shape, jnp.float32),
+        compiler_params=pltpu.CompilerParams(vmem_limit_bytes=16 * MIB),
+        cost_estimate=pl.CostEstimate(flops=x.size, bytes_accessed=12 * x.size, transcendentals=0),
+        name="sum_after",
+    )(x, y, tie)
 
 
 def plan_of(line):
@@ -78,6 +95,8 @@
     source = source * slab + lax.rem(column, slab)
     perm = jnp.where(lax.broadcasted_iota(jnp.int32, (f_dev, f_dev), 0) == source, 1.0, 0.0).astype(jnp.bfloat16)
 
+    for copy in copies:
+        copy.wait()
     for i in range(blocks):
         part = slice(i * TILE, (i + 1) * TILE)
         goal = jnp.where(ones[i] > 0.5, ahead[i : i + 1] + (bases[i] - starts[i]), -1)
@@ -88,7 +107,6 @@
         packed_w = lax.dot_general(weights.astype(jnp.bfloat16), pack, (((1,), (1,)), ((), ())), preferred_element_type=jnp.float32)
         acc_w_ref[:, pl.ds(starts[i], PACK)] += packed_w[:, :PACK]
         acc_w_ref[:, pl.ds(starts[i] + PACK, TILE)] = packed_w[:, PACK:]
-        copies[i].wait()
         binned = buf_ref[part, :].astype(jnp.float32).astype(jnp.bfloat16)
         packed = jnp.dot(pack, binned, preferred_element_type=jnp.float32).astype(jnp.bfloat16)
         acc_ref[pl.ds(starts[i], PACK), :] += packed[:PACK]
@@ -303,8 +321,11 @@
     owners = owner_ref.shape[0]
     z, core = lax.axis_index("dp"), lax.axis_index("sub")
     place = 2 * z + core
-    route_ref = out_refs[-1]
-    route_ref[...] = jnp.full(route_ref.shape, source_of(place, child_ref, owner_ref), jnp.int32)
+    mine = source_of(place, child_ref, owner_ref)
+    twin = source_of(2 * z + 1 - core, child_ref, owner_ref)
+    row = lax.broadcasted_iota(jnp.int32, (8, lanes), 0)
+    route = jnp.where(row == 0, (mine // 2) ^ z, (twin // 2) ^ z)
+    out_refs[-1][...] = jnp.where(row == 2, jnp.where(lax.rem(mine, 2) == core, 1, 0), route)
     slab_at = jnp.int32(0)
     for q in range(owners):
         slab_at = jnp.where(owner_ref[q] == place, q, slab_at)
@@ -447,19 +468,25 @@
     )(last, right, left, par_grad, par_hess, bounds, tie)
 
 
-def finish_kernel(width, route_ref, *refs):
+def chosen(shift, got):
+    value = got[0]
+    for s in range(1, len(got)):
+        value = jnp.where(shift == s, got[s], value)
+    return value
+
+
+def finish_kernel(width, line, route_ref, *refs):
     out_ref = refs[-1]
-    chunks = len(refs) - 1
+    chunks = (len(refs) - 1) // (line + 1)
     slab = width * chunks
     lanes = route_ref.shape[1]
-    source = route_ref[:1, :]
+    shift, same = route_ref[:1, :], route_ref[2:3, :]
     total = jnp.zeros((128, 128), jnp.float32)
     column = lax.broadcasted_iota(jnp.int32, (128, 128), 1)
     for child in range(2):
         for c in range(chunks):
-            gain = refs[c][0, child]
-            for s in range(1, refs[c].shape[0]):
-                gain = jnp.where(source == s, refs[c][s, child], gain)
+            got = [ref[child] for ref in refs[c * (line + 1) : (c + 1) * (line + 1)]]
+            gain = jnp.where(same == 1, chosen(shift, got[:line]), got[line])
             at = child * slab + c * width
             pieces = []
             for j in range(lanes // width):
@@ -473,14 +500,15 @@
         out_ref[:, child, :] = turned[child * slab : (child + 1) * slab]
 
 
-def finish(width, nbins, route, parts):
+def finish(width, nbins, line, route, parts):
+    flat = [x for part in parts for x in part]
     return pl.pallas_call(
-        functools.partial(finish_kernel, width),
-        in_specs=[VMEM_SPEC] * (1 + len(parts)),
+        functools.partial(finish_kernel, width, line),
+        in_specs=[VMEM_SPEC] * (1 + len(flat)),
         out_specs=VMEM_SPEC,
         out_shape=jax.ShapeDtypeStruct((width * len(parts), 2, nbins), jnp.float32),
         name="finish",
-    )(route, *parts)
+    )(route, *flat)
 
 
 def one_of(z, members):
@@ -533,21 +561,21 @@
 def sum_line_of_4(line, chunks, units, unit, set_up):
     inward, outer, middle = [(0, 1), (3, 2)], [(0, 1), (1, 0), (2, 3), (3, 2)], [(1, 2), (2, 1)]
     a0, a1, a2, b1, b2, last = {}, {}, {}, {}, {}, {}
+    final = chunks - 1
     for c in range(chunks):
         a0[c] = lax.ppermute(units[0, c], "dp", inward)
-    last[0] = unit(3, 0, (units[0, chunks - 1],))
     for c in range(chunks):
-        units[1, c] = unit(1, c, (a0[c], units[1, c - 1] if c else last[0]))
-        b1[c] = lax.ppermute(units[0, c] + a0[c], "dp", middle)
+        units[1, c] = unit(1, c, (units[1, c - 1] if c else units[0, final],))
         a1[c] = lax.ppermute(units[1, c], "dp", inward)
+        b1[c] = lax.ppermute(sum_after(units[0, c], a0[c], units[1, c]), "dp", middle)
     for c in range(chunks):
-        units[2, c] = unit(2, c, (a1[c], units[2, c - 1] if c else units[1, chunks - 1]))
-        b2[c] = lax.ppermute(units[1, c] + a1[c], "dp", middle)
+        units[2, c] = unit(2, c, (units[2, c - 1], b1[c - 1], a1[c - 1]) if c else (units[1, final], a0[final]))
         a2[c] = lax.ppermute(units[2, c] + b1[c], "dp", outer)
-    layout = set_up(units[2, 0])
-    for c in range(1, chunks):
-        last[c] = unit(3, c, (units[2, chunks - 1],))
-    return last, a2, b2, layout
+    for c in range(chunks):
+        last[c] = unit(3, c, (last[c - 1], a1[c]) if c else (units[2, final], b1[final]))
+    for c in range(chunks):
+        b2[c] = lax.ppermute(sum_after(units[1, c], a1[c], last[c - 1] if c else units[2, c]), "dp", middle)
+    return last, a2, b2, set_up(last[final])
 
 
 def per_device(bins, grads, hess, node_side, signs, child_owner, parent_owner, parent_grad, parent_hess, node_low, node_high):
@@ -588,9 +616,10 @@
         gain = gains_of(
             width, levels, lanes, kdim, last[c], from_left[c], from_right[c], par_grad[c], par_hess[c], bounds[c], last[chunks - 1]
         )
-        everyone = jnp.broadcast_to(gain[None], (2 * line, *gain.shape))
-        done.append(lax.all_to_all(everyone, ("dp", "sub"), 0, 0))
-    return finish(width, nbins, route, done)[None]
+        got = [gain] + [lax.ppermute(gain, "dp", [(i, i ^ s) for i in range(line)]) for s in range(1, line)]
+        crossed = lax.ppermute(chosen(route[1, 0], got), "sub", swap)
+        done.append([*got, crossed])
+    return finish(width, nbins, line, route, done)[None]
 
 
 def solution(mesh):

time: 117 us -> 106 us (0.906)
  blocking collectives: 12.8 us -> 0 us
  between operations: 0.4 us -> 2.49 us
    all_to_all x1 -> x0, blocking collectives: 12.8 us -> none  [per_device(): done.append(lax.all_to_all(everyone, ('dp', 'sub'), 0, 0))]
    ppermute x4 -> x12, starting transfers between devices: 2.91 us -> 12.9 us  [the longest x6 9.81 us: per_device(): lax.ppermute(gain, 'dp', [(i, i ^ s) for i in range(line)])]
    all_to_all x1 -> x0, waiting for transfers between devices: 8.06 us -> none  [per_device(): done.append(lax.all_to_all(everyone, ('dp', 'sub'), 0, 0))]
    ppermute x2, starting transfers between devices: 10.1 us -> 4.17 us  [sum_line_of_4(): a2[c] = lax.ppermute(units[2, c] + b1[c], 'dp', outer)]
    ppermute x4 -> x12, waiting for transfers between devices: 0.01 us -> 4.57 us  [the longest x6 3.39 us: per_device(): lax.ppermute(gain, 'dp', [(i, i ^ s) for i in range(line)])]
    all_to_all x1 -> x0, starting transfers between devices: 3.41 us -> none  [per_device(): done.append(lax.all_to_all(everyone, ('dp', 'sub'), 0, 0))]
    ppermute x2, waiting for transfers between devices: 3.13 us -> 6.24 us  [sum_line_of_4(): a0[c] = lax.ppermute(units[0, c], 'dp', inward)]
    ppermute x2, waiting for transfers between devices: 2.39 us -> 0.01 us  [sum_line_of_4(): a1[c] = lax.ppermute(units[1, c], 'dp', inward)]
  transfers between devices with their start and end apart: 13 -> 20, of which waited for: 5 -> 7; matrix products, arithmetic and copies ran while one was open for 1% -> 1% of each run, Pallas kernels for 35% -> 39%
where the time goes in v5:
time: 106 us; the launch traced here: 105 us
  Pallas kernels  53.9 us (51%)
  starting transfers between devices  32.7 us (31%)
  waiting for transfers between devices  12.7 us (12%)
  local copies, waits for them, and re-layouts  3.36 us (3%)
  between operations  2.49 us (2%)
    pallas_call x9, Pallas kernels, hist(): pl.pallas_call(functools.partial(hist_kernel, first_column, width, levels...  40 us
    ppermute x6, starting transfers between devices, per_device(): lax.ppermute(gain, 'dp', [(i, i ^ s) for i in range(line)])  9.81 us
    ppermute x2, starting transfers between devices, sum_line_of_4(): a1[c] = lax.ppermute(units[1, c], 'dp', inward)  8.84 us
    pallas_call x1, Pallas kernels, prep(): pl.pallas_call(functools.partial(prep_kernel, line, slab), in_specs=[SMEM...  7.55 us
    ppermute x2, starting transfers between devices, sum_line_of_4(): a0[c] = lax.ppermute(units[0, c], 'dp', inward)  6.25 us
    ppermute x2, waiting for transfers between devices, sum_line_of_4(): a0[c] = lax.ppermute(units[0, c], 'dp', inward)  6.24 us
    ppermute x2, starting transfers between devices, sum_line_of_4(): a2[c] = lax.ppermute(units[2, c] + b1[c], 'dp', outer)  4.17 us
    ppermute x6, waiting for transfers between devices, per_device(): lax.ppermute(gain, 'dp', [(i, i ^ s) for i in range(line)])  3.39 us
  transfers between devices with their start and end apart: 20, of which 7 were waited for; matrix products, arithmetic and copies ran while one was open for 1% of the time, Pallas kernels for 39%

profile of v5, /device:TPU:0, one launch (start us, length us, event | category | flops | bytes accessed | tf_op | source)
XLA Modules:
  0.0 105.3 jit_solution(6032933691841276093)
XLA Ops:
  0.0 7.6 %prep.1 = (bf16[2048,256]{1,0:T(8,128)(2,1)}, f32[2048,256]{1,0:T(8,128)}, bf16[48,2048]{1,0:T(8,128)(2,1)}, f32[40,2048]{1,0:T(8,128)}) custom-call(s32[8]{0:T(128)} %owner_ref.3, s32[2048,512]{1,0:T(8,128)} %bins_ref.1, bf16[32,2048]{1,0:T(8,128)(2,1)} %bitcast.12, bf16[2048]{0:T(1024)(128)(2,1)} %hess_ref.1, s32[1,2048]{1,0:T(1,128)} %bitcast.13), custom_call_target="tpu_custom_call" | custom-call | flops 2147483648 | bytes 8388608 | tf_op jit(solution)/shard_map/prep/pallas_call | solution.py:147
  10.3 3.1 %hist.9.refs_2_ = f32[528,256]{1,0:T(8,128)S(1)} custom-call(bf16[2048,256]{1,0:T(8,128)(2,1)S(1)} %copy-done, bf16[48,2048]{1,0:T(8,128)(2,1)S(1)} %copy-done.2), custom_call_target="tpu_custom_call" | custom-call | flops 524288 | bytes 524288 | tf_op jit(solution)/shard_map/hist/pallas_call | solution.py:281
  13.4 3.1 %hist.10.refs_4_.x_ref = f32[528,256]{1,0:T(8,128)S(1)} custom-call(f32[2048,256]{1,0:T(8,128)S(1)} %collective-permute-done.refs_0_.refs_2_, f32[40,2048]{1,0:T(8,128)S(1)} %collective-permute-done.1.refs_1_.refs_3_, f32[528,256]{1,0:T(8,128)S(1)} %hist.9.refs_2_), custom_call_target="tpu_custom_call" | custom-call | flops 524288 | bytes 524288 | tf_op jit(solution)/shard_map/hist/pallas_call | solution.py:281
  16.5 4.9 %collective-permute-start.3 = (f32[528,256]{1,0:T(8,128)S(1)}, f32[528,256]{1,0:T(8,128)S(1)}, u32[]{:S(2)}, u32[]{:S(2)}) collective-permute-start(f32[528,256]{1,0:T(8,128)S(1)} %hist.10.refs_4_.x_ref), channel_id=1, source_target_pairs={{0,4},{12,8},{1,5},{13,9},{2,6},{14,10},{3,7},{15,11},{16,20},{28,... | collective-permute-start | bytes 1622024 | tf_op jit(solution)/shard_map/ppermute | solution.py:566
  21.5 4.8 %hist.11.refs_4_.x_ref = f32[528,256]{1,0:T(8,128)S(1)} custom-call(bf16[2048,256]{1,0:T(8,128)(2,1)S(1)} %copy-done.1, bf16[48,2048]{1,0:T(8,128)(2,1)S(1)} %copy-done.2, f32[2048,256]{1,0:T(8,128)S(1)} %collective-permute-done.refs_0_.refs_2_, f32[40,2048]{1,0:T(8,128)S(1)} %collective-permute-done.1.refs_1_.refs_3_, f32[528,256]{1,0:T(8,128)S(1)} %hist.10.refs_4_.x_ref), custom_call_target="tpu_custom_call" | custom-call | flops 1048576 | bytes 1048576 | tf_op jit(solution)/shard_map/hist/pallas_call | solution.py:281
  26.3 1.3 %collective-permute-start.2 = (f32[528,256]{1,0:T(8,128)S(1)}, f32[528,256]{1,0:T(8,128)S(1)}, u32[]{:S(2)}, u32[]{:S(2)}) collective-permute-start(f32[528,256]{1,0:T(8,128)S(1)} %hist.11.refs_4_.x_ref), channel_id=1, source_target_pairs={{0,4},{12,8},{1,5},{13,9},{2,6},{14,10},{3,7},{15,11},{16,20},{28,... | collective-permute-start | bytes 1622024 | tf_op jit(solution)/shard_map/ppermute | solution.py:566
  27.6 4.8 %hist.12.refs_4_.tie_ref.x_ref = f32[528,256]{1,0:T(8,128)S(1)} custom-call(bf16[2048,256]{1,0:T(8,128)(2,1)S(1)} %copy-done.1, bf16[48,2048]{1,0:T(8,128)(2,1)S(1)} %copy-done.2, f32[2048,256]{1,0:T(8,128)S(1)} %collective-permute-done.refs_0_.refs_2_, f32[40,2048]{1,0:T(8,128)S(1)} %collective-permute-done.1.refs_1_.refs_3_, f32[528,256]{1,0:T(8,128)S(1)} %hist.11.refs_4_.x_ref), custom_call_target="tpu_custom_call" | custom-call | flops 1048576 | bytes 1048576 | tf_op jit(solution)/shard_map/hist/pallas_call | solution.py:281
  34.8 4.8 %hist.13.refs_4_.tie_ref.x_ref = f32[528,256]{1,0:T(8,128)S(1)} custom-call(bf16[2048,256]{1,0:T(8,128)(2,1)S(1)} %copy-done.1, bf16[48,2048]{1,0:T(8,128)(2,1)S(1)} %copy-done.2, f32[2048,256]{1,0:T(8,128)S(1)} %collective-permute-done.refs_0_.refs_2_, f32[40,2048]{1,0:T(8,128)S(1)} %collective-permute-done.1.refs_1_.refs_3_, ...), custom_call_target="tpu_custom_call" | custom-call | flops 1048576 | bytes 1048576 | tf_op jit(solution)/shard_map/hist/pallas_call | solution.py:281
  39.6 6.0 %collective-permute-done.2.refs_5_.y_ref = f32[528,256]{1,0:T(8,128)S(1)} collective-permute-done((f32[528,256]{1,0:T(8,128)S(1)}, f32[528,256]{1,0:T(8,128)S(1)}, u32[]{:S(2)}, u32[]{:S(2)}) %collective-permute-start.2) | collective-permute-done | bytes 540704 | tf_op jit(solution)/shard_map/ppermute | solution.py:566
  46.4 7.5 %collective-permute-start.7 = (f32[528,256]{1,0:T(8,128)S(1)}, f32[528,256]{1,0:T(8,128)S(1)}, u32[]{:S(2)}, u32[]{:S(2)}) collective-permute-start(f32[528,256]{1,0:T(8,128)S(1)} %hist.13.refs_4_.tie_ref.x_ref), channel_id=1, source_target_pairs={{0,4},{12,8},{1,5},{13,9},{2,6},{14,10},{3,7},{15,11},{16,20},{28,... | collective-permute-start | bytes 1622024 | tf_op jit(solution)/shard_map/ppermute | solution.py:569
  53.9 4.8 %hist.14.refs_4_.tie_ref = f32[528,256]{1,0:T(8,128)S(1)} custom-call(bf16[2048,256]{1,0:T(8,128)(2,1)S(1)} %copy-done.1, bf16[48,2048]{1,0:T(8,128)(2,1)S(1)} %copy-done.2, f32[2048,256]{1,0:T(8,128)S(1)} %collective-permute-done.refs_0_.refs_2_, f32[40,2048]{1,0:T(8,128)S(1)} %collective-permute-done.1.refs_1_.refs_3_, ...), custom_call_target="tpu_custom_call" | custom-call | flops 1048576 | bytes 1048576 | tf_op jit(solution)/shard_map/hist/pallas_call | solution.py:281
  59.6 4.1 %collective-permute-start.8 = (f32[528,256]{1,0:T(8,128)S(1)}, f32[528,256]{1,0:T(8,128)S(1)}, u32[]{:S(2)}, u32[]{:S(2)}) collective-permute-start(f32[528,256]{1,0:T(8,128)S(1)} %add.6), channel_id=1, source_target_pairs={{0,4},{4,0},{8,12},{12,8},{1,5},{5,1},{9,13},{13,9},{2,6},{6,2},{1... | collective-permute-start | bytes 1622024 | tf_op jit(solution)/shard_map/ppermute | solution.py:573
  63.7 4.8 %hist.15.refs_4_ = f32[528,256]{1,0:T(8,128)S(1)} custom-call(bf16[2048,256]{1,0:T(8,128)(2,1)S(1)} %copy-done.1, bf16[48,2048]{1,0:T(8,128)(2,1)S(1)} %copy-done.2, f32[2048,256]{1,0:T(8,128)S(1)} %collective-permute-done.refs_0_.refs_2_, f32[40,2048]{1,0:T(8,128)S(1)} %collective-permute-done.1.refs_1_.refs_3_, f32[528,256]{1,0:T(8,128)S(1)} %hist.14.refs_4_.tie_ref, ...), custom_call_target="tpu_custom_call" | custom-call | flops 1048576 | bytes 1048576 | tf_op jit(solution)/shard_map/hist/pallas_call | solution.py:281
  68.7 4.8 %hist.16.refs_4_.last_ref.tie_ref = f32[528,256]{1,0:T(8,128)S(1)} custom-call(bf16[2048,256]{1,0:T(8,128)(2,1)S(1)} %copy-done.1, bf16[48,2048]{1,0:T(8,128)(2,1)S(1)} %copy-done.2, f32[2048,256]{1,0:T(8,128)S(1)} %collective-permute-done.refs_0_.refs_2_, f32[40,2048]{1,0:T(8,128)S(1)} %collective-permute-done.1.refs_1_.refs_3_, ...), custom_call_target="tpu_custom_call" | custom-call | flops 1048576 | bytes 1048576 | tf_op jit(solution)/shard_map/hist/pallas_call | solution.py:281
  74.6 4.8 %hist.17.tie_ref.last_ref = f32[528,256]{1,0:T(8,128)S(1)} custom-call(bf16[2048,256]{1,0:T(8,128)(2,1)S(1)} %copy-done.1, bf16[48,2048]{1,0:T(8,128)(2,1)S(1)} %copy-done.2, f32[2048,256]{1,0:T(8,128)S(1)} %collective-permute-done.refs_0_.refs_2_, f32[40,2048]{1,0:T(8,128)S(1)} %collective-permute-done.1.refs_1_.refs_3_, ...), custom_call_target="tpu_custom_call" | custom-call | flops 1048576 | bytes 1048576 | tf_op jit(solution)/shard_map/hist/pallas_call | solution.py:281
  80.8 1.6 %gains.2.refs_0_ = f32[2,16,256]{2,1,0:T(8,128)S(1)} custom-call(f32[528,256]{1,0:T(8,128)S(1)} %hist.16.refs_4_.last_ref.tie_ref, f32[528,256]{1,0:T(8,128)S(1)} %collective-permute-done.8.right_ref, f32[528,256]{1,0:T(8,128)S(1)} %collective-permute-done.9.left_ref, f32[512,256]{1,0:T(8,128)S(1)} %get-tuple-element.21.par_grad_ref, ...), custom_call_target="tpu_custom_call" | custom-call | flops 6553600 | bytes 2097152 | tf_op jit(solution)/shard_map/gains/pallas_call | solution.py:456
  82.3 2.5 %collective-permute-start.12 = (f32[2,16,256]{2,1,0:T(8,128)S(1)}, f32[2,16,256]{2,1,0:T(8,128)S(1)}, u32[]{:S(2)}, u32[]{:S(2)}) collective-permute-start(f32[2,16,256]{2,1,0:T(8,128)S(1)} %gains.2.refs_0_), channel_id=1, source_target_pairs={{0,12},{4,8},{8,4},{12,0},{1,13},{5,9},{9,5},{13,1},{2,14},{6,10},... | collective-permute-start | bytes 98312 | tf_op jit(solution)/shard_map/ppermute | solution.py:619
  84.8 2.4 %collective-permute-start.11 = (f32[2,16,256]{2,1,0:T(8,128)S(1)}, f32[2,16,256]{2,1,0:T(8,128)S(1)}, u32[]{:S(2)}, u32[]{:S(2)}) collective-permute-start(f32[2,16,256]{2,1,0:T(8,128)S(1)} %gains.2.refs_0_), channel_id=1, source_target_pairs={{0,8},{4,12},{8,0},{12,4},{1,9},{5,13},{9,1},{13,5},{2,10},{6,14},... | collective-permute-start | bytes 98312 | tf_op jit(solution)/shard_map/ppermute | solution.py:619
  90.1 1.8 %collective-permute-done.14.right_ref = f32[528,256]{1,0:T(8,128)S(1)} collective-permute-done((f32[528,256]{1,0:T(8,128)S(1)}, f32[528,256]{1,0:T(8,128)S(1)}, u32[]{:S(2)}, u32[]{:S(2)}) %collective-permute-start.14) | collective-permute-done | bytes 540704 | tf_op jit(solution)/shard_map/ppermute | solution.py:573
  92.0 1.6 %gains.3.refs_5_ = f32[2,16,256]{2,1,0:T(8,128)S(1)} custom-call(f32[528,256]{1,0:T(8,128)S(1)} %hist.17.tie_ref.last_ref, f32[528,256]{1,0:T(8,128)S(1)} %collective-permute-done.14.right_ref, f32[528,256]{1,0:T(8,128)S(1)} %collective-permute-done.15.left_ref, f32[512,256]{1,0:T(8,128)S(1)} %get-tuple-element.24.par_grad_ref, ...), custom_call_target="tpu_custom_call" | custom-call | flops 6553600 | bytes 2097152 | tf_op jit(solution)/shard_map/gains/pallas_call | solution.py:456
  93.6 2.8 %collective-permute-start.18 = (f32[2,16,256]{2,1,0:T(8,128)S(1)}, f32[2,16,256]{2,1,0:T(8,128)S(1)}, u32[]{:S(2)}, u32[]{:S(2)}) collective-permute-start(f32[2,16,256]{2,1,0:T(8,128)S(1)} %gains.3.refs_5_), channel_id=1, source_target_pairs={{0,12},{4,8},{8,4},{12,0},{1,13},{5,9},{9,5},{13,1},{2,14},{6,10},... | collective-permute-start | bytes 98312 | tf_op jit(solution)/shard_map/ppermute | solution.py:619
  98.2 1.5 %collective-permute-done.18.refs_8_ = f32[2,16,256]{2,1,0:T(8,128)S(1)} collective-permute-done((f32[2,16,256]{2,1,0:T(8,128)S(1)}, f32[2,16,256]{2,1,0:T(8,128)S(1)}, u32[]{:S(2)}, u32[]{:S(2)}) %collective-permute-start.18) | collective-permute-done | bytes 32800 | tf_op jit(solution)/shard_map/ppermute | solution.py:619
  99.7 1.5 %collective-permute-done.17.refs_7_ = f32[2,16,256]{2,1,0:T(8,128)S(1)} collective-permute-done((f32[2,16,256]{2,1,0:T(8,128)S(1)}, f32[2,16,256]{2,1,0:T(8,128)S(1)}, u32[]{:S(2)}, u32[]{:S(2)}) %collective-permute-start.17) | collective-permute-done | bytes 32800 | tf_op jit(solution)/shard_map/ppermute | solution.py:619
  103.6 1.8 %finish.1 = f32[64,2,128]{2,1,0:T(2,128)} custom-call(s32[8,256]{1,0:T(8,128)} %copy-done.7, f32[2,16,256]{2,1,0:T(8,128)} %copy-done.4, f32[2,16,256]{2,1,0:T(8,128)} %copy-done.15, f32[2,16,256]{2,1,0:T(8,128)} %copy-done.14, f32[2,16,256]{2,1,0:T(8,128)} %copy-done.13, f32[2,16,256]{2,1,0:T(8,128)} %copy-done.19, f32[2,16,256]{2,1,0:T(8,128)} %copy-done.5, ...), custom_call_target="tpu_custom_call" | custom-call | tf_op jit(solution)/shard_map/finish/pallas_call | solution.py:505
  (81 shorter events, 13.9 us)
Async XLA Ops:
  7.6 5.9 %collective-permute-start = (f32[2048,256]{1,0:T(8,128)}, f32[2048,256]{1,0:T(8,128)S(1)}, u32[]{:S(2)}, u32[]{:S(2)}) collective-permute-start(f32[2048,256]{1,0:T(8,128)} %get-tuple-element.18), channel_id=1, source_target_pairs={{0,1},{1,0},{2,3},{3,2},{4,5},{5,4},{6,7},{7,6},{8,9},{9,8},{10,11... | collective-permute-start | bytes 6291464 | tf_op jit(solution)/shard_map/ppermute | solution.py:594
  8.1 5.3 %collective-permute-start.1 = (f32[40,2048]{1,0:T(8,128)}, f32[40,2048]{1,0:T(8,128)S(1)}, u32[]{:S(2)}, u32[]{:S(2)}) collective-permute-start(f32[40,2048]{1,0:T(8,128)} %get-tuple-element.19), channel_id=1, source_target_pairs={{0,1},{1,0},{2,3},{3,2},{4,5},{5,4},{6,7},{7,6},{8,9},{9,8},{10,11... | collective-permute-start | bytes 983048 | tf_op jit(solution)/shard_map/ppermute | solution.py:593
  13.4 8.1 %copy-start.1 = (bf16[2048,256]{1,0:T(8,128)(2,1)S(1)}, bf16[2048,256]{1,0:T(8,128)(2,1)}, u32[]{:S(2)}) copy-start(bf16[2048,256]{1,0:T(8,128)(2,1)} %get-tuple-element.16.refs_0_) | copy-start | bytes 3145732
  16.5 17.5 %collective-permute-start.3 = (f32[528,256]{1,0:T(8,128)S(1)}, f32[528,256]{1,0:T(8,128)S(1)}, u32[]{:S(2)}, u32[]{:S(2)}) collective-permute-start(f32[528,256]{1,0:T(8,128)S(1)} %hist.10.refs_4_.x_ref), channel_id=1, source_target_pairs={{0,4},{12,8},{1,5},{13,9},{2,6},{14,10},{3,7},{15,11},{16,20},{28,... | collective-permute-start | bytes 1622024 | tf_op jit(solution)/shard_map/ppermute | solution.py:566
  26.3 19.3 %collective-permute-start.2 = (f32[528,256]{1,0:T(8,128)S(1)}, f32[528,256]{1,0:T(8,128)S(1)}, u32[]{:S(2)}, u32[]{:S(2)}) collective-permute-start(f32[528,256]{1,0:T(8,128)S(1)} %hist.11.refs_4_.x_ref), channel_id=1, source_target_pairs={{0,4},{12,8},{1,5},{13,9},{2,6},{14,10},{3,7},{15,11},{16,20},{28,... | collective-permute-start | bytes 1622024 | tf_op jit(solution)/shard_map/ppermute | solution.py:566
  32.4 26.3 %collective-permute-start.5 = (f32[528,256]{1,0:T(8,128)S(1)}, f32[528,256]{1,0:T(8,128)S(1)}, u32[]{:S(2)}, u32[]{:S(2)}) collective-permute-start(f32[528,256]{1,0:T(8,128)S(1)} %hist.12.refs_4_.tie_ref.x_ref), channel_id=1, source_target_pairs={{0,4},{12,8},{1,5},{13,9},{2,6},{14,10},{3,7},{15,11},{16,20},{28,... | collective-permute-start | bytes 1622024 | tf_op jit(solution)/shard_map/ppermute | solution.py:569
  34.1 25.4 %collective-permute-start.4 = (f32[528,256]{1,0:T(8,128)S(1)}, f32[528,256]{1,0:T(8,128)S(1)}, u32[]{:S(2)}, u32[]{:S(2)}) collective-permute-start(f32[528,256]{1,0:T(8,128)S(1)} %sum_after.4), channel_id=1, source_target_pairs={{4,8},{8,4},{5,9},{9,5},{6,10},{10,6},{7,11},{11,7},{20,24},{24,20... | collective-permute-start | bytes 1622024 | tf_op jit(solution)/shard_map/ppermute | solution.py:570
  45.7 22.9 %collective-permute-start.6 = (f32[528,256]{1,0:T(8,128)S(1)}, f32[528,256]{1,0:T(8,128)S(1)}, u32[]{:S(2)}, u32[]{:S(2)}) collective-permute-start(f32[528,256]{1,0:T(8,128)S(1)} %sum_after.5), channel_id=1, source_target_pairs={{4,8},{8,4},{5,9},{9,5},{6,10},{10,6},{7,11},{11,7},{20,24},{24,20... | collective-permute-start | bytes 1622024 | tf_op jit(solution)/shard_map/ppermute | solution.py:570
  46.4 27.2 %collective-permute-start.7 = (f32[528,256]{1,0:T(8,128)S(1)}, f32[528,256]{1,0:T(8,128)S(1)}, u32[]{:S(2)}, u32[]{:S(2)}) collective-permute-start(f32[528,256]{1,0:T(8,128)S(1)} %hist.13.refs_4_.tie_ref.x_ref), channel_id=1, source_target_pairs={{0,4},{12,8},{1,5},{13,9},{2,6},{14,10},{3,7},{15,11},{16,20},{28,... | collective-permute-start | bytes 1622024 | tf_op jit(solution)/shard_map/ppermute | solution.py:569
  58.8 21.9 %collective-permute-start.9 = (f32[528,256]{1,0:T(8,128)S(1)}, f32[528,256]{1,0:T(8,128)S(1)}, u32[]{:S(2)}, u32[]{:S(2)}) collective-permute-start(f32[528,256]{1,0:T(8,128)S(1)} %sum_after.6), channel_id=1, source_target_pairs={{4,8},{8,4},{5,9},{9,5},{6,10},{10,6},{7,11},{11,7},{20,24},{24,20... | collective-permute-start | bytes 1622024 | tf_op jit(solution)/shard_map/ppermute | solution.py:577
  59.6 21.1 %collective-permute-start.8 = (f32[528,256]{1,0:T(8,128)S(1)}, f32[528,256]{1,0:T(8,128)S(1)}, u32[]{:S(2)}, u32[]{:S(2)}) collective-permute-start(f32[528,256]{1,0:T(8,128)S(1)} %add.6), channel_id=1, source_target_pairs={{0,4},{4,0},{8,12},{12,8},{1,5},{5,1},{9,13},{13,9},{2,6},{6,2},{1... | collective-permute-start | bytes 1622024 | tf_op jit(solution)/shard_map/ppermute | solution.py:573
  68.6 23.3 %collective-permute-start.14 = (f32[528,256]{1,0:T(8,128)S(1)}, f32[528,256]{1,0:T(8,128)S(1)}, u32[]{:S(2)}, u32[]{:S(2)}) collective-permute-start(f32[528,256]{1,0:T(8,128)S(1)} %add.7), channel_id=1, source_target_pairs={{0,4},{4,0},{8,12},{12,8},{1,5},{5,1},{9,13},{13,9},{2,6},{6,2},{1... | collective-permute-start | bytes 1622024 | tf_op jit(solution)/shard_map/ppermute | solution.py:573
  73.7 18.2 %collective-permute-start.15 = (f32[528,256]{1,0:T(8,128)S(1)}, f32[528,256]{1,0:T(8,128)S(1)}, u32[]{:S(2)}, u32[]{:S(2)}) collective-permute-start(f32[528,256]{1,0:T(8,128)S(1)} %sum_after.7), channel_id=1, source_target_pairs={{4,8},{8,4},{5,9},{9,5},{6,10},{10,6},{7,11},{11,7},{20,24},{24,20... | collective-permute-start | bytes 1622024 | tf_op jit(solution)/shard_map/ppermute | solution.py:577
  80.7 12.8 %copy-start.7 = (s32[8,256]{1,0:T(8,128)}, s32[8,256]{1,0:T(8,128)S(1)}, u32[]{:S(2)}) copy-start(s32[8,256]{1,0:T(8,128)S(1)} %get-tuple-element.20.route_ref) | copy-start | bytes 24580
  82.3 20.5 %copy-start.4 = (f32[2,16,256]{2,1,0:T(8,128)}, f32[2,16,256]{2,1,0:T(8,128)S(1)}, u32[]{:S(2)}) copy-start(f32[2,16,256]{2,1,0:T(8,128)S(1)} %gains.2.refs_0_) | copy-start | bytes 98308
  82.3 15.2 %collective-permute-start.12 = (f32[2,16,256]{2,1,0:T(8,128)S(1)}, f32[2,16,256]{2,1,0:T(8,128)S(1)}, u32[]{:S(2)}, u32[]{:S(2)}) collective-permute-start(f32[2,16,256]{2,1,0:T(8,128)S(1)} %gains.2.refs_0_), channel_id=1, source_target_pairs={{0,12},{4,8},{8,4},{12,0},{1,13},{5,9},{9,5},{13,1},{2,14},{6,10},... | collective-permute-start | bytes 98312 | tf_op jit(solution)/shard_map/ppermute | solution.py:619
  84.8 13.3 %collective-permute-start.11 = (f32[2,16,256]{2,1,0:T(8,128)S(1)}, f32[2,16,256]{2,1,0:T(8,128)S(1)}, u32[]{:S(2)}, u32[]{:S(2)}) collective-permute-start(f32[2,16,256]{2,1,0:T(8,128)S(1)} %gains.2.refs_0_), channel_id=1, source_target_pairs={{0,8},{4,12},{8,0},{12,4},{1,9},{5,13},{9,1},{13,5},{2,10},{6,14},... | collective-permute-start | bytes 98312 | tf_op jit(solution)/shard_map/ppermute | solution.py:619
  87.2 10.9 %collective-permute-start.10 = (f32[2,16,256]{2,1,0:T(8,128)S(1)}, f32[2,16,256]{2,1,0:T(8,128)S(1)}, u32[]{:S(2)}, u32[]{:S(2)}) collective-permute-start(f32[2,16,256]{2,1,0:T(8,128)S(1)} %gains.2.refs_0_), channel_id=1, source_target_pairs={{0,4},{4,0},{8,12},{12,8},{1,5},{5,1},{9,13},{13,9},{2,6},{6,2},{1... | collective-permute-start | bytes 98312 | tf_op jit(solution)/shard_map/ppermute | solution.py:619
  93.6 9.3 %copy-start.5 = (f32[2,16,256]{2,1,0:T(8,128)}, f32[2,16,256]{2,1,0:T(8,128)S(1)}, u32[]{:S(2)}) copy-start(f32[2,16,256]{2,1,0:T(8,128)S(1)} %gains.3.refs_5_) | copy-start | bytes 98308
  93.6 6.1 %collective-permute-start.18 = (f32[2,16,256]{2,1,0:T(8,128)S(1)}, f32[2,16,256]{2,1,0:T(8,128)S(1)}, u32[]{:S(2)}, u32[]{:S(2)}) collective-permute-start(f32[2,16,256]{2,1,0:T(8,128)S(1)} %gains.3.refs_5_), channel_id=1, source_target_pairs={{0,12},{4,8},{8,4},{12,0},{1,13},{5,9},{9,5},{13,1},{2,14},{6,10},... | collective-permute-start | bytes 98312 | tf_op jit(solution)/shard_map/ppermute | solution.py:619
  96.4 4.8 %collective-permute-start.17 = (f32[2,16,256]{2,1,0:T(8,128)S(1)}, f32[2,16,256]{2,1,0:T(8,128)S(1)}, u32[]{:S(2)}, u32[]{:S(2)}) collective-permute-start(f32[2,16,256]{2,1,0:T(8,128)S(1)} %gains.3.refs_5_), channel_id=1, source_target_pairs={{0,8},{4,12},{8,0},{12,4},{1,9},{5,13},{9,1},{13,5},{2,10},{6,14},... | collective-permute-start | bytes 98312 | tf_op jit(solution)/shard_map/ppermute | solution.py:619
  97.6 4.0 %collective-permute-start.16 = (f32[2,16,256]{2,1,0:T(8,128)S(1)}, f32[2,16,256]{2,1,0:T(8,128)S(1)}, u32[]{:S(2)}, u32[]{:S(2)}) collective-permute-start(f32[2,16,256]{2,1,0:T(8,128)S(1)} %gains.3.refs_5_), channel_id=1, source_target_pairs={{0,4},{4,0},{8,12},{12,8},{1,5},{5,1},{9,13},{13,9},{2,6},{6,2},{1... | collective-permute-start | bytes 98312 | tf_op jit(solution)/shard_map/ppermute | solution.py:619
  98.1 3.6 %collective-permute-start.13 = (f32[2,16,256]{2,1,0:T(8,128)S(1)}, f32[2,16,256]{2,1,0:T(8,128)S(1)}, u32[]{:S(2)}, u32[]{:S(2)}) collective-permute-start(f32[2,16,256]{2,1,0:T(8,128)S(1)} %select_select_fusion.1), channel_id=1, source_target_pairs={{0,1},{1,0},{2,3},{3,2},{4,5},{5,4},{6,7},{7,6},{8,9},{9,8},{10,11... | collective-permute-start | bytes 98312 | tf_op jit(solution)/shard_map/ppermute | solution.py:620
  101.6 1.3 %collective-permute-start.19 = (f32[2,16,256]{2,1,0:T(8,128)S(1)}, f32[2,16,256]{2,1,0:T(8,128)S(1)}, u32[]{:S(2)}, u32[]{:S(2)}) collective-permute-start(f32[2,16,256]{2,1,0:T(8,128)S(1)} %select_select_fusion), channel_id=1, source_target_pairs={{0,1},{1,0},{2,3},{3,2},{4,5},{5,4},{6,7},{7,6},{8,9},{9,8},{10,11... | collective-permute-start | bytes 98312 | tf_op jit(solution)/shard_map/ppermute | solution.py:620
  (17 other events, 65.5 us)

commit v6 on v5

--- a/solution.py
+++ b/solution.py
@@ -12,6 +12,7 @@
 TILE = 256
 PACK = 128
 FAST = 9
+HEAD = 5
 PREP_MIB = 56
 MIB = 1024 * 1024
 VMEM_SPEC = pl.BlockSpec(memory_space=pltpu.VMEM)
@@ -128,8 +129,15 @@
         return carry
 
     total = bases[blocks]
-    used = (total + TILE - 1) // TILE
-    lax.fori_loop(0, used, move, 0)
+    used = jnp.maximum((total + TILE - 1) // TILE, HEAD)
+    head = pl.ds(0, HEAD * TILE)
+    send_buf[head, :] = jnp.dot(acc_ref[head, :], perm[:, half:], preferred_element_type=jnp.float32)
+    send_head = pltpu.make_async_copy(send_buf.at[head, :], send_ref.at[head, :], out_sems.at[0, 1])
+    send_head.start()
+    own_buf[head, :] = jnp.dot(acc_ref[head, :], perm[:, :half], preferred_element_type=jnp.float32).astype(jnp.bfloat16)
+    own_head = pltpu.make_async_copy(own_buf.at[head, :], own_ref.at[head, :], out_sems.at[0, 0])
+    own_head.start()
+    lax.fori_loop(HEAD, used, move, 0)
     lane = lax.broadcasted_iota(jnp.int32, (acc_w_ref.shape[0], rows), 1)
     row = lax.broadcasted_iota(jnp.int32, lane.shape, 0)
     packed = jnp.where(lane < total, acc_w_ref[:, :rows], 0.0)
@@ -137,7 +145,9 @@
     packed = jnp.where(row == kdim + 1, packs, packed)
     wt_ref[...] = packed.astype(jnp.bfloat16)
     wt_send_ref[...] = packed[: kdim + 8]
-    lax.fori_loop(0, used, moved_out, 0)
+    send_head.wait()
+    own_head.wait()
+    lax.fori_loop(HEAD, used, moved_out, 0)
 
 
 def prep(line, slab, owners, bins, grads, hess, side):
@@ -221,8 +231,10 @@
         place_weights(height)
         tiles = [(r, min(TILE, parts * height - r)) for r in range(0, parts * height, TILE)]
 
-        def two_levels(step, carry):
-            some = [2 * step, 2 * step + 1]
+        together = 4 if parts == 1 and levels % 4 == 0 else 2
+
+        def some_levels(step, carry):
+            some = [together * step + i for i in range(together)]
             for b, (grad, hess) in zip(some, sums_of(some, tiles)):
                 grad_spot, hess_spot = spots_of(b)
                 if has_init:
@@ -231,7 +243,7 @@
                 out_ref[hess_spot, :] = hess
             return carry
 
-        lax.fori_loop(0, levels // 2, two_levels, 0)
+        lax.fori_loop(0, levels // together, some_levels, 0)
 
     def general():
         for i, (bins_ref, _) in enumerate(pairs):
@@ -507,6 +519,7 @@
         in_specs=[VMEM_SPEC] * (1 + len(flat)),
         out_specs=VMEM_SPEC,
         out_shape=jax.ShapeDtypeStruct((width * len(parts), 2, nbins), jnp.float32),
+        compiler_params=pltpu.CompilerParams(vmem_limit_bytes=16 * MIB),
         name="finish",
     )(route, *flat)
 

time: 106 us -> 103 us (0.972)
  Pallas kernels: 53.9 us -> 52.1 us
    unnamed x42 -> x20, local copies, waits for them, and re-layouts: 2.85 us -> 2.2 us
  transfers between devices with their start and end apart: 20 -> 20, of which waited for: 7 -> 7; matrix products, arithmetic and copies ran while one was open for 1% -> 1% of each run, Pallas kernels for 39% -> 40%
where the time goes in v6:
time: 103 us
  Pallas kernels  52.1 us (51%)
  starting transfers between devices  32.4 us (31%)
  waiting for transfers between devices  13 us (13%)
  local copies, waits for them, and re-layouts  2.71 us (3%)
  between operations  2.37 us (2%)
    pallas_call x9, Pallas kernels, hist(): pl.pallas_call(functools.partial(hist_kernel, first_column, width, levels...  39 us
    ppermute x6, starting transfers between devices, per_device(): lax.ppermute(gain, 'dp', [(i, i ^ s) for i in range(line)])  9.77 us
    ppermute x2, starting transfers between devices, sum_line_of_4(): a1[c] = lax.ppermute(units[1, c], 'dp', inward)  8.53 us
    pallas_call x1, Pallas kernels, prep(): pl.pallas_call(functools.partial(prep_kernel, line, slab), in_specs=[SMEM...  7.64 us
    ppermute x2, starting transfers between devices, sum_line_of_4(): a0[c] = lax.ppermute(units[0, c], 'dp', inward)  6.24 us
    ppermute x2, waiting for transfers between devices, sum_line_of_4(): a0[c] = lax.ppermute(units[0, c], 'dp', inward)  6.24 us
    ppermute x2, starting transfers between devices, sum_line_of_4(): a2[c] = lax.ppermute(units[2, c] + b1[c], 'dp', outer)  4.17 us
    ppermute x6, waiting for transfers between devices, per_device(): lax.ppermute(gain, 'dp', [(i, i ^ s) for i in range(line)])  3.38 us
  transfers between devices with their start and end apart: 20, of which 7 were waited for; matrix products, arithmetic and copies ran while one was open for 1% of the time, Pallas kernels for 40%

profile of v6, /device:TPU:0, one launch (start us, length us, event | category | flops | bytes accessed | tf_op | source)
XLA Modules:
  0.0 102.8 jit_solution(281934741592087122)
XLA Ops:
  0.0 7.6 %prep.1 = (bf16[2048,256]{1,0:T(8,128)(2,1)}, f32[2048,256]{1,0:T(8,128)}, bf16[48,2048]{1,0:T(8,128)(2,1)}, f32[40,2048]{1,0:T(8,128)}) custom-call(s32[8]{0:T(128)} %owner_ref.3, s32[2048,512]{1,0:T(8,128)} %bins_ref.1, bf16[32,2048]{1,0:T(8,128)(2,1)} %bitcast.12, bf16[2048]{0:T(1024)(128)(2,1)} %hess_ref.1, s32[1,2048]{1,0:T(1,128)} %bitcast.13), custom_call_target="tpu_custom_call" | custom-call | flops 2147483648 | bytes 8388608 | tf_op jit(solution)/shard_map/prep/pallas_call | solution.py:157
  10.4 2.6 %hist.9.refs_2_ = f32[528,256]{1,0:T(8,128)S(1)} custom-call(bf16[2048,256]{1,0:T(8,128)(2,1)S(1)} %copy-done, bf16[48,2048]{1,0:T(8,128)(2,1)S(1)} %copy-done.2), custom_call_target="tpu_custom_call" | custom-call | flops 524288 | bytes 524288 | tf_op jit(solution)/shard_map/hist/pallas_call | solution.py:293
  13.1 2.6 %hist.10.refs_4_.x_ref = f32[528,256]{1,0:T(8,128)S(1)} custom-call(f32[2048,256]{1,0:T(8,128)S(1)} %collective-permute-done.refs_0_.refs_2_, f32[40,2048]{1,0:T(8,128)S(1)} %collective-permute-done.1.refs_1_.refs_3_, f32[528,256]{1,0:T(8,128)S(1)} %hist.9.refs_2_), custom_call_target="tpu_custom_call" | custom-call | flops 524288 | bytes 524288 | tf_op jit(solution)/shard_map/hist/pallas_call | solution.py:293
  15.6 4.9 %collective-permute-start.3 = (f32[528,256]{1,0:T(8,128)S(1)}, f32[528,256]{1,0:T(8,128)S(1)}, u32[]{:S(2)}, u32[]{:S(2)}) collective-permute-start(f32[528,256]{1,0:T(8,128)S(1)} %hist.10.refs_4_.x_ref), channel_id=1, source_target_pairs={{0,4},{12,8},{1,5},{13,9},{2,6},{14,10},{3,7},{15,11},{16,20},{28,... | collective-permute-start | bytes 1622024 | tf_op jit(solution)/shard_map/ppermute | solution.py:579
  20.6 4.8 %hist.11.refs_4_.x_ref = f32[528,256]{1,0:T(8,128)S(1)} custom-call(bf16[2048,256]{1,0:T(8,128)(2,1)S(1)} %copy-done.1, bf16[48,2048]{1,0:T(8,128)(2,1)S(1)} %copy-done.2, f32[2048,256]{1,0:T(8,128)S(1)} %collective-permute-done.refs_0_.refs_2_, f32[40,2048]{1,0:T(8,128)S(1)} %collective-permute-done.1.refs_1_.refs_3_, f32[528,256]{1,0:T(8,128)S(1)} %hist.10.refs_4_.x_ref), custom_call_target="tpu_custom_call" | custom-call | flops 1048576 | bytes 1048576 | tf_op jit(solution)/shard_map/hist/pallas_call | solution.py:293
  25.4 1.3 %collective-permute-start.2 = (f32[528,256]{1,0:T(8,128)S(1)}, f32[528,256]{1,0:T(8,128)S(1)}, u32[]{:S(2)}, u32[]{:S(2)}) collective-permute-start(f32[528,256]{1,0:T(8,128)S(1)} %hist.11.refs_4_.x_ref), channel_id=1, source_target_pairs={{0,4},{12,8},{1,5},{13,9},{2,6},{14,10},{3,7},{15,11},{16,20},{28,... | collective-permute-start | bytes 1622024 | tf_op jit(solution)/shard_map/ppermute | solution.py:579
  26.7 4.8 %hist.12.refs_4_.tie_ref.x_ref = f32[528,256]{1,0:T(8,128)S(1)} custom-call(bf16[2048,256]{1,0:T(8,128)(2,1)S(1)} %copy-done.1, bf16[48,2048]{1,0:T(8,128)(2,1)S(1)} %copy-done.2, f32[2048,256]{1,0:T(8,128)S(1)} %collective-permute-done.refs_0_.refs_2_, f32[40,2048]{1,0:T(8,128)S(1)} %collective-permute-done.1.refs_1_.refs_3_, f32[528,256]{1,0:T(8,128)S(1)} %hist.11.refs_4_.x_ref), custom_call_target="tpu_custom_call" | custom-call | flops 1048576 | bytes 1048576 | tf_op jit(solution)/shard_map/hist/pallas_call | solution.py:293
  31.6 1.3 %collective-permute-start.5 = (f32[528,256]{1,0:T(8,128)S(1)}, f32[528,256]{1,0:T(8,128)S(1)}, u32[]{:S(2)}, u32[]{:S(2)}) collective-permute-start(f32[528,256]{1,0:T(8,128)S(1)} %hist.12.refs_4_.tie_ref.x_ref), channel_id=1, source_target_pairs={{0,4},{12,8},{1,5},{13,9},{2,6},{14,10},{3,7},{15,11},{16,20},{28,... | collective-permute-start | bytes 1622024 | tf_op jit(solution)/shard_map/ppermute | solution.py:582
  33.9 4.8 %hist.13.refs_4_.tie_ref.x_ref = f32[528,256]{1,0:T(8,128)S(1)} custom-call(bf16[2048,256]{1,0:T(8,128)(2,1)S(1)} %copy-done.1, bf16[48,2048]{1,0:T(8,128)(2,1)S(1)} %copy-done.2, f32[2048,256]{1,0:T(8,128)S(1)} %collective-permute-done.refs_0_.refs_2_, f32[40,2048]{1,0:T(8,128)S(1)} %collective-permute-done.1.refs_1_.refs_3_, ...), custom_call_target="tpu_custom_call" | custom-call | flops 1048576 | bytes 1048576 | tf_op jit(solution)/shard_map/hist/pallas_call | solution.py:293
  38.8 6.0 %collective-permute-done.2.refs_5_.y_ref = f32[528,256]{1,0:T(8,128)S(1)} collective-permute-done((f32[528,256]{1,0:T(8,128)S(1)}, f32[528,256]{1,0:T(8,128)S(1)}, u32[]{:S(2)}, u32[]{:S(2)}) %collective-permute-start.2) | collective-permute-done | bytes 540704 | tf_op jit(solution)/shard_map/ppermute | solution.py:579
  45.5 7.2 %collective-permute-start.7 = (f32[528,256]{1,0:T(8,128)S(1)}, f32[528,256]{1,0:T(8,128)S(1)}, u32[]{:S(2)}, u32[]{:S(2)}) collective-permute-start(f32[528,256]{1,0:T(8,128)S(1)} %hist.13.refs_4_.tie_ref.x_ref), channel_id=1, source_target_pairs={{0,4},{12,8},{1,5},{13,9},{2,6},{14,10},{3,7},{15,11},{16,20},{28,... | collective-permute-start | bytes 1622024 | tf_op jit(solution)/shard_map/ppermute | solution.py:582
  52.7 4.8 %hist.14.refs_4_.tie_ref = f32[528,256]{1,0:T(8,128)S(1)} custom-call(bf16[2048,256]{1,0:T(8,128)(2,1)S(1)} %copy-done.1, bf16[48,2048]{1,0:T(8,128)(2,1)S(1)} %copy-done.2, f32[2048,256]{1,0:T(8,128)S(1)} %collective-permute-done.refs_0_.refs_2_, f32[40,2048]{1,0:T(8,128)S(1)} %collective-permute-done.1.refs_1_.refs_3_, ...), custom_call_target="tpu_custom_call" | custom-call | flops 1048576 | bytes 1048576 | tf_op jit(solution)/shard_map/hist/pallas_call | solution.py:293
  58.4 4.1 %collective-permute-start.8 = (f32[528,256]{1,0:T(8,128)S(1)}, f32[528,256]{1,0:T(8,128)S(1)}, u32[]{:S(2)}, u32[]{:S(2)}) collective-permute-start(f32[528,256]{1,0:T(8,128)S(1)} %add.6), channel_id=1, source_target_pairs={{0,4},{4,0},{8,12},{12,8},{1,5},{5,1},{9,13},{13,9},{2,6},{6,2},{1... | collective-permute-start | bytes 1622024 | tf_op jit(solution)/shard_map/ppermute | solution.py:586
  62.5 4.8 %hist.15.refs_4_ = f32[528,256]{1,0:T(8,128)S(1)} custom-call(bf16[2048,256]{1,0:T(8,128)(2,1)S(1)} %copy-done.1, bf16[48,2048]{1,0:T(8,128)(2,1)S(1)} %copy-done.2, f32[2048,256]{1,0:T(8,128)S(1)} %collective-permute-done.refs_0_.refs_2_, f32[40,2048]{1,0:T(8,128)S(1)} %collective-permute-done.1.refs_1_.refs_3_, f32[528,256]{1,0:T(8,128)S(1)} %hist.14.refs_4_.tie_ref, ...), custom_call_target="tpu_custom_call" | custom-call | flops 1048576 | bytes 1048576 | tf_op jit(solution)/shard_map/hist/pallas_call | solution.py:293
  67.5 4.8 %hist.16.refs_4_.last_ref.tie_ref = f32[528,256]{1,0:T(8,128)S(1)} custom-call(bf16[2048,256]{1,0:T(8,128)(2,1)S(1)} %copy-done.1, bf16[48,2048]{1,0:T(8,128)(2,1)S(1)} %copy-done.2, f32[2048,256]{1,0:T(8,128)S(1)} %collective-permute-done.refs_0_.refs_2_, f32[40,2048]{1,0:T(8,128)S(1)} %collective-permute-done.1.refs_1_.refs_3_, ...), custom_call_target="tpu_custom_call" | custom-call | flops 1048576 | bytes 1048576 | tf_op jit(solution)/shard_map/hist/pallas_call | solution.py:293
  73.4 4.9 %hist.17.tie_ref.last_ref = f32[528,256]{1,0:T(8,128)S(1)} custom-call(bf16[2048,256]{1,0:T(8,128)(2,1)S(1)} %copy-done.1, bf16[48,2048]{1,0:T(8,128)(2,1)S(1)} %copy-done.2, f32[2048,256]{1,0:T(8,128)S(1)} %collective-permute-done.refs_0_.refs_2_, f32[40,2048]{1,0:T(8,128)S(1)} %collective-permute-done.1.refs_1_.refs_3_, ...), custom_call_target="tpu_custom_call" | custom-call | flops 1048576 | bytes 1048576 | tf_op jit(solution)/shard_map/hist/pallas_call | solution.py:293
  79.6 1.6 %gains.2.refs_0_ = f32[2,16,256]{2,1,0:T(8,128)S(1)} custom-call(f32[528,256]{1,0:T(8,128)S(1)} %hist.16.refs_4_.last_ref.tie_ref, f32[528,256]{1,0:T(8,128)S(1)} %collective-permute-done.8.right_ref, f32[528,256]{1,0:T(8,128)S(1)} %collective-permute-done.9.left_ref, f32[512,256]{1,0:T(8,128)S(1)} %get-tuple-element.21.par_grad_ref, ...), custom_call_target="tpu_custom_call" | custom-call | flops 6553600 | bytes 2097152 | tf_op jit(solution)/shard_map/gains/pallas_call | solution.py:468
  81.1 2.5 %collective-permute-start.12 = (f32[2,16,256]{2,1,0:T(8,128)S(1)}, f32[2,16,256]{2,1,0:T(8,128)S(1)}, u32[]{:S(2)}, u32[]{:S(2)}) collective-permute-start(f32[2,16,256]{2,1,0:T(8,128)S(1)} %gains.2.refs_0_), channel_id=1, source_target_pairs={{0,12},{4,8},{8,4},{12,0},{1,13},{5,9},{9,5},{13,1},{2,14},{6,10},... | collective-permute-start | bytes 98312 | tf_op jit(solution)/shard_map/ppermute | solution.py:632
  83.6 2.7 %collective-permute-start.11 = (f32[2,16,256]{2,1,0:T(8,128)S(1)}, f32[2,16,256]{2,1,0:T(8,128)S(1)}, u32[]{:S(2)}, u32[]{:S(2)}) collective-permute-start(f32[2,16,256]{2,1,0:T(8,128)S(1)} %gains.2.refs_0_), channel_id=1, source_target_pairs={{0,8},{4,12},{8,0},{12,4},{1,9},{5,13},{9,1},{13,5},{2,10},{6,14},... | collective-permute-start | bytes 98312 | tf_op jit(solution)/shard_map/ppermute | solution.py:632
  88.9 2.2 %collective-permute-done.14.right_ref = f32[528,256]{1,0:T(8,128)S(1)} collective-permute-done((f32[528,256]{1,0:T(8,128)S(1)}, f32[528,256]{1,0:T(8,128)S(1)}, u32[]{:S(2)}, u32[]{:S(2)}) %collective-permute-start.14) | collective-permute-done | bytes 540704 | tf_op jit(solution)/shard_map/ppermute | solution.py:586
  91.1 1.6 %gains.3.refs_5_ = f32[2,16,256]{2,1,0:T(8,128)S(1)} custom-call(f32[528,256]{1,0:T(8,128)S(1)} %hist.17.tie_ref.last_ref, f32[528,256]{1,0:T(8,128)S(1)} %collective-permute-done.14.right_ref, f32[528,256]{1,0:T(8,128)S(1)} %collective-permute-done.15.left_ref, f32[512,256]{1,0:T(8,128)S(1)} %get-tuple-element.24.par_grad_ref, ...), custom_call_target="tpu_custom_call" | custom-call | flops 6553600 | bytes 2097152 | tf_op jit(solution)/shard_map/gains/pallas_call | solution.py:468
  92.7 2.5 %collective-permute-start.18 = (f32[2,16,256]{2,1,0:T(8,128)S(1)}, f32[2,16,256]{2,1,0:T(8,128)S(1)}, u32[]{:S(2)}, u32[]{:S(2)}) collective-permute-start(f32[2,16,256]{2,1,0:T(8,128)S(1)} %gains.3.refs_5_), channel_id=1, source_target_pairs={{0,12},{4,8},{8,4},{12,0},{1,13},{5,9},{9,5},{13,1},{2,14},{6,10},... | collective-permute-start | bytes 98312 | tf_op jit(solution)/shard_map/ppermute | solution.py:632
  95.2 1.5 %collective-permute-start.17 = (f32[2,16,256]{2,1,0:T(8,128)S(1)}, f32[2,16,256]{2,1,0:T(8,128)S(1)}, u32[]{:S(2)}, u32[]{:S(2)}) collective-permute-start(f32[2,16,256]{2,1,0:T(8,128)S(1)} %gains.3.refs_5_), channel_id=1, source_target_pairs={{0,8},{4,12},{8,0},{12,4},{1,9},{5,13},{9,1},{13,5},{2,10},{6,14},... | collective-permute-start | bytes 98312 | tf_op jit(solution)/shard_map/ppermute | solution.py:632
  97.2 1.6 %collective-permute-done.18.refs_8_ = f32[2,16,256]{2,1,0:T(8,128)S(1)} collective-permute-done((f32[2,16,256]{2,1,0:T(8,128)S(1)}, f32[2,16,256]{2,1,0:T(8,128)S(1)}, u32[]{:S(2)}, u32[]{:S(2)}) %collective-permute-start.18) | collective-permute-done | bytes 32800 | tf_op jit(solution)/shard_map/ppermute | solution.py:632
  (59 shorter events, 12.7 us)
Async XLA Ops:
  7.6 5.4 %collective-permute-start = (f32[2048,256]{1,0:T(8,128)}, f32[2048,256]{1,0:T(8,128)S(1)}, u32[]{:S(2)}, u32[]{:S(2)}) collective-permute-start(f32[2048,256]{1,0:T(8,128)} %get-tuple-element.18), channel_id=1, source_target_pairs={{0,1},{1,0},{2,3},{3,2},{4,5},{5,4},{6,7},{7,6},{8,9},{9,8},{10,11... | collective-permute-start | bytes 6291464 | tf_op jit(solution)/shard_map/ppermute | solution.py:607
  8.2 4.9 %collective-permute-start.1 = (f32[40,2048]{1,0:T(8,128)}, f32[40,2048]{1,0:T(8,128)S(1)}, u32[]{:S(2)}, u32[]{:S(2)}) collective-permute-start(f32[40,2048]{1,0:T(8,128)} %get-tuple-element.19), channel_id=1, source_target_pairs={{0,1},{1,0},{2,3},{3,2},{4,5},{5,4},{6,7},{7,6},{8,9},{9,8},{10,11... | collective-permute-start | bytes 983048 | tf_op jit(solution)/shard_map/ppermute | solution.py:606
  13.0 7.6 %copy-start.1 = (bf16[2048,256]{1,0:T(8,128)(2,1)S(1)}, bf16[2048,256]{1,0:T(8,128)(2,1)}, u32[]{:S(2)}) copy-start(bf16[2048,256]{1,0:T(8,128)(2,1)} %get-tuple-element.16.refs_0_) | copy-start | bytes 3145732
  15.6 17.5 %collective-permute-start.3 = (f32[528,256]{1,0:T(8,128)S(1)}, f32[528,256]{1,0:T(8,128)S(1)}, u32[]{:S(2)}, u32[]{:S(2)}) collective-permute-start(f32[528,256]{1,0:T(8,128)S(1)} %hist.10.refs_4_.x_ref), channel_id=1, source_target_pairs={{0,4},{12,8},{1,5},{13,9},{2,6},{14,10},{3,7},{15,11},{16,20},{28,... | collective-permute-start | bytes 1622024 | tf_op jit(solution)/shard_map/ppermute | solution.py:579
  25.4 19.3 %collective-permute-start.2 = (f32[528,256]{1,0:T(8,128)S(1)}, f32[528,256]{1,0:T(8,128)S(1)}, u32[]{:S(2)}, u32[]{:S(2)}) collective-permute-start(f32[528,256]{1,0:T(8,128)S(1)} %hist.11.refs_4_.x_ref), channel_id=1, source_target_pairs={{0,4},{12,8},{1,5},{13,9},{2,6},{14,10},{3,7},{15,11},{16,20},{28,... | collective-permute-start | bytes 1622024 | tf_op jit(solution)/shard_map/ppermute | solution.py:579
  31.6 26.0 %collective-permute-start.5 = (f32[528,256]{1,0:T(8,128)S(1)}, f32[528,256]{1,0:T(8,128)S(1)}, u32[]{:S(2)}, u32[]{:S(2)}) collective-permute-start(f32[528,256]{1,0:T(8,128)S(1)} %hist.12.refs_4_.tie_ref.x_ref), channel_id=1, source_target_pairs={{0,4},{12,8},{1,5},{13,9},{2,6},{14,10},{3,7},{15,11},{16,20},{28,... | collective-permute-start | bytes 1622024 | tf_op jit(solution)/shard_map/ppermute | solution.py:582
  33.2 25.1 %collective-permute-start.4 = (f32[528,256]{1,0:T(8,128)S(1)}, f32[528,256]{1,0:T(8,128)S(1)}, u32[]{:S(2)}, u32[]{:S(2)}) collective-permute-start(f32[528,256]{1,0:T(8,128)S(1)} %sum_after.4), channel_id=1, source_target_pairs={{4,8},{8,4},{5,9},{9,5},{6,10},{10,6},{7,11},{11,7},{20,24},{24,20... | collective-permute-start | bytes 1622024 | tf_op jit(solution)/shard_map/ppermute | solution.py:583
  44.8 22.6 %collective-permute-start.6 = (f32[528,256]{1,0:T(8,128)S(1)}, f32[528,256]{1,0:T(8,128)S(1)}, u32[]{:S(2)}, u32[]{:S(2)}) collective-permute-start(f32[528,256]{1,0:T(8,128)S(1)} %sum_after.5), channel_id=1, source_target_pairs={{4,8},{8,4},{5,9},{9,5},{6,10},{10,6},{7,11},{11,7},{20,24},{24,20... | collective-permute-start | bytes 1622024 | tf_op jit(solution)/shard_map/ppermute | solution.py:583
  45.5 26.9 %collective-permute-start.7 = (f32[528,256]{1,0:T(8,128)S(1)}, f32[528,256]{1,0:T(8,128)S(1)}, u32[]{:S(2)}, u32[]{:S(2)}) collective-permute-start(f32[528,256]{1,0:T(8,128)S(1)} %hist.13.refs_4_.tie_ref.x_ref), channel_id=1, source_target_pairs={{0,4},{12,8},{1,5},{13,9},{2,6},{14,10},{3,7},{15,11},{16,20},{28,... | collective-permute-start | bytes 1622024 | tf_op jit(solution)/shard_map/ppermute | solution.py:582
  57.7 21.9 %collective-permute-start.9 = (f32[528,256]{1,0:T(8,128)S(1)}, f32[528,256]{1,0:T(8,128)S(1)}, u32[]{:S(2)}, u32[]{:S(2)}) collective-permute-start(f32[528,256]{1,0:T(8,128)S(1)} %sum_after.6), channel_id=1, source_target_pairs={{4,8},{8,4},{5,9},{9,5},{6,10},{10,6},{7,11},{11,7},{20,24},{24,20... | collective-permute-start | bytes 1622024 | tf_op jit(solution)/shard_map/ppermute | solution.py:590
  58.4 21.1 %collective-permute-start.8 = (f32[528,256]{1,0:T(8,128)S(1)}, f32[528,256]{1,0:T(8,128)S(1)}, u32[]{:S(2)}, u32[]{:S(2)}) collective-permute-start(f32[528,256]{1,0:T(8,128)S(1)} %add.6), channel_id=1, source_target_pairs={{0,4},{4,0},{8,12},{12,8},{1,5},{5,1},{9,13},{13,9},{2,6},{6,2},{1... | collective-permute-start | bytes 1622024 | tf_op jit(solution)/shard_map/ppermute | solution.py:586
  67.5 23.6 %collective-permute-start.14 = (f32[528,256]{1,0:T(8,128)S(1)}, f32[528,256]{1,0:T(8,128)S(1)}, u32[]{:S(2)}, u32[]{:S(2)}) collective-permute-start(f32[528,256]{1,0:T(8,128)S(1)} %add.7), channel_id=1, source_target_pairs={{0,4},{4,0},{8,12},{12,8},{1,5},{5,1},{9,13},{13,9},{2,6},{6,2},{1... | collective-permute-start | bytes 1622024 | tf_op jit(solution)/shard_map/ppermute | solution.py:586
  72.5 5.8 %copy-start.3 = (f32[1,64,4096]{2,1,0:T(8,128)S(1)}, f32[1,64,4096]{2,1,0:T(8,128)}, u32[]{:S(2)}) copy-start(f32[1,64,4096]{2,1,0:T(8,128)} %param.18) | copy-start | bytes 3145732
  72.5 5.8 %copy-start.4 = (f32[1,64,128]{2,1,0:T(8,128)S(1)}, f32[1,64,128]{2,1,0:T(8,128)}, u32[]{:S(2)}) copy-start(f32[1,64,128]{2,1,0:T(8,128)} %param.19) | copy-start | bytes 98308
  72.5 5.8 %copy-start.5 = (s32[1024]{0:T(1024)S(1)}, s32[1024]{0:T(1024)}, u32[]{:S(2)}) copy-start(s32[1024]{0:T(1024)} %param.15) | copy-start | bytes 12292
  72.6 18.5 %collective-permute-start.15 = (f32[528,256]{1,0:T(8,128)S(1)}, f32[528,256]{1,0:T(8,128)S(1)}, u32[]{:S(2)}, u32[]{:S(2)}) collective-permute-start(f32[528,256]{1,0:T(8,128)S(1)} %sum_after.7), channel_id=1, source_target_pairs={{4,8},{8,4},{5,9},{9,5},{6,10},{10,6},{7,11},{11,7},{20,24},{24,20... | collective-permute-start | bytes 1622024 | tf_op jit(solution)/shard_map/ppermute | solution.py:590
  81.1 15.6 %collective-permute-start.12 = (f32[2,16,256]{2,1,0:T(8,128)S(1)}, f32[2,16,256]{2,1,0:T(8,128)S(1)}, u32[]{:S(2)}, u32[]{:S(2)}) collective-permute-start(f32[2,16,256]{2,1,0:T(8,128)S(1)} %gains.2.refs_0_), channel_id=1, source_target_pairs={{0,12},{4,8},{8,4},{12,0},{1,13},{5,9},{9,5},{13,1},{2,14},{6,10},... | collective-permute-start | bytes 98312 | tf_op jit(solution)/shard_map/ppermute | solution.py:632
  83.6 13.5 %collective-permute-start.11 = (f32[2,16,256]{2,1,0:T(8,128)S(1)}, f32[2,16,256]{2,1,0:T(8,128)S(1)}, u32[]{:S(2)}, u32[]{:S(2)}) collective-permute-start(f32[2,16,256]{2,1,0:T(8,128)S(1)} %gains.2.refs_0_), channel_id=1, source_target_pairs={{0,8},{4,12},{8,0},{12,4},{1,9},{5,13},{9,1},{13,5},{2,10},{6,14},... | collective-permute-start | bytes 98312 | tf_op jit(solution)/shard_map/ppermute | solution.py:632
  86.4 10.8 %collective-permute-start.10 = (f32[2,16,256]{2,1,0:T(8,128)S(1)}, f32[2,16,256]{2,1,0:T(8,128)S(1)}, u32[]{:S(2)}, u32[]{:S(2)}) collective-permute-start(f32[2,16,256]{2,1,0:T(8,128)S(1)} %gains.2.refs_0_), channel_id=1, source_target_pairs={{0,4},{4,0},{8,12},{12,8},{1,5},{5,1},{9,13},{13,9},{2,6},{6,2},{1... | collective-permute-start | bytes 98312 | tf_op jit(solution)/shard_map/ppermute | solution.py:632
  92.7 6.1 %collective-permute-start.18 = (f32[2,16,256]{2,1,0:T(8,128)S(1)}, f32[2,16,256]{2,1,0:T(8,128)S(1)}, u32[]{:S(2)}, u32[]{:S(2)}) collective-permute-start(f32[2,16,256]{2,1,0:T(8,128)S(1)} %gains.3.refs_5_), channel_id=1, source_target_pairs={{0,12},{4,8},{8,4},{12,0},{1,13},{5,9},{9,5},{13,1},{2,14},{6,10},... | collective-permute-start | bytes 98312 | tf_op jit(solution)/shard_map/ppermute | solution.py:632
  95.2 4.8 %collective-permute-start.17 = (f32[2,16,256]{2,1,0:T(8,128)S(1)}, f32[2,16,256]{2,1,0:T(8,128)S(1)}, u32[]{:S(2)}, u32[]{:S(2)}) collective-permute-start(f32[2,16,256]{2,1,0:T(8,128)S(1)} %gains.3.refs_5_), channel_id=1, source_target_pairs={{0,8},{4,12},{8,0},{12,4},{1,9},{5,13},{9,1},{13,5},{2,10},{6,14},... | collective-permute-start | bytes 98312 | tf_op jit(solution)/shard_map/ppermute | solution.py:632
  96.7 3.9 %collective-permute-start.16 = (f32[2,16,256]{2,1,0:T(8,128)S(1)}, f32[2,16,256]{2,1,0:T(8,128)S(1)}, u32[]{:S(2)}, u32[]{:S(2)}) collective-permute-start(f32[2,16,256]{2,1,0:T(8,128)S(1)} %gains.3.refs_5_), channel_id=1, source_target_pairs={{0,4},{4,0},{8,12},{12,8},{1,5},{5,1},{9,13},{13,9},{2,6},{6,2},{1... | collective-permute-start | bytes 98312 | tf_op jit(solution)/shard_map/ppermute | solution.py:632
  97.2 3.5 %collective-permute-start.13 = (f32[2,16,256]{2,1,0:T(8,128)S(1)}, f32[2,16,256]{2,1,0:T(8,128)S(1)}, u32[]{:S(2)}, u32[]{:S(2)}) collective-permute-start(f32[2,16,256]{2,1,0:T(8,128)S(1)} %select_select_fusion.1), channel_id=1, source_target_pairs={{0,1},{1,0},{2,3},{3,2},{4,5},{5,4},{6,7},{7,6},{8,9},{9,8},{10,11... | collective-permute-start | bytes 98312 | tf_op jit(solution)/shard_map/ppermute | solution.py:633
  100.6 1.3 %collective-permute-start.19 = (f32[2,16,256]{2,1,0:T(8,128)S(1)}, f32[2,16,256]{2,1,0:T(8,128)S(1)}, u32[]{:S(2)}, u32[]{:S(2)}) collective-permute-start(f32[2,16,256]{2,1,0:T(8,128)S(1)} %select_select_fusion), channel_id=1, source_target_pairs={{0,1},{1,0},{2,3},{3,2},{4,5},{5,4},{6,7},{7,6},{8,9},{9,8},{10,11... | collective-permute-start | bytes 98312 | tf_op jit(solution)/shard_map/ppermute | solution.py:633
  (6 other events, 25.2 us)

commit v7 on v6

--- a/solution.py
+++ b/solution.py
@@ -52,7 +52,7 @@
     return roles
 
 
-def prep_kernel(line, slab, owner_ref, bins_ref, grads_ref, hess_ref, side_ref, own_ref, send_ref, wt_ref, wt_send_ref, buf_ref, sems, acc_ref, acc_w_ref, own_buf, send_buf, out_sems):
+def prep_kernel(line, slab, owner_ref, bins_ref, grads_ref, hess_ref, side_ref, own_ref, send_ref, buf_ref, sems, acc_ref, acc_w_ref, own_buf, send_buf, out_sems):
     rows, f_dev = bins_ref.shape
     half = f_dev // 2
     kdim = grads_ref.shape[0]
@@ -143,8 +143,17 @@
     packed = jnp.where(lane < total, acc_w_ref[:, :rows], 0.0)
     packs = ((total + PACK - 1) // PACK).astype(jnp.float32)
     packed = jnp.where(row == kdim + 1, packs, packed)
-    wt_ref[...] = packed.astype(jnp.bfloat16)
-    wt_send_ref[...] = packed[: kdim + 8]
+    for i in range(rows // half):
+        part = packed[:, i * half : (i + 1) * half]
+        own_buf[rows + i * (kdim + 16) : rows + (i + 1) * (kdim + 16), :] = part.astype(jnp.bfloat16)
+        send_buf[rows + i * (kdim + 16) : rows + (i + 1) * (kdim + 16), :] = part
+    below = pl.ds(rows, own_ref.shape[0] - rows)
+    own_tail = pltpu.make_async_copy(own_buf.at[below, :], own_ref.at[below, :], out_sems.at[blocks, 0])
+    own_tail.start()
+    send_tail = pltpu.make_async_copy(send_buf.at[below, :], send_ref.at[below, :], out_sems.at[blocks, 1])
+    send_tail.start()
+    own_tail.wait()
+    send_tail.wait()
     send_head.wait()
     own_head.wait()
     lax.fori_loop(HEAD, used, moved_out, 0)
@@ -154,24 +163,23 @@
     rows, f_dev = bins.shape
     kdim = grads.shape[1]
     half = f_dev // 2
+    height = rows + (kdim + 16) * (rows // half)
     return pl.pallas_call(
         functools.partial(prep_kernel, line, slab),
         in_specs=[SMEM_SPEC, pl.BlockSpec(memory_space=pl.ANY), VMEM_SPEC, VMEM_SPEC, VMEM_SPEC],
-        out_specs=[pl.BlockSpec(memory_space=pl.ANY)] * 2 + [VMEM_SPEC] * 2,
+        out_specs=[pl.BlockSpec(memory_space=pl.ANY)] * 2,
         out_shape=[
-            jax.ShapeDtypeStruct((rows, half), jnp.bfloat16),
-            jax.ShapeDtypeStruct((rows, half), jnp.float32),
-            jax.ShapeDtypeStruct((kdim + 16, rows), jnp.bfloat16),
-            jax.ShapeDtypeStruct((kdim + 8, rows), jnp.float32),
+            jax.ShapeDtypeStruct((height, half), jnp.bfloat16),
+            jax.ShapeDtypeStruct((height, half), jnp.float32),
         ],
         scratch_shapes=[
             pltpu.VMEM((rows, f_dev), jnp.int32),
             pltpu.SemaphoreType.DMA((rows // TILE,)),
             pltpu.VMEM((rows + TILE + PACK, f_dev), jnp.bfloat16),
             pltpu.VMEM((kdim + 16, rows + TILE + PACK), jnp.float32),
-            pltpu.VMEM((rows, half), jnp.bfloat16),
-            pltpu.VMEM((rows, half), jnp.float32),
-            pltpu.SemaphoreType.DMA((rows // TILE, 2)),
+            pltpu.VMEM((height, half), jnp.bfloat16),
+            pltpu.VMEM((height, half), jnp.float32),
+            pltpu.SemaphoreType.DMA((rows // TILE + 1, 2)),
         ],
         compiler_params=pltpu.CompilerParams(vmem_limit_bytes=PREP_MIB * MIB),
         cost_estimate=pl.CostEstimate(flops=4 * rows * f_dev * f_dev, bytes_accessed=8 * rows * f_dev, transcendentals=0),
@@ -179,16 +187,17 @@
     )(owners, bins, grads.T, hess, side.reshape(1, rows))
 
 
-def tiles_in(wt_ref, kdim):
-    return jnp.max(wt_ref[:, :128].astype(jnp.float32)[kdim + 1 : kdim + 2]).astype(jnp.int32)
-
-
-def hist_kernel(first_column, width, levels, parts, kdim, has_init, *refs):
-    pairs = [refs[2 * i : 2 * i + 2] for i in range(parts)]
-    init_ref = refs[2 * parts] if has_init else None
+def tiles_in(rows_ref, rows, kdim):
+    first = rows_ref[rows : rows + kdim + 16, :].astype(jnp.float32)
+    return jnp.max(first[kdim + 1 : kdim + 2]).astype(jnp.int32)
+
+
+def hist_kernel(first_column, width, levels, rows, parts, kdim, has_init, *refs):
+    sources = refs[:parts]
+    init_ref = refs[parts] if has_init else None
     out_ref, rel_ref, wt_ref = refs[-3:]
     lanes = out_ref.shape[1]
-    rows, half = pairs[0][0].shape
+    half = sources[0].shape[1]
     src = lax.broadcasted_iota(jnp.int32, (half, lanes), 0)
     dst = lax.broadcasted_iota(jnp.int32, (half, lanes), 1)
     spread = jnp.where(src == first_column + lax.rem(dst, width), 1.0, 0.0).astype(jnp.bfloat16)
@@ -203,11 +212,12 @@
         rel_ref[pl.ds(target, size), :] = (moved - shift).astype(jnp.bfloat16)
 
     def place_weights(height):
-        for i, (_, w_ref) in enumerate(pairs):
-            weights = w_ref[:, :height]
-            if w_ref.dtype != jnp.bfloat16:
-                weights = jnp.concatenate([weights, jnp.zeros((8, height), jnp.float32)], axis=0).astype(jnp.bfloat16)
-            wt_ref[:, i * height : (i + 1) * height] = weights
+        for i, rows_ref in enumerate(sources):
+            for j in range(0, height, half):
+                size = min(half, height - j)
+                at = rows + (j // half) * (kdim + 16)
+                weights = rows_ref[at : at + kdim + 16, :].astype(jnp.bfloat16)
+                wt_ref[:, i * height + j : i * height + j + size] = weights[:, :size]
 
     def sums_of(some, tiles):
         values = [jnp.full((TILE, lanes), b.astype(jnp.float32), jnp.float32).astype(jnp.bfloat16) for b in some]
@@ -225,7 +235,7 @@
 
     def fast():
         height = FAST * PACK
-        for i, (bins_ref, _) in enumerate(pairs):
+        for i, bins_ref in enumerate(sources):
             for r in range(0, height, 3 * PACK):
                 place_rows(bins_ref, r, i * height + r, 3 * PACK)
         place_weights(height)
@@ -246,7 +256,7 @@
         lax.fori_loop(0, levels // together, some_levels, 0)
 
     def general():
-        for i, (bins_ref, _) in enumerate(pairs):
+        for i, bins_ref in enumerate(sources):
 
             def one_pack(p, carry):
                 r = pl.multiple_of(p * PACK, PACK)
@@ -272,9 +282,9 @@
 
         lax.fori_loop(0, parts * rows // step, group, 0)
 
-    needed = tiles_in(pairs[0][1], kdim)
-    for _, w_ref in pairs[1:]:
-        needed = jnp.maximum(needed, tiles_in(w_ref, kdim))
+    needed = tiles_in(sources[0], rows, kdim)
+    for rows_ref in sources[1:]:
+        needed = jnp.maximum(needed, tiles_in(rows_ref, rows, kdim))
     if FAST * PACK < rows:
         pl.when(needed <= FAST)(fast)
         pl.when(needed > FAST)(general)
@@ -282,16 +292,15 @@
         general()
 
 
-def hist(first_column, width, levels, lanes, kdim, pairs, init=None, tie=()):
-    rows = pairs[0][0].shape[0]
-    parts = len(pairs)
-    operands = [x for pair in pairs for x in pair]
+def hist(first_column, width, levels, lanes, rows, kdim, sources, init=None, tie=()):
+    parts = len(sources)
+    operands = list(sources)
     if init is not None:
         operands.append(init)
     specs = [VMEM_SPEC] * len(operands) + [pl.BlockSpec(memory_space=pl.ANY)] * len(tie)
     height = levels * (kdim + 1)
     return pl.pallas_call(
-        functools.partial(hist_kernel, first_column, width, levels, parts, kdim, init is not None),
+        functools.partial(hist_kernel, first_column, width, levels, rows, parts, kdim, init is not None),
         in_specs=specs,
         out_specs=VMEM_SPEC,
         out_shape=jax.ShapeDtypeStruct((height, lanes), jnp.float32),
@@ -601,15 +610,12 @@
     lanes = min(256, width * nbins * kdim // 128)
     levels = nbins // (lanes // width)
 
-    own, send, wt, wt_send = prep(line, slab, parent_owner, bins, grads, hess, node_side)
+    mine, send = prep(line, slab, parent_owner, bins, grads, hess, node_side)
     swap = [(0, 1), (1, 0)]
-    wt_other = lax.ppermute(wt_send, "sub", swap)
-    other = lax.ppermute(send, "sub", swap)
-    mine = (own, wt)
-    theirs = (other, wt_other)
-
-    def unit(p, c, pairs, init=None, tie=()):
-        return hist(p * slab + c * width, width, levels, lanes, kdim, pairs, init, tie)
+    theirs = lax.ppermute(send, "sub", swap)
+
+    def unit(p, c, sources, init=None, tie=()):
+        return hist(p * slab + c * width, width, levels, lanes, bins.shape[0], kdim, sources, init, tie)
 
     def set_up(tie):
         return parent_layout(

time: 103 us -> 102 us (level)
    unnamed x20 -> x18, local copies, waits for them, and re-layouts: 2.2 us -> 1.34 us
  transfers between devices with their start and end apart: 20 -> 19, of which waited for: 7 -> 8; matrix products, arithmetic and copies ran while one was open for 1% -> 1% of each run, Pallas kernels for 40% -> 40%
where the time goes in v7:
time: 102 us
  Pallas kernels  51.5 us (50%)
  starting transfers between devices  32.2 us (32%)
  waiting for transfers between devices  13.6 us (13%)
  between operations  2.35 us (2%)
  local copies, waits for them, and re-layouts  1.85 us (2%)
    pallas_call x9, Pallas kernels, hist(): pl.pallas_call(functools.partial(hist_kernel, first_column, width, levels...  39.1 us
    ppermute x6, starting transfers between devices, per_device(): lax.ppermute(gain, 'dp', [(i, i ^ s) for i in range(line)])  9.77 us
    ppermute x2, starting transfers between devices, sum_line_of_4(): a1[c] = lax.ppermute(units[1, c], 'dp', inward)  8.53 us
    pallas_call x1, Pallas kernels, prep(): pl.pallas_call(functools.partial(prep_kernel, line, slab), in_specs=[SMEM...  7.01 us
    ppermute x2, waiting for transfers between devices, sum_line_of_4(): a0[c] = lax.ppermute(units[0, c], 'dp', inward)  6.25 us
    ppermute x2, starting transfers between devices, sum_line_of_4(): a0[c] = lax.ppermute(units[0, c], 'dp', inward)  6.21 us
    ppermute x2, starting transfers between devices, sum_line_of_4(): a2[c] = lax.ppermute(units[2, c] + b1[c], 'dp', outer)  4.17 us
    ppermute x6, waiting for transfers between devices, per_device(): lax.ppermute(gain, 'dp', [(i, i ^ s) for i in range(line)])  3.38 us
  transfers between devices with their start and end apart: 19, of which 8 were waited for; matrix products, arithmetic and copies ran while one was open for 1% of the time, Pallas kernels for 40%

profile of v7, /device:TPU:0, one launch (start us, length us, event | category | flops | bytes accessed | tf_op | source)
XLA Modules:
  0.0 101.8 jit_solution(4270178845006286419)
XLA Ops:
  0.0 7.0 %prep.1 = (bf16[2432,256]{1,0:T(8,128)(2,1)}, f32[2432,256]{1,0:T(8,128)}) custom-call(s32[8]{0:T(128)} %owner_ref.3, s32[2048,512]{1,0:T(8,128)} %bins_ref.1, bf16[32,2048]{1,0:T(8,128)(2,1)} %bitcast.12, bf16[2048]{0:T(1024)(128)(2,1)} %hess_ref.1, s32[1,2048]{1,0:T(1,128)} %bitcast.13), custom_call_target="tpu_custom_call" | custom-call | flops 2147483648 | bytes 8388608 | tf_op jit(solution)/shard_map/prep/pallas_call | solution.py:167
  8.8 2.6 %hist.9.refs_1_ = f32[528,256]{1,0:T(8,128)S(1)} custom-call(bf16[2432,256]{1,0:T(8,128)(2,1)S(1)} %copy-done), custom_call_target="tpu_custom_call" | custom-call | flops 524288 | bytes 524288 | tf_op jit(solution)/shard_map/hist/pallas_call | solution.py:302
  12.1 2.6 %hist.10.refs_2_.x_ref = f32[528,256]{1,0:T(8,128)S(1)} custom-call(f32[2432,256]{1,0:T(8,128)S(1)} %collective-permute-done.refs_0_.refs_1_, f32[528,256]{1,0:T(8,128)S(1)} %hist.9.refs_1_), custom_call_target="tpu_custom_call" | custom-call | flops 524288 | bytes 524288 | tf_op jit(solution)/shard_map/hist/pallas_call | solution.py:302
  14.7 4.9 %collective-permute-start.2 = (f32[528,256]{1,0:T(8,128)S(1)}, f32[528,256]{1,0:T(8,128)S(1)}, u32[]{:S(2)}, u32[]{:S(2)}) collective-permute-start(f32[528,256]{1,0:T(8,128)S(1)} %hist.10.refs_2_.x_ref), channel_id=1, source_target_pairs={{0,4},{12,8},{1,5},{13,9},{2,6},{14,10},{3,7},{15,11},{16,20},{28,... | collective-permute-start | bytes 1622024 | tf_op jit(solution)/shard_map/ppermute | solution.py:588
  19.6 4.8 %hist.11.refs_2_.x_ref = f32[528,256]{1,0:T(8,128)S(1)} custom-call(bf16[2432,256]{1,0:T(8,128)(2,1)S(1)} %copy-done.1, f32[2432,256]{1,0:T(8,128)S(1)} %collective-permute-done.refs_0_.refs_1_, f32[528,256]{1,0:T(8,128)S(1)} %hist.10.refs_2_.x_ref), custom_call_target="tpu_custom_call" | custom-call | flops 1048576 | bytes 1048576 | tf_op jit(solution)/shard_map/hist/pallas_call | solution.py:302
  24.4 1.3 %collective-permute-start.1 = (f32[528,256]{1,0:T(8,128)S(1)}, f32[528,256]{1,0:T(8,128)S(1)}, u32[]{:S(2)}, u32[]{:S(2)}) collective-permute-start(f32[528,256]{1,0:T(8,128)S(1)} %hist.11.refs_2_.x_ref), channel_id=1, source_target_pairs={{0,4},{12,8},{1,5},{13,9},{2,6},{14,10},{3,7},{15,11},{16,20},{28,... | collective-permute-start | bytes 1622024 | tf_op jit(solution)/shard_map/ppermute | solution.py:588
  25.8 4.8 %hist.12.refs_2_.tie_ref.x_ref = f32[528,256]{1,0:T(8,128)S(1)} custom-call(bf16[2432,256]{1,0:T(8,128)(2,1)S(1)} %copy-done.1, f32[2432,256]{1,0:T(8,128)S(1)} %collective-permute-done.refs_0_.refs_1_, f32[528,256]{1,0:T(8,128)S(1)} %hist.11.refs_2_.x_ref), custom_call_target="tpu_custom_call" | custom-call | flops 1048576 | bytes 1048576 | tf_op jit(solution)/shard_map/hist/pallas_call | solution.py:302
  30.6 1.3 %collective-permute-start.4 = (f32[528,256]{1,0:T(8,128)S(1)}, f32[528,256]{1,0:T(8,128)S(1)}, u32[]{:S(2)}, u32[]{:S(2)}) collective-permute-start(f32[528,256]{1,0:T(8,128)S(1)} %hist.12.refs_2_.tie_ref.x_ref), channel_id=1, source_target_pairs={{0,4},{12,8},{1,5},{13,9},{2,6},{14,10},{3,7},{15,11},{16,20},{28,... | collective-permute-start | bytes 1622024 | tf_op jit(solution)/shard_map/ppermute | solution.py:591
  33.0 4.8 %hist.13.refs_2_.tie_ref.x_ref = f32[528,256]{1,0:T(8,128)S(1)} custom-call(bf16[2432,256]{1,0:T(8,128)(2,1)S(1)} %copy-done.1, f32[2432,256]{1,0:T(8,128)S(1)} %collective-permute-done.refs_0_.refs_1_, f32[528,256]{1,0:T(8,128)S(1)} %hist.12.refs_2_.tie_ref.x_ref), custom_call_target="tpu_custom_call" | custom-call | flops 1048576 | bytes 1048576 | tf_op jit(solution)/shard_map/hist/pallas_call | solution.py:302
  37.8 6.0 %collective-permute-done.1.refs_3_.y_ref = f32[528,256]{1,0:T(8,128)S(1)} collective-permute-done((f32[528,256]{1,0:T(8,128)S(1)}, f32[528,256]{1,0:T(8,128)S(1)}, u32[]{:S(2)}, u32[]{:S(2)}) %collective-permute-start.1) | collective-permute-done | bytes 540704 | tf_op jit(solution)/shard_map/ppermute | solution.py:588
  44.6 7.2 %collective-permute-start.6 = (f32[528,256]{1,0:T(8,128)S(1)}, f32[528,256]{1,0:T(8,128)S(1)}, u32[]{:S(2)}, u32[]{:S(2)}) collective-permute-start(f32[528,256]{1,0:T(8,128)S(1)} %hist.13.refs_2_.tie_ref.x_ref), channel_id=1, source_target_pairs={{0,4},{12,8},{1,5},{13,9},{2,6},{14,10},{3,7},{15,11},{16,20},{28,... | collective-permute-start | bytes 1622024 | tf_op jit(solution)/shard_map/ppermute | solution.py:591
  51.8 4.8 %hist.14.refs_2_.tie_ref = f32[528,256]{1,0:T(8,128)S(1)} custom-call(bf16[2432,256]{1,0:T(8,128)(2,1)S(1)} %copy-done.1, f32[2432,256]{1,0:T(8,128)S(1)} %collective-permute-done.refs_0_.refs_1_, f32[528,256]{1,0:T(8,128)S(1)} %hist.13.refs_2_.tie_ref.x_ref, f32[528,256]{1,0:T(8,128)S(1)} %collective-permute-done.1.refs_3_.y_ref), custom_call_target="tpu_custom_call" | custom-call | flops 1048576 | bytes 1048576 | tf_op jit(solution)/shard_map/hist/pallas_call | solution.py:302
  57.5 4.1 %collective-permute-start.7 = (f32[528,256]{1,0:T(8,128)S(1)}, f32[528,256]{1,0:T(8,128)S(1)}, u32[]{:S(2)}, u32[]{:S(2)}) collective-permute-start(f32[528,256]{1,0:T(8,128)S(1)} %add.6), channel_id=1, source_target_pairs={{0,4},{4,0},{8,12},{12,8},{1,5},{5,1},{9,13},{13,9},{2,6},{6,2},{1... | collective-permute-start | bytes 1622024 | tf_op jit(solution)/shard_map/ppermute | solution.py:595
  61.6 4.8 %hist.15.refs_2_ = f32[528,256]{1,0:T(8,128)S(1)} custom-call(bf16[2432,256]{1,0:T(8,128)(2,1)S(1)} %copy-done.1, f32[2432,256]{1,0:T(8,128)S(1)} %collective-permute-done.refs_0_.refs_1_, f32[528,256]{1,0:T(8,128)S(1)} %hist.14.refs_2_.tie_ref, f32[528,256]{1,0:T(8,128)S(1)} %collective-permute-done.3.refs_3_, ...), custom_call_target="tpu_custom_call" | custom-call | flops 1048576 | bytes 1048576 | tf_op jit(solution)/shard_map/hist/pallas_call | solution.py:302
  66.6 4.8 %hist.16.refs_2_.last_ref.tie_ref = f32[528,256]{1,0:T(8,128)S(1)} custom-call(bf16[2432,256]{1,0:T(8,128)(2,1)S(1)} %copy-done.1, f32[2432,256]{1,0:T(8,128)S(1)} %collective-permute-done.refs_0_.refs_1_, f32[528,256]{1,0:T(8,128)S(1)} %hist.15.refs_2_, f32[528,256]{1,0:T(8,128)S(1)} %collective-permute-done.5.refs_3_), custom_call_target="tpu_custom_call" | custom-call | flops 1048576 | bytes 1048576 | tf_op jit(solution)/shard_map/hist/pallas_call | solution.py:302
  72.4 4.9 %hist.17.tie_ref.last_ref = f32[528,256]{1,0:T(8,128)S(1)} custom-call(bf16[2432,256]{1,0:T(8,128)(2,1)S(1)} %copy-done.1, f32[2432,256]{1,0:T(8,128)S(1)} %collective-permute-done.refs_0_.refs_1_, f32[528,256]{1,0:T(8,128)S(1)} %hist.16.refs_2_.last_ref.tie_ref, f32[528,256]{1,0:T(8,128)S(1)} %collective-permute-done.6.refs_3_.y_ref), custom_call_target="tpu_custom_call" | custom-call | flops 1048576 | bytes 1048576 | tf_op jit(solution)/shard_map/hist/pallas_call | solution.py:302
  78.6 1.6 %gains.2.refs_0_ = f32[2,16,256]{2,1,0:T(8,128)S(1)} custom-call(f32[528,256]{1,0:T(8,128)S(1)} %hist.16.refs_2_.last_ref.tie_ref, f32[528,256]{1,0:T(8,128)S(1)} %collective-permute-done.7.right_ref, f32[528,256]{1,0:T(8,128)S(1)} %collective-permute-done.8.left_ref, f32[512,256]{1,0:T(8,128)S(1)} %get-tuple-element.17.par_grad_ref, ...), custom_call_target="tpu_custom_call" | custom-call | flops 6553600 | bytes 2097152 | tf_op jit(solution)/shard_map/gains/pallas_call | solution.py:477
  80.2 2.5 %collective-permute-start.11 = (f32[2,16,256]{2,1,0:T(8,128)S(1)}, f32[2,16,256]{2,1,0:T(8,128)S(1)}, u32[]{:S(2)}, u32[]{:S(2)}) collective-permute-start(f32[2,16,256]{2,1,0:T(8,128)S(1)} %gains.2.refs_0_), channel_id=1, source_target_pairs={{0,12},{4,8},{8,4},{12,0},{1,13},{5,9},{9,5},{13,1},{2,14},{6,10},... | collective-permute-start | bytes 98312 | tf_op jit(solution)/shard_map/ppermute | solution.py:638
  82.7 2.7 %collective-permute-start.10 = (f32[2,16,256]{2,1,0:T(8,128)S(1)}, f32[2,16,256]{2,1,0:T(8,128)S(1)}, u32[]{:S(2)}, u32[]{:S(2)}) collective-permute-start(f32[2,16,256]{2,1,0:T(8,128)S(1)} %gains.2.refs_0_), channel_id=1, source_target_pairs={{0,8},{4,12},{8,0},{12,4},{1,9},{5,13},{9,1},{13,5},{2,10},{6,14},... | collective-permute-start | bytes 98312 | tf_op jit(solution)/shard_map/ppermute | solution.py:638
  88.0 2.2 %collective-permute-done.13.right_ref = f32[528,256]{1,0:T(8,128)S(1)} collective-permute-done((f32[528,256]{1,0:T(8,128)S(1)}, f32[528,256]{1,0:T(8,128)S(1)}, u32[]{:S(2)}, u32[]{:S(2)}) %collective-permute-start.13) | collective-permute-done | bytes 540704 | tf_op jit(solution)/shard_map/ppermute | solution.py:595
  90.1 1.6 %gains.3.refs_5_ = f32[2,16,256]{2,1,0:T(8,128)S(1)} custom-call(f32[528,256]{1,0:T(8,128)S(1)} %hist.17.tie_ref.last_ref, f32[528,256]{1,0:T(8,128)S(1)} %collective-permute-done.13.right_ref, f32[528,256]{1,0:T(8,128)S(1)} %collective-permute-done.14.left_ref, f32[512,256]{1,0:T(8,128)S(1)} %get-tuple-element.20.par_grad_ref, ...), custom_call_target="tpu_custom_call" | custom-call | flops 6553600 | bytes 2097152 | tf_op jit(solution)/shard_map/gains/pallas_call | solution.py:477
  91.7 2.5 %collective-permute-start.17 = (f32[2,16,256]{2,1,0:T(8,128)S(1)}, f32[2,16,256]{2,1,0:T(8,128)S(1)}, u32[]{:S(2)}, u32[]{:S(2)}) collective-permute-start(f32[2,16,256]{2,1,0:T(8,128)S(1)} %gains.3.refs_5_), channel_id=1, source_target_pairs={{0,12},{4,8},{8,4},{12,0},{1,13},{5,9},{9,5},{13,1},{2,14},{6,10},... | collective-permute-start | bytes 98312 | tf_op jit(solution)/shard_map/ppermute | solution.py:638
  94.3 1.5 %collective-permute-start.16 = (f32[2,16,256]{2,1,0:T(8,128)S(1)}, f32[2,16,256]{2,1,0:T(8,128)S(1)}, u32[]{:S(2)}, u32[]{:S(2)}) collective-permute-start(f32[2,16,256]{2,1,0:T(8,128)S(1)} %gains.3.refs_5_), channel_id=1, source_target_pairs={{0,8},{4,12},{8,0},{12,4},{1,9},{5,13},{9,1},{13,5},{2,10},{6,14},... | collective-permute-start | bytes 98312 | tf_op jit(solution)/shard_map/ppermute | solution.py:638
  96.3 1.6 %collective-permute-done.17.refs_8_ = f32[2,16,256]{2,1,0:T(8,128)S(1)} collective-permute-done((f32[2,16,256]{2,1,0:T(8,128)S(1)}, f32[2,16,256]{2,1,0:T(8,128)S(1)}, u32[]{:S(2)}, u32[]{:S(2)}) %collective-permute-start.17) | collective-permute-done | bytes 32800 | tf_op jit(solution)/shard_map/ppermute | solution.py:638
  (55 shorter events, 12.5 us)
Async XLA Ops:
  7.0 5.1 %collective-permute-start = (f32[2432,256]{1,0:T(8,128)}, f32[2432,256]{1,0:T(8,128)S(1)}, u32[]{:S(2)}, u32[]{:S(2)}) collective-permute-start(f32[2432,256]{1,0:T(8,128)} %get-tuple-element.15), channel_id=1, source_target_pairs={{0,1},{1,0},{2,3},{3,2},{4,5},{5,4},{6,7},{7,6},{8,9},{9,8},{10,11... | collective-permute-start | bytes 7471112 | tf_op jit(solution)/shard_map/ppermute | solution.py:615
  8.8 10.8 %copy-start.1 = (bf16[2432,256]{1,0:T(8,128)(2,1)S(1)}, bf16[2432,256]{1,0:T(8,128)(2,1)}, u32[]{:S(2)}) copy-start(bf16[2432,256]{1,0:T(8,128)(2,1)} %get-tuple-element.14.refs_0_) | copy-start | bytes 3735556
  14.7 17.5 %collective-permute-start.2 = (f32[528,256]{1,0:T(8,128)S(1)}, f32[528,256]{1,0:T(8,128)S(1)}, u32[]{:S(2)}, u32[]{:S(2)}) collective-permute-start(f32[528,256]{1,0:T(8,128)S(1)} %hist.10.refs_2_.x_ref), channel_id=1, source_target_pairs={{0,4},{12,8},{1,5},{13,9},{2,6},{14,10},{3,7},{15,11},{16,20},{28,... | collective-permute-start | bytes 1622024 | tf_op jit(solution)/shard_map/ppermute | solution.py:588
  24.4 19.3 %collective-permute-start.1 = (f32[528,256]{1,0:T(8,128)S(1)}, f32[528,256]{1,0:T(8,128)S(1)}, u32[]{:S(2)}, u32[]{:S(2)}) collective-permute-start(f32[528,256]{1,0:T(8,128)S(1)} %hist.11.refs_2_.x_ref), channel_id=1, source_target_pairs={{0,4},{12,8},{1,5},{13,9},{2,6},{14,10},{3,7},{15,11},{16,20},{28,... | collective-permute-start | bytes 1622024 | tf_op jit(solution)/shard_map/ppermute | solution.py:588
  30.6 26.0 %collective-permute-start.4 = (f32[528,256]{1,0:T(8,128)S(1)}, f32[528,256]{1,0:T(8,128)S(1)}, u32[]{:S(2)}, u32[]{:S(2)}) collective-permute-start(f32[528,256]{1,0:T(8,128)S(1)} %hist.12.refs_2_.tie_ref.x_ref), channel_id=1, source_target_pairs={{0,4},{12,8},{1,5},{13,9},{2,6},{14,10},{3,7},{15,11},{16,20},{28,... | collective-permute-start | bytes 1622024 | tf_op jit(solution)/shard_map/ppermute | solution.py:591
  32.3 25.1 %collective-permute-start.3 = (f32[528,256]{1,0:T(8,128)S(1)}, f32[528,256]{1,0:T(8,128)S(1)}, u32[]{:S(2)}, u32[]{:S(2)}) collective-permute-start(f32[528,256]{1,0:T(8,128)S(1)} %sum_after.4), channel_id=1, source_target_pairs={{4,8},{8,4},{5,9},{9,5},{6,10},{10,6},{7,11},{11,7},{20,24},{24,20... | collective-permute-start | bytes 1622024 | tf_op jit(solution)/shard_map/ppermute | solution.py:592
  43.8 22.6 %collective-permute-start.5 = (f32[528,256]{1,0:T(8,128)S(1)}, f32[528,256]{1,0:T(8,128)S(1)}, u32[]{:S(2)}, u32[]{:S(2)}) collective-permute-start(f32[528,256]{1,0:T(8,128)S(1)} %sum_after.5), channel_id=1, source_target_pairs={{4,8},{8,4},{5,9},{9,5},{6,10},{10,6},{7,11},{11,7},{20,24},{24,20... | collective-permute-start | bytes 1622024 | tf_op jit(solution)/shard_map/ppermute | solution.py:592
  44.6 26.9 %collective-permute-start.6 = (f32[528,256]{1,0:T(8,128)S(1)}, f32[528,256]{1,0:T(8,128)S(1)}, u32[]{:S(2)}, u32[]{:S(2)}) collective-permute-start(f32[528,256]{1,0:T(8,128)S(1)} %hist.13.refs_2_.tie_ref.x_ref), channel_id=1, source_target_pairs={{0,4},{12,8},{1,5},{13,9},{2,6},{14,10},{3,7},{15,11},{16,20},{28,... | collective-permute-start | bytes 1622024 | tf_op jit(solution)/shard_map/ppermute | solution.py:591
  56.7 21.9 %collective-permute-start.8 = (f32[528,256]{1,0:T(8,128)S(1)}, f32[528,256]{1,0:T(8,128)S(1)}, u32[]{:S(2)}, u32[]{:S(2)}) collective-permute-start(f32[528,256]{1,0:T(8,128)S(1)} %sum_after.6), channel_id=1, source_target_pairs={{4,8},{8,4},{5,9},{9,5},{6,10},{10,6},{7,11},{11,7},{20,24},{24,20... | collective-permute-start | bytes 1622024 | tf_op jit(solution)/shard_map/ppermute | solution.py:599
  57.5 21.1 %collective-permute-start.7 = (f32[528,256]{1,0:T(8,128)S(1)}, f32[528,256]{1,0:T(8,128)S(1)}, u32[]{:S(2)}, u32[]{:S(2)}) collective-permute-start(f32[528,256]{1,0:T(8,128)S(1)} %add.6), channel_id=1, source_target_pairs={{0,4},{4,0},{8,12},{12,8},{1,5},{5,1},{9,13},{13,9},{2,6},{6,2},{1... | collective-permute-start | bytes 1622024 | tf_op jit(solution)/shard_map/ppermute | solution.py:595
  66.5 23.6 %collective-permute-start.13 = (f32[528,256]{1,0:T(8,128)S(1)}, f32[528,256]{1,0:T(8,128)S(1)}, u32[]{:S(2)}, u32[]{:S(2)}) collective-permute-start(f32[528,256]{1,0:T(8,128)S(1)} %add.7), channel_id=1, source_target_pairs={{0,4},{4,0},{8,12},{12,8},{1,5},{5,1},{9,13},{13,9},{2,6},{6,2},{1... | collective-permute-start | bytes 1622024 | tf_op jit(solution)/shard_map/ppermute | solution.py:595
  71.5 5.8 %copy-start.2 = (f32[1,64,4096]{2,1,0:T(8,128)S(1)}, f32[1,64,4096]{2,1,0:T(8,128)}, u32[]{:S(2)}) copy-start(f32[1,64,4096]{2,1,0:T(8,128)} %param.18) | copy-start | bytes 3145732
  71.5 5.8 %copy-start.3 = (f32[1,64,128]{2,1,0:T(8,128)S(1)}, f32[1,64,128]{2,1,0:T(8,128)}, u32[]{:S(2)}) copy-start(f32[1,64,128]{2,1,0:T(8,128)} %param.19) | copy-start | bytes 98308
  71.5 5.8 %copy-start.4 = (s32[1024]{0:T(1024)S(1)}, s32[1024]{0:T(1024)}, u32[]{:S(2)}) copy-start(s32[1024]{0:T(1024)} %param.15) | copy-start | bytes 12292
  71.5 5.8 %copy-start.5 = (s32[8]{0:T(128)S(1)}, s32[8]{0:T(128)}, u32[]{:S(2)}) copy-start(s32[8]{0:T(128)} %child_ref.1) | copy-start | bytes 100
  71.6 18.5 %collective-permute-start.14 = (f32[528,256]{1,0:T(8,128)S(1)}, f32[528,256]{1,0:T(8,128)S(1)}, u32[]{:S(2)}, u32[]{:S(2)}) collective-permute-start(f32[528,256]{1,0:T(8,128)S(1)} %sum_after.7), channel_id=1, source_target_pairs={{4,8},{8,4},{5,9},{9,5},{6,10},{10,6},{7,11},{11,7},{20,24},{24,20... | collective-permute-start | bytes 1622024 | tf_op jit(solution)/shard_map/ppermute | solution.py:599
  80.2 15.5 %collective-permute-start.11 = (f32[2,16,256]{2,1,0:T(8,128)S(1)}, f32[2,16,256]{2,1,0:T(8,128)S(1)}, u32[]{:S(2)}, u32[]{:S(2)}) collective-permute-start(f32[2,16,256]{2,1,0:T(8,128)S(1)} %gains.2.refs_0_), channel_id=1, source_target_pairs={{0,12},{4,8},{8,4},{12,0},{1,13},{5,9},{9,5},{13,1},{2,14},{6,10},... | collective-permute-start | bytes 98312 | tf_op jit(solution)/shard_map/ppermute | solution.py:638
  82.7 13.5 %collective-permute-start.10 = (f32[2,16,256]{2,1,0:T(8,128)S(1)}, f32[2,16,256]{2,1,0:T(8,128)S(1)}, u32[]{:S(2)}, u32[]{:S(2)}) collective-permute-start(f32[2,16,256]{2,1,0:T(8,128)S(1)} %gains.2.refs_0_), channel_id=1, source_target_pairs={{0,8},{4,12},{8,0},{12,4},{1,9},{5,13},{9,1},{13,5},{2,10},{6,14},... | collective-permute-start | bytes 98312 | tf_op jit(solution)/shard_map/ppermute | solution.py:638
  85.4 10.8 %collective-permute-start.9 = (f32[2,16,256]{2,1,0:T(8,128)S(1)}, f32[2,16,256]{2,1,0:T(8,128)S(1)}, u32[]{:S(2)}, u32[]{:S(2)}) collective-permute-start(f32[2,16,256]{2,1,0:T(8,128)S(1)} %gains.2.refs_0_), channel_id=1, source_target_pairs={{0,4},{4,0},{8,12},{12,8},{1,5},{5,1},{9,13},{13,9},{2,6},{6,2},{1... | collective-permute-start | bytes 98312 | tf_op jit(solution)/shard_map/ppermute | solution.py:638
  91.7 6.1 %collective-permute-start.17 = (f32[2,16,256]{2,1,0:T(8,128)S(1)}, f32[2,16,256]{2,1,0:T(8,128)S(1)}, u32[]{:S(2)}, u32[]{:S(2)}) collective-permute-start(f32[2,16,256]{2,1,0:T(8,128)S(1)} %gains.3.refs_5_), channel_id=1, source_target_pairs={{0,12},{4,8},{8,4},{12,0},{1,13},{5,9},{9,5},{13,1},{2,14},{6,10},... | collective-permute-start | bytes 98312 | tf_op jit(solution)/shard_map/ppermute | solution.py:638
  94.3 4.8 %collective-permute-start.16 = (f32[2,16,256]{2,1,0:T(8,128)S(1)}, f32[2,16,256]{2,1,0:T(8,128)S(1)}, u32[]{:S(2)}, u32[]{:S(2)}) collective-permute-start(f32[2,16,256]{2,1,0:T(8,128)S(1)} %gains.3.refs_5_), channel_id=1, source_target_pairs={{0,8},{4,12},{8,0},{12,4},{1,9},{5,13},{9,1},{13,5},{2,10},{6,14},... | collective-permute-start | bytes 98312 | tf_op jit(solution)/shard_map/ppermute | solution.py:638
  95.7 3.9 %collective-permute-start.15 = (f32[2,16,256]{2,1,0:T(8,128)S(1)}, f32[2,16,256]{2,1,0:T(8,128)S(1)}, u32[]{:S(2)}, u32[]{:S(2)}) collective-permute-start(f32[2,16,256]{2,1,0:T(8,128)S(1)} %gains.3.refs_5_), channel_id=1, source_target_pairs={{0,4},{4,0},{8,12},{12,8},{1,5},{5,1},{9,13},{13,9},{2,6},{6,2},{1... | collective-permute-start | bytes 98312 | tf_op jit(solution)/shard_map/ppermute | solution.py:638
  96.2 3.5 %collective-permute-start.12 = (f32[2,16,256]{2,1,0:T(8,128)S(1)}, f32[2,16,256]{2,1,0:T(8,128)S(1)}, u32[]{:S(2)}, u32[]{:S(2)}) collective-permute-start(f32[2,16,256]{2,1,0:T(8,128)S(1)} %select_select_fusion.1), channel_id=1, source_target_pairs={{0,1},{1,0},{2,3},{3,2},{4,5},{5,4},{6,7},{7,6},{8,9},{9,8},{10,11... | collective-permute-start | bytes 98312 | tf_op jit(solution)/shard_map/ppermute | solution.py:639
  99.7 1.3 %collective-permute-start.18 = (f32[2,16,256]{2,1,0:T(8,128)S(1)}, f32[2,16,256]{2,1,0:T(8,128)S(1)}, u32[]{:S(2)}, u32[]{:S(2)}) collective-permute-start(f32[2,16,256]{2,1,0:T(8,128)S(1)} %select_select_fusion), channel_id=1, source_target_pairs={{0,1},{1,0},{2,3},{3,2},{4,5},{5,4},{6,7},{7,6},{8,9},{9,8},{10,11... | collective-permute-start | bytes 98312 | tf_op jit(solution)/shard_map/ppermute | solution.py:639
  (4 other events, 18.6 us)
